TPU v7x, 128 devices: a whole 4x4x4 slice. The times are simulated.
128 devices in a mesh: seq: 8 (over z, core), ch: 16 (over y, x).
Axes of the slice: x: 4, y: 4, z: 4, core: 2. Of those that a mesh axis runs over, the one named last changes fastest.
Arguments:
- tokens: bfloat16 [2, 1024, 2048], P(None, 'seq'), may hold values from -6 to 6
- cotangent: bfloat16 [2, 1024, 2048], P(None, 'seq'), may hold values from -6 to 6
- short_lengths: int32 [8], replicated, may hold values from 1 to 898, 1024 in all
- long_lengths: int32 [3], replicated, may hold values from 1 to 898, 1024 in all
- gain_one: float32 [2048], replicated, may hold values from 0.25 to 1.75
- gain_two: float32 [2048], replicated, may hold values from 0.25 to 1.75
- w_y: bfloat16 [2048, 2736], P(None, 'ch'), may hold values from -0.125 to 0.125
- w_x: bfloat16 [2048, 2736], P(None, 'ch'), may hold values from -0.125 to 0.125
- conv_w: float32 [4, 2736], P(None, 'ch'), may hold values from -3 to 3
- conv_b: float32 [2736], P('ch'), may hold values from -0.5 to 0.5
- gate_a: bfloat16 [16, 171, 171], P('ch'), may hold values from -0.4375 to 0.4375
- gate_x: bfloat16 [16, 171, 171], P('ch'), may hold values from -0.4375 to 0.4375
- bias_a: float32 [2736], P('ch'), may hold values from -1 to 1
- bias_x: float32 [2736], P('ch'), may hold values from -1 to 1
- lam: float32 [2736], P('ch'), may hold values from 4 to 12
- w_out: bfloat16 [2736, 2048], P('ch'), may hold values from -0.3125 to 0.3125
- w_one: bfloat16 [2048, 6144], P(None, 'ch'), may hold values from -0.125 to 0.125
- w_two: bfloat16 [2048, 6144], P(None, 'ch'), may hold values from -0.125 to 0.125
- w_three: bfloat16 [6144, 2048], P('ch'), may hold values from -0.15625 to 0.15625
Outputs:
- layer_out: bfloat16 [2, 1024, 2048], P(None, 'seq')
- d_tokens: float32 [2, 1024, 2048], P(None, 'seq')
- g_gain_one: float32 [2048], P('ch')
- g_gain_two: float32 [2048], P('ch')
- g_w_y: float32 [2048, 2736], P(None, 'ch')
- g_w_x: float32 [2048, 2736], P(None, 'ch')
- g_conv_w: float32 [4, 2736], P(None, 'ch')
- g_conv_b: float32 [2736], P('ch')
- g_gate_a: float32 [16, 171, 171], P('ch')
- g_gate_x: float32 [16, 171, 171], P('ch')
- g_bias_a: float32 [2736], P('ch')
- g_bias_x: float32 [2736], P('ch')
- g_lam: float32 [2736], P('ch')
- g_w_out: float32 [2736, 2048], P('ch')
- g_w_one: float32 [2048, 6144], P(None, 'ch')
- g_w_two: float32 [2048, 6144], P(None, 'ch')
- g_w_three: float32 [6144, 2048], P('ch')
Inputs may be any that keep to these rules, and one draw needn't show every extreme that they name: `short_lengths`: each row's document lengths sum to 1024 and the longest has exactly 898 positions. `long_lengths`: each row's document lengths sum to 1024 and the longest has exactly 898 positions.
All inputs are finite; a program needn't handle non-finite values.
Results may differ from a plain program's by a relative error of at most 0.023.
Values may be sent and summed in bfloat16 or wider, within the bound.
No kernel may reach another device: no remote copies, remote signals or barrier semaphores. Data moves between devices by JAX's collectives and lax.ppermute only.
A program may use at most 128 MiB of HBM per device.

v0:
```python
from functools import partial

import jax
import jax.numpy as jnp
from jax import lax
from jax.sharding import PartitionSpec as P

EPS_NORM = 1e-06


def from_behind(block, axis, distance):
    devices = range(lax.axis_size(axis))
    route = [(i - distance, i) for i in devices if i - distance in devices]
    return lax.ppermute(block, axis, route)


def carried_in(value, axis, join, neutral, backward):
    count, mine = (lax.axis_size(axis), lax.axis_index(axis))
    pieces = jax.tree.map(lambda part: lax.all_gather(part, axis), value)
    if backward:
        pieces = jax.tree.map(lambda part: part[::-1], pieces)
        mine = count - 1 - mine
    subtotal = jax.tree.map(
        lambda part, zero: jnp.full_like(part, 0) + jnp.asarray(zero, part.dtype), value, neutral
    )

    def hop(position, subtotal):
        longer = join(subtotal, jax.tree.map(lambda part: part[position], pieces))
        return jax.tree.map(lambda new, old: jnp.where(position < mine, new, old), longer, subtotal)

    return lax.fori_loop(0, count - 1, hop, subtotal)


def matmul(left, right, form):
    return jnp.einsum(form, left, right, preferred_element_type=jnp.float32)


def combine(earlier, later):
    return (earlier[0] * later[0], later[1] + later[0] * earlier[1])


def doc_index(lengths, positions):
    doc_ends = jnp.cumsum(lengths)
    return jnp.sum((positions[:, None] >= doc_ends[None, :]).astype(jnp.int32), axis=1)


def doc_masks(lengths, positions, width):
    doc_ids = doc_index(lengths, positions)
    result = [jnp.ones(positions.shape, jnp.float32)]
    for offset in range(1, width):
        before = doc_index(lengths, positions - offset)
        result.append(((positions - offset >= 0) & (doc_ids == before)).astype(jnp.float32))
    return jnp.stack(result)


def rms_scale(features, gain_vec):
    inverse = lax.rsqrt(jnp.mean(features * features, axis=-1, keepdims=True) + EPS_NORM)
    return features * inverse * gain_vec


def recurrence_inputs(raw_a, raw_x, conv_out, lam, bias_a, bias_x, reset):
    rate_gate = jax.nn.sigmoid(raw_a + bias_a)
    inlet_gate = jax.nn.sigmoid(raw_x + bias_x)
    log_decay = -8.0 * jax.nn.softplus(-lam) * rate_gate
    keep_gate = jnp.exp(log_decay) * reset
    drive_term = jnp.sqrt(-jnp.expm1(2.0 * log_decay)) * inlet_gate * conv_out
    return (keep_gate, drive_term)


def gelu_tanh(values):
    return jax.nn.gelu(values, approximate=True)


def body(
    tokens,
    cotangent,
    short_lengths,
    long_lengths,
    gain_one,
    gain_two,
    w_y,
    w_x,
    conv_w,
    conv_b,
    gate_a,
    gate_x,
    bias_a,
    bias_x,
    lam,
    w_out,
    w_one,
    w_two,
    w_three,
):
    f32 = jnp.float32
    bf16 = jnp.bfloat16
    group_count, row_count, model_width = tokens.shape
    tap_count = conv_w.shape[0]
    local_blocks, block_width, _ = gate_a.shape
    channels = w_x.shape[1]
    row_start = lax.axis_index("seq") * row_count
    positions = row_start + jnp.arange(row_count + tap_count - 1, dtype=jnp.int32)
    all_masks = jnp.stack(
        [
            doc_masks(short_lengths, positions, tap_count),
            doc_masks(long_lengths, positions, tap_count),
        ],
        axis=1,
    )
    inner_masks = all_masks[:, :, :row_count, None]
    share_width = model_width // lax.axis_size("ch")
    col_start = lax.axis_index("ch") * share_width
    tokens_f = tokens.astype(f32)
    cotangent_f = cotangent.astype(f32)
    normed_one = rms_scale(tokens_f, gain_one).astype(bf16)
    gate_pre = matmul(normed_one, w_y, "gtd,dc->gtc")
    gate_branch = gelu_tanh(gate_pre)
    conv_input = matmul(normed_one, w_x, "gtd,dc->gtc").astype(bf16)
    edge_rows = from_behind(conv_input[:, row_count - tap_count + 1 :], "seq", 1)
    conv_ext = jnp.concatenate([edge_rows, conv_input], axis=1).astype(f32)
    conv_out = conv_b + jnp.zeros((group_count, row_count, channels), f32)
    for offset in range(tap_count):
        conv_out = (
            conv_out
            + conv_w[offset]
            * conv_ext[:, tap_count - 1 - offset : tap_count - 1 - offset + row_count]
            * inner_masks[offset]
        )
    conv_low = conv_out.astype(bf16).reshape(group_count, row_count, local_blocks, block_width)
    raw_a = matmul(conv_low, gate_a, "gtbi,bij->gtbj").reshape(group_count, row_count, channels)
    raw_x = matmul(conv_low, gate_x, "gtbi,bij->gtbj").reshape(group_count, row_count, channels)
    gates_fn = partial(recurrence_inputs, reset=inner_masks[1])
    (keep_gate, drive_term), pull_gates = jax.vjp(
        gates_fn, raw_a, raw_x, conv_out, lam, bias_a, bias_x
    )
    decay_run, local_state = lax.associative_scan(combine, (keep_gate, drive_term), axis=1)
    identity = (jnp.ones((group_count, channels), f32), jnp.zeros((group_count, channels), f32))
    _, state_in = carried_in(
        (decay_run[:, -1], local_state[:, -1]), "seq", combine, identity, False
    )
    hidden = local_state + decay_run * state_in[:, None]
    mixed_in = (hidden * gate_branch).astype(bf16)
    mix_partial = matmul(mixed_in, w_out, "gtc,cd->gtd")
    resid_mid = tokens_f + lax.psum(mix_partial, "ch")
    normed_two = rms_scale(resid_mid, gain_two).astype(bf16)
    mlp_gate = matmul(normed_two, w_one, "gtd,df->gtf")
    mlp_up = matmul(normed_two, w_two, "gtd,df->gtf")
    gate_value, gelu_pull = jax.vjp(gelu_tanh, mlp_gate)
    mlp_hidden = (gate_value * mlp_up).astype(bf16)
    partial_out = matmul(mlp_hidden, w_three, "gtf,fd->gtd")
    layer_out = (
        resid_mid + lax.psum(partial_out.astype(jnp.bfloat16), "ch").astype(jnp.float32)
    ).astype(bf16)
    g_w_three = matmul(mlp_hidden, cotangent, "gtf,gtd->fd")
    d_hidden_mlp = matmul(cotangent, w_three, "gtd,fd->gtf")
    d_gate = gelu_pull(d_hidden_mlp * mlp_up)[0].astype(bf16)
    d_up = (d_hidden_mlp * gate_value).astype(bf16)
    g_w_one = matmul(normed_two, d_gate, "gtd,gtf->df")
    g_w_two = matmul(normed_two, d_up, "gtd,gtf->df")
    partial_two = matmul(d_gate, w_one, "gtf,df->gtd") + matmul(d_up, w_two, "gtf,df->gtd")
    _, norm_two_pull = jax.vjp(rms_scale, resid_mid, gain_two)
    d_mid_norm, g_gain_two = norm_two_pull(
        lax.psum(partial_two.astype(jnp.bfloat16), "ch").astype(jnp.float32)
    )
    d_mid = cotangent_f + d_mid_norm
    d_mix = d_mid.astype(bf16)
    g_w_out = matmul(mixed_in, d_mix, "gtc,gtd->cd")
    d_mixed = matmul(d_mix, w_out, "gtd,cd->gtc")
    d_state = d_mixed * gate_branch
    _, branch_pull = jax.vjp(gelu_tanh, gate_pre)
    d_gate_pre = branch_pull(d_mixed * hidden)[0].astype(bf16)
    follow_gate = jnp.concatenate([keep_gate[:, 1:], jnp.ones_like(keep_gate[:, :1])], axis=1)
    reach, local_adjoint = lax.associative_scan(
        combine, (follow_gate, d_state), reverse=True, axis=1
    )
    stretch_first = (decay_run[:, -1], keep_gate[:, 0] * local_adjoint[:, 0])
    _, beyond = carried_in(stretch_first, "seq", combine, identity, True)
    adjoint = local_adjoint + reach * beyond[:, None]
    prior_state = jnp.concatenate([state_in[:, None], hidden[:, :-1]], axis=1)
    g_raw_a, g_raw_x, d_conv_gate, g_lam, g_bias_a, g_bias_x = pull_gates(
        (adjoint * prior_state, adjoint)
    )
    raw_a_low = g_raw_a.astype(bf16).reshape(group_count, row_count, local_blocks, block_width)
    raw_x_low = g_raw_x.astype(bf16).reshape(group_count, row_count, local_blocks, block_width)
    g_gate_a = matmul(conv_low, raw_a_low, "gtbi,gtbj->bij")
    g_gate_x = matmul(conv_low, raw_x_low, "gtbi,gtbj->bij")
    d_conv = d_conv_gate + (
        matmul(raw_a_low, gate_a, "gtbj,bij->gtbi") + matmul(raw_x_low, gate_x, "gtbj,bij->gtbi")
    ).reshape(group_count, row_count, channels)
    g_conv_b = jnp.sum(d_conv, axis=(0, 1))
    tap_grads = []
    for offset in range(tap_count):
        tap_grads.append(
            jnp.sum(
                d_conv
                * inner_masks[offset]
                * conv_ext[:, tap_count - 1 - offset : tap_count - 1 - offset + row_count],
                axis=(0, 1),
            )
        )
    g_conv_w = jnp.stack(tap_grads)
    lead_rows = from_behind(d_conv[:, : tap_count - 1], "seq", -1)
    d_conv_ext = jnp.concatenate([d_conv, lead_rows], axis=1)
    d_input_f = jnp.zeros((group_count, row_count, channels), f32)
    for offset in range(tap_count):
        d_input_f = (
            d_input_f
            + conv_w[offset]
            * all_masks[offset, :, offset : offset + row_count, None]
            * d_conv_ext[:, offset : offset + row_count]
        )
    d_input = d_input_f.astype(bf16)
    g_w_x = matmul(normed_one, d_input, "gtd,gtc->dc")
    g_w_y = matmul(normed_one, d_gate_pre, "gtd,gtc->dc")
    partial_one = matmul(d_input, w_x, "gtc,dc->gtd") + matmul(d_gate_pre, w_y, "gtc,dc->gtd")
    _, norm_one_pull = jax.vjp(rms_scale, tokens_f, gain_one)
    d_tokens_norm, g_gain_one = norm_one_pull(
        lax.psum(partial_one.astype(jnp.bfloat16), "ch").astype(jnp.float32)
    )
    d_tokens = d_mid + d_tokens_norm
    g_gain_one = lax.dynamic_slice_in_dim(g_gain_one, col_start, share_width, 0)
    g_gain_two = lax.dynamic_slice_in_dim(g_gain_two, col_start, share_width, 0)
    totals = (
        lax.psum(g_gain_one.astype(jnp.bfloat16), "seq").astype(jnp.float32),
        lax.psum(g_gain_two.astype(jnp.bfloat16), "seq").astype(jnp.float32),
        lax.psum(g_w_y.astype(jnp.bfloat16), "seq").astype(jnp.float32),
        lax.psum(g_w_x.astype(jnp.bfloat16), "seq").astype(jnp.float32),
        lax.psum(g_conv_w.astype(jnp.bfloat16), "seq").astype(jnp.float32),
        lax.psum(g_conv_b.astype(jnp.bfloat16), "seq").astype(jnp.float32),
        lax.psum(g_gate_a.astype(jnp.bfloat16), "seq").astype(jnp.float32),
        lax.psum(g_gate_x.astype(jnp.bfloat16), "seq").astype(jnp.float32),
        lax.psum(g_bias_a.astype(jnp.bfloat16), "seq").astype(jnp.float32),
        lax.psum(g_bias_x.astype(jnp.bfloat16), "seq").astype(jnp.float32),
        lax.psum(g_lam.astype(jnp.bfloat16), "seq").astype(jnp.float32),
        lax.psum(g_w_out.astype(jnp.bfloat16), "seq").astype(jnp.float32),
        lax.psum(g_w_one.astype(jnp.bfloat16), "seq").astype(jnp.float32),
        lax.psum(g_w_two.astype(jnp.bfloat16), "seq").astype(jnp.float32),
        lax.psum(g_w_three.astype(jnp.bfloat16), "seq").astype(jnp.float32),
    )
    return (
        layer_out,
        d_tokens,
        totals[0],
        totals[1],
        totals[2],
        totals[3],
        totals[4],
        totals[5],
        totals[6],
        totals[7],
        totals[8],
        totals[9],
        totals[10],
        totals[11],
        totals[12],
        totals[13],
        totals[14],
    )


def solution(mesh):
    placed = (
        P(None, "seq", None),
        P(None, "seq", None),
        P(),
        P(),
        P(),
        P(),
        P(None, "ch"),
        P(None, "ch"),
        P(None, "ch"),
        P("ch"),
        P("ch", None, None),
        P("ch", None, None),
        P("ch"),
        P("ch"),
        P("ch"),
        P("ch", None),
        P(None, "ch"),
        P(None, "ch"),
        P("ch", None),
    )
    return jax.shard_map(
        body,
        mesh=mesh,
        in_specs=placed,
        out_specs=(
            P(None, "seq", None),
            P(None, "seq", None),
            P("ch"),
            P("ch"),
            P(None, "ch"),
            P(None, "ch"),
            P(None, "ch"),
            P("ch"),
            P("ch", None, None),
            P("ch", None, None),
            P("ch"),
            P("ch"),
            P("ch"),
            P("ch", None),
            P(None, "ch"),
            P(None, "ch"),
            P("ch", None),
        ),
        check_vma=False,
    )
```

profile of v0, /device:TPU:1, one launch (start us, length us, event | category | flops | bytes accessed | tf_op | source)
XLA Modules:
  0.0 876.8 jit_solution(7026740874961044688)
XLA Ops:
  12.2 4.9 collective-permute-start
  23.9 3.0 slice.536
  26.9 3.0 slice.535
  70.1 3.6 slice.534
  73.7 3.6 slice.533
  127.4 3.1 pad.187
  137.3 4.0 pad.186
  141.5 13.4 %all-gather = f32[16,1,171]{2,1,0:T(1,128)S(1)} all-gather(f32[2,1,171]{2,1,0:T(1,128)S(1)} %copy.128), channel_id=2, replica_groups=mesh['seq'=8,'ch'=16] {'seq'}, dimensions={0}, use_global_device_ids=true | all-gather | bytes 12312 | tf_op jit(solution)/shard_map/all_gather | solution.py:19
  155.6 4.6 pad.201
  161.2 4.4 pad.200
  168.5 11.2 %all-gather.1 = f32[16,1,171]{2,1,0:T(1,128)S(1)} all-gather(f32[2,1,171]{2,1,0:T(1,128)S(1)} %copy.129), channel_id=3, replica_groups=mesh['seq'=8,'ch'=16] {'seq'}, dimensions={0}, use_global_device_ids=true | all-gather | bytes 12312 | tf_op jit(solution)/shard_map/all_gather | solution.py:19
  179.8 9.0 %while.28 = (s32[]{:T(128)}, f32[2,171]{1,0:T(2,128)}, s32[]{:T(128)}, f32[8,2,171]{2,1,0:T(2,128)}, f32[8,2,171]{2,1,0:T(2,128)S(1)}, /*index=5*/s32[]{:T(128)}, s32[]{:T(128)}) while((s32[]{:T(128)}, f32[2,171]{1,0:T(2,128)}, s32[]{:T(128)}, f32[8,2,171]{2,1,0:T(2,128)}, f32[8,2,171]{2,1,0:T(2,128)S(1)}, ...), condition=%wide.region_12.13_spmd.clone, body=%wide.region_11.12_spmd.clone.sunk | while | flops 1372 | bytes 5581 | solution.py:31
  194.0 89.3 %all-reduce.67.cloned.1.call-done = f32[2,128,2048]{2,1,0:T(8,128)} async-done(((f32[2,128,2048]{2,1,0:T(8,128)}), f32[2,128,2048]{2,1,0:T(8,128)}) %all-reduce.67.cloned.1.call-update) | async-done | bytes 2097168 | tf_op jit(solution)/shard_map/psum | solution.py:144
  297.6 3.0 slice.612
  308.9 71.3 %all-reduce.69.cloned.1.call-done = bf16[2,128,2048]{2,1,0:T(8,128)(2,1)} async-done(((bf16[2,128,2048]{2,1,0:T(8,128)(2,1)}), bf16[2,128,2048]{2,1,0:T(8,128)(2,1)}) %all-reduce.69.cloned.1.call-update) | async-done | bytes 1048592 | tf_op jit(solution)/shard_map/psum | solution.py:163
  380.2 3.3 fusion.15
  391.1 3.0 slice.608
  460.7 4.5 slice.599
  525.1 3.1 pad.225
  532.4 3.1 pad.211
  544.2 3.0 slice.600
  557.5 3.1 pad.214
  560.5 4.0 pad.215
  570.1 3.1 pad.228
  573.2 3.1 pad.229
  578.0 14.0 %all-gather.2 = f32[16,1,171]{2,1,0:T(1,128)S(1)} all-gather(f32[2,1,171]{2,1,0:T(1,128)S(1)} %copy.130), channel_id=4, replica_groups=mesh['seq'=8,'ch'=16] {'seq'}, dimensions={0}, use_global_device_ids=true | all-gather | bytes 12312 | tf_op jit(solution)/shard_map/all_gather | solution.py:19
  592.1 4.8 while.29
  607.2 3.0 collective-permute-done.1
  625.5 73.9 %all-reduce.71.cloned.1.call-done = (bf16[2,128,2048]{2,1,0:T(8,128)(2,1)}, bf16[2,128,2048]{2,1,0:T(8,128)(2,1)}) async-done(((bf16[2,128,2048]{2,1,0:T(8,128)(2,1)}, bf16[2,128,2048]{2,1,0:T(8,128)(2,1)}), (bf16[2,128,2048]{2,1,0:T(8,128)(2,1)}, bf16[2,128,2048]{2,1,0:T(8,128)(2,1)})) %all-reduce.71.cloned.1.call-update) | async-done | bytes 2097168 | tf_op jit(solution)/shard_map/psum | solution.py:152
  704.4 3.3 add_convert_fusion
  709.6 53.6 %all-reduce.73.cloned.1.call-done = (bf16[1,171,171]{2,1,0:T(8,128)(2,1)}, bf16[1,171,171]{2,1,0:T(8,128)(2,1)}, bf16[128]{0:T(256)(128)(2,1)}, bf16[128]{0:T(25...) async-done(((bf16[1,171,171]{2,1,0:T(8,128)(2,1)}, ...) | async-done | bytes 120228 | tf_op jit(solution)/shard_map/psum | solution.py:230
  774.9 83.9 %all-reduce.75.cloned.1.call-done = (bf16[2048,171]{0,1:T(8,128)(2,1)}, bf16[2048,171]{0,1:T(8,128)(2,1)}, bf16[171,2048]{1,0:T(8,128)(2,1)}, bf16[2048,384]{1,0...) async-done(((bf16[2048,171]{0,1:T(8,128)(2,1)}, bf16[2048,171]{0,1:T(8,128)(2,1)}, bf16[171,2048]{1,0:T(8,128)(2,1)}, bf16[2048,384]{1,0:T(8,128)(2,1)}, ...) | async-done | bytes 6819856 | tf_op jit(solution)/shard_map/psum | solution.py:226
  (525 shorter events, 373.5 us)
Async XLA Ops:
  7.2 282.4 %copy-start = (bf16[384,2048]{1,0:T(8,128)(2,1)S(1)}, bf16[384,2048]{1,0:T(8,128)(2,1)}, u32[]{:S(2)}) copy-start(bf16[384,2048]{1,0:T(8,128)(2,1)} %param.41) | copy-start | bytes 4718596
  7.2 10.0 %copy-start.101 = (s32[3]{0:T(128)S(1)}, s32[3]{0:T(128)}, u32[]{:S(2)}) copy-start(s32[3]{0:T(128)} %param.26) | copy-start | bytes 40
  7.2 10.2 %copy-start.102 = (s32[8]{0:T(128)S(1)}, s32[8]{0:T(128)}, u32[]{:S(2)}) copy-start(s32[8]{0:T(128)} %param.25) | copy-start | bytes 100
  7.2 10.7 %copy-start.93 = (f32[171]{0:T(256)S(1)}, f32[171]{0:T(256)}, u32[]{:S(2)}) copy-start(f32[171]{0:T(256)} %param.37) | copy-start | bytes 2056
  7.2 10.8 %copy-start.92 = (f32[4,171]{1,0:T(4,128)S(1)}, f32[4,171]{1,0:T(4,128)}, u32[]{:S(2)}) copy-start(f32[4,171]{1,0:T(4,128)} %param.31) | copy-start | bytes 8212
  7.2 276.1 %all-reduce.67.cloned.1.call-start = ((), (), s32[]{:S(2)}) async-start(), calls=%async_computation | async-start | bytes 4194304 | tf_op jit(solution)/shard_map/psum | solution.py:144
  8.9 10.0 %copy-start.96 = (f32[171]{0:T(256)S(1)}, f32[171]{0:T(256)}, u32[]{:S(2)}) copy-start(f32[171]{0:T(256)} %param.32) | copy-start | bytes 2056
  10.1 9.2 %copy-start.97 = (bf16[1,171,171]{2,1,0:T(8,128)(2,1)S(1)}, bf16[1,171,171]{2,1,0:T(8,128)(2,1)}, u32[]{:S(2)}) copy-start(bf16[1,171,171]{2,1,0:T(8,128)(2,1)} %param.34) | copy-start | bytes 175450
  10.1 9.2 %copy-start.99 = (f32[171]{0:T(256)S(1)}, f32[171]{0:T(256)}, u32[]{:S(2)}) copy-start(f32[171]{0:T(256)} %param.36) | copy-start | bytes 2056
  12.2 6.5 collective-permute-start
  63.0 10.7 %copy-start.22 = (f32[2,128,171]{1,2,0:T(8,128)S(1)}, f32[2,128,171]{1,2,0:T(8,128)}, u32[]{:S(2)}) copy-start(f32[2,128,171]{1,2,0:T(8,128)} %copy-done.21) | copy-start | bytes 525316
  63.0 14.3 %copy-start.46 = (f32[2,1,171]{1,2,0:T(8,128)S(1)}, f32[2,1,171]{1,2,0:T(8,128)}, u32[]{:S(2)}) copy-start(f32[2,1,171]{1,2,0:T(8,128)} %get-tuple-element.427) | copy-start | bytes 4108
  124.0 10.8 %copy-start.45 = (f32[2,63,171]{1,2,0:T(8,128)S(1)}, f32[2,63,171]{1,2,0:T(8,128)}, u32[]{:S(2)}) copy-start(f32[2,63,171]{1,2,0:T(8,128)} %slice.534) | copy-start | bytes 258556
  130.5 10.9 %copy-start.42 = (f32[2,128,171]{1,2,0:T(8,128)}, f32[2,128,171]{1,2,0:T(8,128)S(1)}, u32[]{:S(2)}) copy-start(f32[2,128,171]{1,2,0:T(8,128)S(1)} %pad.187) | copy-start | bytes 525316
  136.5 52.3 %copy-start.6 = (bf16[2,128,2048]{2,1,0:T(8,128)(2,1)S(1)}, bf16[2,128,2048]{2,1,0:T(8,128)(2,1)}, u32[]{:S(2)}) copy-start(bf16[2,128,2048]{2,1,0:T(8,128)(2,1)} %param.23) | copy-start | bytes 3145732
  141.2 20.0 %copy-start.43 = (f32[2,128,171]{1,2,0:T(8,128)}, f32[2,128,171]{1,2,0:T(8,128)S(1)}, u32[]{:S(2)}) copy-start(f32[2,128,171]{1,2,0:T(8,128)S(1)} %pad.186) | copy-start | bytes 525316
  165.6 26.6 %copy-start.23 = (bf16[171,2048]{1,0:T(8,128)(2,1)S(1)}, bf16[171,2048]{1,0:T(8,128)(2,1)}, u32[]{:S(2)}) copy-start(bf16[171,2048]{1,0:T(8,128)(2,1)} %param.38) | copy-start | bytes 2101252
  194.0 91.4 %copy-start.62 = (f32[2048]{0:T(1024)S(1)}, f32[2048]{0:T(1024)}, u32[]{:S(2)}) copy-start(f32[2048]{0:T(1024)} %param.28) | copy-start | bytes 24580
  194.0 186.2 %all-reduce.69.cloned.1.call-start = ((), (), s32[]{:S(2)}) async-start(), calls=%async_computation.1 | async-start | bytes 2097152 | tf_op jit(solution)/shard_map/psum | solution.py:163
  294.2 10.0 %copy-start.63 = (f32[2,171]{1,0:T(2,128)S(1)}, f32[2,171]{1,0:T(2,128)}, u32[]{:S(2)}) copy-start(f32[2,171]{1,0:T(2,128)} %get-tuple-element.205) | copy-start | bytes 4108
  294.2 405.1 %all-reduce.71.cloned.1.call-start = ((), (), s32[]{:S(2)}) async-start(), calls=%async_computation.2 | async-start | bytes 4194304 | tf_op jit(solution)/shard_map/psum | solution.py:152
  305.0 78.5 %copy-start.86 = (f32[2,128]{1,0:T(2,128)S(1)}, f32[2,128]{1,0:T(2,128)}, u32[]{:S(2)}) copy-start(f32[2,128]{1,0:T(2,128)} %copy-done.85) | copy-start | bytes 3076
  305.0 78.5 %copy-start.66 = (f32[2,128]{1,0:T(2,128)S(1)}, f32[2,128]{1,0:T(2,128)}, u32[]{:S(2)}) copy-start(f32[2,128]{1,0:T(2,128)} %copy-done.65) | copy-start | bytes 3076
  557.3 15.8 %copy-start.44 = (f32[2,64,171]{1,2,0:T(8,128)S(1)}, f32[2,64,171]{1,2,0:T(8,128)}, u32[]{:S(2)}) copy-start(f32[2,64,171]{1,2,0:T(8,128)} %add.678) | copy-start | bytes 262660
  564.5 32.4 %copy-start.28 = (f32[2,128,171]{1,2,0:T(8,128)S(1)}, f32[2,128,171]{1,2,0:T(8,128)}, u32[]{:S(2)}) copy-start(f32[2,128,171]{1,2,0:T(8,128)} %copy-done.27) | copy-start | bytes 525316
  564.6 32.4 %copy-start.82 = (f32[2,128]{1,0:T(2,128)S(1)}, f32[2,128]{1,0:T(2,128)}, u32[]{:S(2)}) copy-start(f32[2,128]{1,0:T(2,128)} %copy-done.81) | copy-start | bytes 3076
  564.6 32.4 %copy-start.84 = (f32[171]{0:T(256)S(1)}, f32[171]{0:T(256)}, u32[]{:S(2)}) copy-start(f32[171]{0:T(256)} %copy-done.83) | copy-start | bytes 2056
  576.3 25.1 %copy-start.20 = (f32[2,131,171]{1,2,0:T(8,128)S(1)}, f32[2,131,171]{1,2,0:T(8,128)}, u32[]{:S(2)}) copy-start(f32[2,131,171]{1,2,0:T(8,128)} %copy-done.19) | copy-start | bytes 537628
  576.3 25.1 %copy-start.78 = (f32[2,128]{1,0:T(2,128)S(1)}, f32[2,128]{1,0:T(2,128)}, u32[]{:S(2)}) copy-start(f32[2,128]{1,0:T(2,128)} %copy-done.77) | copy-start | bytes 3076
  603.3 6.8 collective-permute-start.1
  612.6 150.5 %all-reduce.73.cloned.1.call-start = ((), (), s32[]{:S(2)}) async-start(), calls=%async_computation.3 | async-start | bytes 370688 | tf_op jit(solution)/shard_map/psum | solution.py:230
  702.2 156.5 %all-reduce.75.cloned.1.call-start = ((), (), s32[]{:S(2)}) async-start(), calls=%async_computation.4 | async-start | bytes 13762560 | tf_op jit(solution)/shard_map/psum | solution.py:226
  (82 other events, 313.5 us)
Sparse Core Ops, SparseCore 0:
  194.1 89.1 all-reduce.66
  294.3 85.8 all-reduce.68
  612.7 86.5 all-reduce.70
  703.4 59.6 all-reduce.72
  767.2 91.5 all-reduce.74
where the time goes:
time: 890 us; the launch traced here: 877 us
  waiting for transfers between devices  375 us (42%)
  local copies, waits for them, and re-layouts  263 us (30%)
  other arithmetic  145 us (16%)
  blocking collectives  38.7 us (4%)
  matrix products  31.2 us (4%)
  between operations  16.1 us (2%)
    psum x1, waiting for transfers between devices, body(): resid_mid = tokens_f + lax.psum(mix_partial, 'ch')  89.3 us
    psum x1, waiting for transfers between devices, body(): lax.psum(g_w_y.astype(jnp.bfloat16), 'seq').astype(jnp.float32)  83.9 us
    slice x41, local copies, waits for them, and re-layouts, body(): lax.associative_scan(combine, (follow_gate, d_state), reverse=True, axis=1)  82.3 us
    psum x1, waiting for transfers between devices, body(): lax.psum(partial_out.astype(jnp.bfloat16), 'ch').astype(jnp.float32)  73.9 us
    psum x1, waiting for transfers between devices, body(): lax.psum(partial_two.astype(jnp.bfloat16), 'ch').astype(jnp.float32)  71.3 us
    pad x24, local copies, waits for them, and re-layouts, body(): lax.associative_scan(combine, (follow_gate, d_state), reverse=True, axis=1)  62.7 us
    psum x1, waiting for transfers between devices, body(): lax.psum(g_gate_a.astype(jnp.bfloat16), 'seq').astype(jnp.float32)  53.6 us
    slice x34, local copies, waits for them, and re-layouts, body(): lax.associative_scan(combine, (keep_gate, drive_term), axis=1)  49.7 us
  transfers between devices with their start and end apart: 7, of which 6 were waited for; matrix products, arithmetic and copies ran while one was open for 5% of the time, Pallas kernels for 0%

commit v1 on v0

v1 whole, which is shorter than its diff:
```python
from functools import partial

import jax
import jax.numpy as jnp
from jax import lax
from jax.experimental import pallas as pl
from jax.experimental.pallas import tpu as pltpu
from jax.sharding import PartitionSpec as P

EPS_NORM = 1e-06
F32 = jnp.float32
BF16 = jnp.bfloat16
TAPS = 4
HALO = 8


def dot(left, right, contract):
    return lax.dot_general(left, right, (contract, ((), ())), preferred_element_type=F32)


def expm1_neg(x):
    series = x * (
        1.0
        + x * (1 / 2)
        * (1.0 + x * (1 / 3) * (1.0 + x * (1 / 4) * (1.0 + x * (1 / 5) * (1.0 + x * (1 / 6) * (1.0 + x * (1 / 7))))))
    )
    return jnp.where(x > -0.35, series, jnp.exp(x) - 1.0)


def doc_masks(ends, count, start, rows):
    positions = start + lax.broadcasted_iota(jnp.int32, (rows, 1), 0)

    def doc(at):
        total = jnp.zeros((rows, 1), jnp.int32)
        for j in range(count):
            total = total + (at >= ends[j]).astype(jnp.int32)
        return total

    here = doc(positions)
    masks = [jnp.ones((rows, 1), F32)]
    for k in range(1, TAPS):
        same = (here == doc(positions - k)) & (positions >= k)
        masks.append(same.astype(F32))
    return masks


def row_ends(length_ref, count):
    ends, total = [], 0
    for j in range(count):
        total = total + length_ref[j]
        ends.append(total)
    return ends


def forward_kernel(
    start_ref,
    short_ref,
    long_ref,
    conv_in_ref,
    edge_ref,
    conv_w_ref,
    conv_b_ref,
    gate_a_ref,
    gate_x_ref,
    bias_a_ref,
    bias_x_ref,
    decay_ref,
    conv_out_ref,
    rate_ref,
    inlet_ref,
    keep_ref,
    run_ref,
    state_ref,
    carry_ref,
    ext,
):
    groups, rows, chans = conv_in_ref.shape
    for g in range(groups):
        length_ref = (short_ref, long_ref)[g]
        count = length_ref.shape[0]
        masks = doc_masks(row_ends(length_ref, count), count, start_ref[0], rows)
        ext[g, HALO - TAPS + 1 : HALO, :] = edge_ref[g].astype(F32)
        ext[g, HALO:, :] = conv_in_ref[g].astype(F32)
        conv_out = jnp.broadcast_to(conv_b_ref[...], (rows, chans))
        for k in range(TAPS):
            conv_out = (
                conv_out + conv_w_ref[k : k + 1, :] * ext[g, HALO - k : HALO - k + rows, :] * masks[k]
            )
        conv_out_ref[g] = conv_out
        low = conv_out.astype(BF16)
        rate = jax.nn.sigmoid(dot(low, gate_a_ref[0], ((1,), (0,))) + bias_a_ref[...])
        inlet = jax.nn.sigmoid(dot(low, gate_x_ref[0], ((1,), (0,))) + bias_x_ref[...])
        rate_ref[g] = rate
        inlet_ref[g] = inlet
        log_decay = decay_ref[...] * rate
        keep_ref[g] = jnp.exp(log_decay) * masks[1]
        state_ref[g] = jnp.sqrt(-expm1_neg(2.0 * log_decay)) * inlet * conv_out

    def step(t, carried):
        out = []
        for g in range(groups):
            run, state = carried[g]
            keep = keep_ref[g, pl.ds(t, 1), :]
            run = run * keep
            state = state * keep + state_ref[g, pl.ds(t, 1), :]
            run_ref[g, pl.ds(t, 1), :] = run
            state_ref[g, pl.ds(t, 1), :] = state
            out.append((run, state))
        return tuple(out)

    first = tuple((jnp.ones((1, chans), F32), jnp.zeros((1, chans), F32)) for _ in range(groups))
    last = lax.fori_loop(0, rows, step, first, unroll=8)
    for g in range(groups):
        carry_ref[0, g : g + 1, :] = last[g][0]
        carry_ref[1, g : g + 1, :] = last[g][1]


def gelu_parts(x):
    root = 0.7978845608028654
    cubic = 0.044715
    inner = root * (x + cubic * x * x * x)
    th = jnp.tanh(inner)
    half = 0.5 * (1.0 + th)
    slope = half + 0.5 * x * (1.0 - th * th) * root * (1.0 + 3.0 * cubic * x * x)
    return x * half, slope


def adjoint_kernel(
    d_mixed_ref,
    gate_pre_ref,
    hidden_ref,
    keep_ref,
    d_gate_pre_ref,
    reach_ref,
    adj_ref,
    carry_ref,
):
    groups, rows, chans = d_mixed_ref.shape
    for g in range(groups):
        branch, slope = gelu_parts(gate_pre_ref[g])
        d_mixed = d_mixed_ref[g]
        d_gate_pre_ref[g] = (d_mixed * hidden_ref[g] * slope).astype(BF16)
        adj_ref[g] = d_mixed * branch

    def step(i, carried):
        t = rows - 1 - i
        out = []
        for g in range(groups):
            reach, passed = carried[g]
            adj = adj_ref[g, pl.ds(t, 1), :] + passed
            adj_ref[g, pl.ds(t, 1), :] = adj
            reach_ref[g, pl.ds(t, 1), :] = reach
            keep = keep_ref[g, pl.ds(t, 1), :]
            out.append((reach * keep, adj * keep))
        return tuple(out)

    first = tuple((jnp.ones((1, chans), F32), jnp.zeros((1, chans), F32)) for _ in range(groups))
    last = lax.fori_loop(0, rows, step, first, unroll=8)
    for g in range(groups):
        carry_ref[0, g : g + 1, :] = last[g][0]
        carry_ref[1, g : g + 1, :] = last[g][1]


def gates_back_kernel(
    start_ref,
    short_ref,
    long_ref,
    adj_ref,
    reach_ref,
    beyond_ref,
    state_in_ref,
    hidden_ref,
    keep_ref,
    rate_ref,
    inlet_ref,
    conv_out_ref,
    conv_in_ref,
    edge_ref,
    conv_w_ref,
    gate_a_ref,
    gate_x_ref,
    decay_ref,
    lam_slope_ref,
    d_conv_head_ref,
    d_input_ref,
    g_gate_a_ref,
    g_gate_x_ref,
    g_rows_ref,
    ext,
    prior,
    d_ext,
):
    groups, rows, chans = adj_ref.shape
    sums = [jnp.zeros((1, chans), F32) for _ in range(8)]
    for g in range(groups):
        length_ref = (short_ref, long_ref)[g]
        count = length_ref.shape[0]
        ends = row_ends(length_ref, count)
        masks = doc_masks(ends, count, start_ref[0], rows)
        adjoint = adj_ref[g] + reach_ref[g] * beyond_ref[g : g + 1, :]
        prior[HALO - 1 : HALO, :] = state_in_ref[g : g + 1, :]
        prior[HALO:, :] = hidden_ref[g]
        d_keep = adjoint * prior[HALO - 1 : HALO - 1 + rows, :]
        rate = rate_ref[g]
        inlet = inlet_ref[g]
        conv_out = conv_out_ref[g]
        decay = decay_ref[...]
        log_decay = decay * rate
        square = -expm1_neg(2.0 * log_decay)
        root = jnp.sqrt(square)
        driven = adjoint * conv_out
        d_log = d_keep * keep_ref[g] - driven * inlet * (1.0 - square) / root
        d_rate_pre = d_log * decay * rate * (1.0 - rate)
        d_inlet_pre = driven * root * inlet * (1.0 - inlet)
        sums[0] = sums[0] + jnp.sum(d_rate_pre, axis=0, keepdims=True)
        sums[1] = sums[1] + jnp.sum(d_inlet_pre, axis=0, keepdims=True)
        sums[2] = sums[2] + jnp.sum(d_log * rate, axis=0, keepdims=True)
        low = conv_out.astype(BF16)
        low_a = d_rate_pre.astype(BF16)
        low_x = d_inlet_pre.astype(BF16)
        grad_a = dot(low, low_a, ((0,), (0,)))
        grad_x = dot(low, low_x, ((0,), (0,)))
        if g == 0:
            g_gate_a_ref[...] = grad_a
            g_gate_x_ref[...] = grad_x
        else:
            g_gate_a_ref[...] += grad_a
            g_gate_x_ref[...] += grad_x
        d_conv = (
            adjoint * root * inlet
            + dot(low_a, gate_a_ref[0], ((1,), (1,)))
            + dot(low_x, gate_x_ref[0], ((1,), (1,)))
        )
        sums[3] = sums[3] + jnp.sum(d_conv, axis=0, keepdims=True)
        ext[HALO - TAPS + 1 : HALO, :] = edge_ref[g].astype(F32)
        ext[HALO:, :] = conv_in_ref[g].astype(F32)
        d_input = conv_w_ref[0:1, :] * d_conv
        sums[4] = sums[4] + jnp.sum(d_conv * ext[HALO:, :], axis=0, keepdims=True)
        d_ext[rows:, :] = jnp.zeros((HALO, chans), F32)
        for k in range(1, TAPS):
            masked = d_conv * masks[k]
            sums[4 + k] = sums[4 + k] + jnp.sum(
                masked * ext[HALO - k : HALO - k + rows, :], axis=0, keepdims=True
            )
            d_ext[:rows, :] = masked
            d_input = d_input + conv_w_ref[k : k + 1, :] * d_ext[k : k + rows, :]
        d_input_ref[g] = d_input
        d_conv_head_ref[g] = d_conv[: TAPS - 1, :]
    sums[2] = sums[2] * lam_slope_ref[...]
    for i, total in enumerate(sums):
        g_rows_ref[i : i + 1, :] = total


def sds(shape, dtype=F32):
    return jax.ShapeDtypeStruct(shape, dtype)


def run_kernel(kernel, name, outs, ins, scratch=(), flops=0, smem=0):
    vmem = pl.BlockSpec(memory_space=pltpu.VMEM)
    scalar = pl.BlockSpec(memory_space=pltpu.SMEM)
    moved = sum(a.size * a.dtype.itemsize for a in list(ins) + list(outs))
    return pl.pallas_call(
        kernel,
        name=name,
        out_shape=outs,
        in_specs=[scalar] * smem + [vmem] * (len(ins) - smem),
        out_specs=[vmem] * len(outs),
        scratch_shapes=list(scratch),
        cost_estimate=pl.CostEstimate(flops=flops, bytes_accessed=moved, transcendentals=0),
        compiler_params=pltpu.CompilerParams(vmem_limit_bytes=32 * 1024 * 1024),
    )(*ins)


def shifted(block, axis, distance):
    count = lax.axis_size(axis)
    route = [(i - distance, i) for i in range(count) if 0 <= i - distance < count]
    return lax.ppermute(block, axis, route)


def gather_small(value, axis):
    count = lax.axis_size(axis)
    return lax.all_to_all(jnp.broadcast_to(value[None], (count,) + value.shape), axis, 0, 0)


def carried_in(value, axis, backward):
    count, mine = lax.axis_size(axis), lax.axis_index(axis)
    pieces = gather_small(value, axis)
    total = jnp.zeros(value.shape[1:], F32)
    order = range(count - 1, 0, -1) if backward else range(count - 1)
    for j in order:
        longer = pieces[j, 1] + pieces[j, 0] * total
        total = jnp.where((j > mine) if backward else (j < mine), longer, total)
    return total


def scatter_rows(partial_sum, extra=None):
    count = lax.axis_size("ch")
    rows, width = partial_sum.shape
    pieces = partial_sum.astype(BF16).reshape(count, rows // count, width)
    if extra is not None:
        extra = jnp.pad(extra.astype(BF16).reshape(count, 1, -1), ((0, 0), (0, rows // count - 1), (0, 0)))
        pieces = jnp.concatenate([pieces, extra], axis=-1)
    got = lax.all_to_all(pieces, "ch", 0, 0)
    total = jnp.sum(got.astype(F32), axis=0)
    if extra is not None:
        return total[:, :width], total[0, width:]
    return total


def gather_rows(share):
    count = lax.axis_size("ch")
    got = lax.all_to_all(jnp.broadcast_to(share[None], (count,) + share.shape), "ch", 0, 0)
    return got.reshape(count * share.shape[0], share.shape[1])


def seq_scatter(bundle):
    return lax.psum_scatter(bundle.astype(BF16), "seq", scatter_dimension=0, tiled=True)


def seq_gather(share):
    return lax.all_gather(share, "seq", axis=0, tiled=True)


def rms(features):
    return lax.rsqrt(jnp.mean(features * features, axis=-1, keepdims=True) + EPS_NORM)


def norm_back(features, scale, gain, grad):
    gained = gain * grad
    mean = jnp.mean(gained * features, axis=-1, keepdims=True)
    return scale * gained - features * (scale * scale * scale) * mean


def body(
    tokens,
    cotangent,
    short_lengths,
    long_lengths,
    gain_one,
    gain_two,
    w_y,
    w_x,
    conv_w,
    conv_b,
    gate_a,
    gate_x,
    bias_a,
    bias_x,
    lam,
    w_out,
    w_one,
    w_two,
    w_three,
):
    groups, rows, width = tokens.shape
    chans = w_x.shape[1]
    hidden_units = w_one.shape[1]
    total_rows = groups * rows
    ch_count, ch_index = lax.axis_size("ch"), lax.axis_index("ch")
    seq_count, seq_index = lax.axis_size("seq"), lax.axis_index("seq")
    share_rows = total_rows // ch_count
    share_width = width // ch_count
    start = (seq_index * rows).astype(jnp.int32)[None]
    grouped = lambda a: a.reshape(groups, rows, a.shape[-1])
    mine = lambda a: lax.dynamic_slice_in_dim(a, ch_index * share_rows, share_rows, 0)

    tokens = tokens.reshape(total_rows, width)
    cotangent = cotangent.reshape(total_rows, width)
    tokens_f = tokens.astype(F32)
    scale_one = rms(tokens_f)
    normed_one = (tokens_f * scale_one * gain_one).astype(BF16)
    conv_input = grouped(dot(normed_one, w_x, ((1,), (0,))).astype(BF16))
    edge = shifted(conv_input[:, rows - TAPS + 1 :], "seq", 1)
    gate_pre = grouped(dot(normed_one, w_y, ((1,), (0,))))

    decay = (-8.0 * jax.nn.softplus(-lam))[None]
    lam_slope = (8.0 * jax.nn.sigmoid(-lam))[None]
    big = sds((groups, rows, chans))
    flops = 2 * total_rows * chans * chans
    conv_out, rate, inlet, keep, decay_run, local_state, carry = run_kernel(
        forward_kernel,
        "conv_gates_scan",
        [big] * 6 + [sds((2, groups, chans))],
        [
            start,
            short_lengths,
            long_lengths,
            conv_input,
            edge,
            conv_w,
            conv_b[None],
            gate_a,
            gate_x,
            bias_a[None],
            bias_x[None],
            decay,
        ],
        [pltpu.VMEM((groups, HALO + rows, chans), F32)],
        flops=2 * flops,
        smem=3,
    )
    state_in = carried_in(carry, "seq", False)
    hidden = local_state + decay_run * state_in[:, None]
    mixed_in = (hidden * jax.nn.gelu(gate_pre, approximate=True)).astype(BF16)
    mixed_in = mixed_in.reshape(total_rows, chans)
    mix_share = scatter_rows(dot(mixed_in, w_out, ((1,), (0,))))
    resid_share = mine(tokens_f) + mix_share
    scale_two = rms(resid_share)
    normed_two = gather_rows((resid_share * scale_two * gain_two).astype(BF16))

    mlp_gate = dot(normed_two, w_one, ((1,), (0,)))
    mlp_up = dot(normed_two, w_two, ((1,), (0,)))
    gate_value, gate_slope = gelu_parts(mlp_gate)
    mlp_hidden = (gate_value * mlp_up).astype(BF16)
    d_hidden = dot(cotangent, w_three, ((1,), (1,)))
    d_gate = (d_hidden * mlp_up * gate_slope).astype(BF16)
    d_up = (d_hidden * gate_value).astype(BF16)
    partial_two = dot(d_gate, w_one, ((1,), (1,))) + dot(d_up, w_two, ((1,), (1,)))
    gain_two_share = resid_share * scale_two
    sum_two = scatter_rows(partial_two)
    gain_two_part = jnp.sum(sum_two * gain_two_share, axis=0)
    d_mid = mine(cotangent.astype(F32)) + norm_back(resid_share, scale_two, gain_two, sum_two)
    d_mix = gather_rows(d_mid.astype(BF16))

    g_mlp = jnp.concatenate(
        [
            dot(normed_two, d_gate, ((0,), (0,))).astype(BF16),
            dot(normed_two, d_up, ((0,), (0,))).astype(BF16),
            dot(cotangent, mlp_hidden, ((0,), (0,))).astype(BF16),
        ],
        axis=1,
    )
    g_mlp = seq_gather(seq_scatter(g_mlp))

    d_mixed = grouped(dot(d_mix, w_out, ((1,), (1,))))
    d_gate_pre, reach, local_adjoint, carry_back = run_kernel(
        adjoint_kernel,
        "adjoint_scan",
        [sds((groups, rows, chans), BF16), big, big, sds((2, groups, chans))],
        [d_mixed, gate_pre, hidden, keep],
    )
    beyond = carried_in(carry_back, "seq", True)
    d_conv_head, d_input, g_gate_a, g_gate_x, g_rows = run_kernel(
        gates_back_kernel,
        "gates_back",
        [
            sds((groups, TAPS - 1, chans)),
            big,
            sds((chans, chans)),
            sds((chans, chans)),
            sds((8, chans)),
        ],
        [
            start,
            short_lengths,
            long_lengths,
            local_adjoint,
            reach,
            beyond,
            state_in,
            hidden,
            keep,
            rate,
            inlet,
            conv_out,
            conv_input,
            edge,
            conv_w,
            gate_a,
            gate_x,
            decay,
            lam_slope,
        ],
        [
            pltpu.VMEM((HALO + rows, chans), F32),
            pltpu.VMEM((HALO + rows, chans), F32),
            pltpu.VMEM((rows + HALO, chans), F32),
        ],
        flops=4 * flops,
        smem=3,
    )
    lead = shifted(d_conv_head, "seq", -1)
    ahead = start[0] + rows + jnp.arange(TAPS - 1, dtype=jnp.int32)
    lead_masks = []
    for lengths in (short_lengths, long_lengths):
        ends = jnp.cumsum(lengths)
        doc = lambda at: jnp.sum((at[:, None] >= ends[None, :]).astype(jnp.int32), axis=1)
        lead_masks.append(jnp.stack([(doc(ahead) == doc(ahead - k)).astype(F32) for k in range(TAPS)]))
    lead_masks = jnp.stack(lead_masks)
    late = []
    for i in range(TAPS - 1):
        total = jnp.zeros((groups, chans), F32)
        for k in range(TAPS):
            j = i + k - (TAPS - 1)
            if j >= 0:
                total = total + conv_w[k] * lead_masks[:, k, j, None] * lead[:, j]
        late.append(total)
    late = jnp.pad(jnp.stack(late, axis=1), ((0, 0), (rows - TAPS + 1, 0), (0, 0)))
    d_input = (d_input + late).astype(BF16).reshape(total_rows, chans)
    d_gate_pre = d_gate_pre.reshape(total_rows, chans)

    partial_one = dot(d_input, w_x, ((1,), (1,))) + dot(d_gate_pre, w_y, ((1,), (1,)))
    gain_one_part = jnp.sum(partial_one * (tokens_f * scale_one), axis=0)
    sum_one, g_gain_one = scatter_rows(partial_one, gain_one_part)
    tokens_share = mine(tokens_f)
    d_tokens = d_mid + norm_back(tokens_share, mine(scale_one), gain_one, sum_one)
    d_tokens = grouped(gather_rows(d_tokens.astype(BF16)).astype(F32))

    gain_two_got = lax.all_to_all(gain_two_part.reshape(ch_count, share_width), "ch", 0, 0)
    g_gain_two = jnp.sum(gain_two_got, axis=0)

    partial_out = dot(mlp_hidden, w_three, ((1,), (0,)))
    out_share = resid_share + scatter_rows(partial_out)
    layer_out = grouped(gather_rows(out_share.astype(BF16)))

    g_mid = jnp.concatenate(
        [
            dot(normed_one, d_gate_pre, ((0,), (0,))).astype(BF16),
            dot(d_mix, mixed_in, ((0,), (0,))).astype(BF16),
        ],
        axis=1,
    )
    g_mid = seq_gather(seq_scatter(g_mid))

    g_w_x = dot(normed_one, d_input, ((0,), (0,)))
    gains = jnp.pad(jnp.stack([g_gain_one, g_gain_two]), ((0, 0), (0, chans - share_width)))
    tail = jnp.concatenate([g_w_x, g_gate_a, g_gate_x, g_rows, gains], axis=0).astype(BF16)
    tail_rows = tail.shape[0]
    tail = jnp.pad(tail, ((0, -tail_rows % (16 * seq_count)), (0, 0)))
    tail = seq_gather(seq_scatter(tail)).astype(F32)
    at = width
    g_gate_a = tail[at : at + chans][None]
    g_gate_x = tail[at + chans : at + 2 * chans][None]
    at = at + 2 * chans
    return (
        layer_out,
        d_tokens,
        tail[at + 8, :share_width],
        tail[at + 9, :share_width],
        g_mid[:, :chans].astype(F32),
        tail[:width],
        tail[at + 4 : at + 8],
        tail[at + 3],
        g_gate_a,
        g_gate_x,
        tail[at],
        tail[at + 1],
        tail[at + 2],
        g_mid[:, chans:].astype(F32).T,
        g_mlp[:, :hidden_units].astype(F32),
        g_mlp[:, hidden_units : 2 * hidden_units].astype(F32),
        g_mlp[:, 2 * hidden_units :].astype(F32).T,
    )


def solution(mesh):
    tokens_spec = P(None, "seq", None)
    column = P(None, "ch")
    block = P("ch", None, None)
    row = P("ch", None)
    vector = P("ch")
    return jax.shard_map(
        body,
        mesh=mesh,
        in_specs=(
            tokens_spec,
            tokens_spec,
            P(),
            P(),
            P(),
            P(),
            column,
            column,
            column,
            vector,
            block,
            block,
            vector,
            vector,
            vector,
            row,
            column,
            column,
            row,
        ),
        out_specs=(
            tokens_spec,
            tokens_spec,
            vector,
            vector,
            column,
            column,
            column,
            vector,
            block,
            block,
            vector,
            vector,
            vector,
            row,
            column,
            column,
            row,
        ),
        check_vma=False,
    )
```

time: 890 us -> 348 us (0.39); the launches traced: 877 us -> 346 us
  waiting for transfers between devices: 375 us -> 127 us
  local copies, waits for them, and re-layouts: 263 us -> 27.2 us
  other arithmetic: 145 us -> 32.6 us
  starting transfers between devices: 7.71 us -> 55.5 us
  blocking collectives: 38.7 us -> 62.9 us
  matrix products: 31.2 us -> 21.5 us
    psum x5 -> x0, waiting for transfers between devices: 372 us -> none  [the longest x1 89.3 us: body(): resid_mid = tokens_f + lax.psum(mix_partial, 'ch')]
    slice x80 -> x7, local copies, waits for them, and re-layouts: 133 us -> 2.98 us  [the longest x1 1.26 us: body(): tail[:width]]
    pad x48 -> x2, local copies, waits for them, and re-layouts: 109 us -> 1.25 us  [the longest x1 1.24 us: body(): tail = jnp.pad(tail, ((0, -tail_rows % (16 * seq_count)), (0, 0)))]
    all_to_all x0 -> x9, waiting for transfers between devices: none -> 92 us  [the longest x4 56.8 us: scatter_rows(): got = lax.all_to_all(pieces, 'ch', 0, 0)]
    all_to_all x0 -> x9, starting transfers between devices: none -> 47.4 us  [the longest x4 20.2 us: scatter_rows(): got = lax.all_to_all(pieces, 'ch', 0, 0)]
    all_to_all x0 -> x2, blocking collectives: none -> 37.7 us  [gather_rows(): lax.all_to_all(jnp.broadcast_to(share[None], (count,) + share.shape), 'ch...]
    mul x27 -> x3, other arithmetic: 33.7 us -> 0.65 us  [the longest x2 0.63 us: norm_back(): return scale * gained - features * (scale * scale * scale) * mean]
    add x31 -> x2, other arithmetic: 31.2 us -> 0.09 us  [the longest x1 0.08 us: body(): total = total + conv_w[k] * lead_masks[:, k, j, None] * lead[:, j]]
  transfers between devices with their start and end apart: 7 -> 16, of which waited for: 6 -> 12; matrix products, arithmetic and copies ran while one was open for 5% -> 13% of each run, Pallas kernels for 0% -> 1%
where the time goes in v1:
time: 348 us; the launch traced here: 346 us
  waiting for transfers between devices  127 us (36%)
  blocking collectives  62.9 us (18%)
  starting transfers between devices  55.5 us (16%)
  other arithmetic  32.6 us (9%)
  local copies, waits for them, and re-layouts  27.2 us (8%)
  matrix products  21.5 us (6%)
  between operations  14.7 us (4%)
  Pallas kernels  5.04 us (1%)
    all_to_all x4, waiting for transfers between devices, scatter_rows(): got = lax.all_to_all(pieces, 'ch', 0, 0)  56.8 us
    all_to_all x2, blocking collectives, gather_rows(): lax.all_to_all(jnp.broadcast_to(share[None], (count,) + share.shape), 'ch...  37.7 us
    all_gather x2, waiting for transfers between devices, seq_gather(): return lax.all_gather(share, 'seq', axis=0, tiled=True)  26.1 us
    all_gather x1, blocking collectives, seq_gather(): return lax.all_gather(share, 'seq', axis=0, tiled=True)  25.1 us
    all_to_all x2, waiting for transfers between devices, gather_rows(): lax.all_to_all(jnp.broadcast_to(share[None], (count,) + share.shape), 'ch...  24.9 us
    dot_general x18, matrix products, dot(): lax.dot_general(left, right, (contract, ((), ())), preferred_element_type...  21.5 us
    all_to_all x4, starting transfers between devices, scatter_rows(): got = lax.all_to_all(pieces, 'ch', 0, 0)  20.2 us
    unnamed x98, local copies, waits for them, and re-layouts  16.4 us
  transfers between devices with their start and end apart: 16, of which 12 were waited for; matrix products, arithmetic and copies ran while one was open for 13% of the time, Pallas kernels for 1%

profile of v1, /device:TPU:1, one launch (start us, length us, event | category | flops | bytes accessed | tf_op | source)
XLA Modules:
  0.0 346.3 jit_solution(10104321066459249242)
XLA Ops:
  10.9 4.9 %collective-permute-start = (bf16[2,3,171]{2,1,0:T(4,128)(2,1)S(1)}, bf16[2,3,171]{2,1,0:T(4,128)(2,1)S(1)}, u32[]{:S(2)}, u32[]{:S(2)}) collective-permute-start(bf16[2,3,171]{2,1,0:T(4,128)(2,1)S(1)} %slice.248), channel_id=1, source_target_pairs={{0,16},{16,32},{32,48},{48,64},{64,80},{80,96},{96,112},{1,17},{17... | collective-permute-start | bytes 6164 | tf_op jit(solution)/shard_map/ppermute | solution.py:277
  20.8 6.1 %all-to-all-start = ((f32[8,2,2,171]{3,2,1,0:T(2,128)}), f32[8,2,2,171]{3,2,1,0:T(2,128)S(1)}, u32[]{:S(2)}, u32[]{:S(2)}) async-start(f32[8,2,2,171]{3,2,1,0:T(2,128)} %broadcast_in_dim.33), calls=%async_computation | async-start | bytes 65536 | tf_op jit(solution)/shard_map/all_to_all | solution.py:282
  28.8 2.8 all-to-all-done
  33.4 2.5 convolution_convert_fusion.4
  35.9 6.9 %all-to-all-start.1 = ((bf16[16,16,2048]{2,1,0:T(8,128)(2,1)}), bf16[16,16,2048]{2,1,0:T(8,128)(2,1)}, u32[]{:S(2)}, u32[]{:S(2)}) async-start(bf16[16,16,2048]{2,1,0:T(8,128)(2,1)} %bitcast.358), calls=%async_computation.1 | async-start | bytes 2097152 | tf_op jit(solution)/shard_map/all_to_all | solution.py:303
  42.9 16.0 %all-to-all-done.1 = bf16[16,16,2048]{2,1,0:T(8,128)(2,1)} async-done(((bf16[16,16,2048]{2,1,0:T(8,128)(2,1)}), bf16[16,16,2048]{2,1,0:T(8,128)(2,1)}, u32[]{:S(2)}, u32[]{:S(2)}) %all-to-all-start.1) | async-done | bytes 1048608 | tf_op jit(solution)/shard_map/all_to_all | solution.py:303
  62.3 20.1 %all_to_all.59 = bf16[16,16,2048]{2,1,0:T(8,128)(2,1)S(1)} all-to-all(bf16[16,16,2048]{2,1,0:T(8,128)(2,1)S(1)} %broadcast_in_dim.34), channel_id=1, replica_groups=mesh['seq'=8,'ch'=16] {'ch'}, dimensions={0} | all-to-all | bytes 2097152 | tf_op jit(solution)/shard_map/all_to_all | solution.py:312
  88.4 4.3 %all-to-all-start.5 = ((bf16[16,16,2048]{2,1,0:T(8,128)(2,1)}), bf16[16,16,2048]{2,1,0:T(8,128)(2,1)}, u32[]{:S(2)}, u32[]{:S(2)}) async-start(bf16[16,16,2048]{2,1,0:T(8,128)(2,1)} %bitcast.355), calls=%async_computation.5 | async-start | bytes 2097152 | tf_op jit(solution)/shard_map/all_to_all | solution.py:303
  92.7 2.6 convolution_convert_fusion.3
  95.3 12.3 %all-to-all-done.5 = bf16[16,16,2048]{2,1,0:T(8,128)(2,1)} async-done(((bf16[16,16,2048]{2,1,0:T(8,128)(2,1)}), bf16[16,16,2048]{2,1,0:T(8,128)(2,1)}, u32[]{:S(2)}, u32[]{:S(2)}) %all-to-all-start.5) | async-done | bytes 1048608 | tf_op jit(solution)/shard_map/all_to_all | solution.py:303
  107.6 4.6 %all-to-all-start.3 = ((bf16[16,16,2048]{2,1,0:T(8,128)(2,1)}), bf16[16,16,2048]{2,1,0:T(8,128)(2,1)S(1)}, u32[]{:S(2)}, u32[]{:S(2)}) async-start(bf16[16,16,2048]{2,1,0:T(8,128)(2,1)} %bitcast.359), calls=%async_computation.3 | async-start | bytes 2097152 | tf_op jit(solution)/shard_map/all_to_all | solution.py:303
  114.8 12.1 %all-to-all-done.3 = bf16[16,16,2048]{2,1,0:T(8,128)(2,1)S(1)} async-done(((bf16[16,16,2048]{2,1,0:T(8,128)(2,1)}), bf16[16,16,2048]{2,1,0:T(8,128)(2,1)S(1)}, u32[]{:S(2)}, u32[]{:S(2)}) %all-to-all-start.3) | async-done | bytes 1048608 | tf_op jit(solution)/shard_map/all_to_all | solution.py:303
  128.3 17.7 %all_to_all.60 = bf16[16,16,2048]{2,1,0:T(8,128)(2,1)S(1)} all-to-all(bf16[16,16,2048]{2,1,0:T(8,128)(2,1)S(1)} %broadcast_in_dim.36), channel_id=1, replica_groups=mesh['seq'=8,'ch'=16] {'ch'}, dimensions={0} | all-to-all | bytes 2097152 | tf_op jit(solution)/shard_map/all_to_all | solution.py:312
  154.3 2.5 pad_maximum_fusion
  158.3 7.5 %all-to-all-start.7 = ((f32[8,2,2,171]{3,2,1,0:T(2,128)}), f32[8,2,2,171]{3,2,1,0:T(2,128)S(1)}, u32[]{:S(2)}, u32[]{:S(2)}) async-start(f32[8,2,2,171]{3,2,1,0:T(2,128)} %broadcast_in_dim.37), calls=%async_computation.7 | async-start | bytes 65536 | tf_op jit(solution)/shard_map/all_to_all | solution.py:282
  165.8 4.7 %all-to-all-done.7 = f32[8,2,2,171]{3,2,1,0:T(2,128)S(1)} async-done(((f32[8,2,2,171]{3,2,1,0:T(2,128)}), f32[8,2,2,171]{3,2,1,0:T(2,128)S(1)}, u32[]{:S(2)}, u32[]{:S(2)}) %all-to-all-start.7) | async-done | bytes 21920 | tf_op jit(solution)/shard_map/all_to_all | solution.py:282
  172.6 2.8 collective-permute-start.1
  175.7 3.5 %all-to-all-start.10 = ((f32[16,1,128]{2,1,0:T(1,128)}), f32[16,1,128]{2,1,0:T(1,128)S(1)}, u32[]{:S(2)}, u32[]{:S(2)}) async-start(f32[16,1,128]{2,1,0:T(1,128)} %bitcast.69), calls=%async_computation.10 | async-start | bytes 16384 | tf_op jit(solution)/shard_map/all_to_all | solution.py:509
  182.6 2.8 all-to-all-done.10
  185.4 4.4 %all-to-all-start.8 = ((bf16[16,16,2176]{2,1,0:T(8,128)(2,1)}), bf16[16,16,2176]{2,1,0:T(8,128)(2,1)}, u32[]{:S(2)}, u32[]{:S(2)}) async-start(bf16[16,16,2176]{2,1,0:T(8,128)(2,1)} %fusion.5), calls=%async_computation.8 | async-start | bytes 2228224 | tf_op jit(solution)/shard_map/all_to_all | solution.py:303
  190.8 16.4 %all-to-all-done.8 = bf16[16,16,2176]{2,1,0:T(8,128)(2,1)} async-done(((bf16[16,16,2176]{2,1,0:T(8,128)(2,1)}), bf16[16,16,2176]{2,1,0:T(8,128)(2,1)}, u32[]{:S(2)}, u32[]{:S(2)}) %all-to-all-start.8) | async-done | bytes 1114144 | tf_op jit(solution)/shard_map/all_to_all | solution.py:303
  212.1 7.5 %reduce-scatter.8.cloned.1.call-done = bf16[256,1152]{0,1:T(8,128)(2,1)} async-done(((bf16[2048,1152]{0,1:T(8,128)(2,1)}), bf16[256,1152]{0,1:T(8,128)(2,1)}) %reduce-scatter.8.cloned.1.call-update) | async-done | bytes 589840 | tf_op jit(solution)/shard_map/reduce_scatter | solution.py:317
  220.7 6.5 %all-to-all-start.4 = ((bf16[16,16,2048]{2,1,0:T(8,128)(2,1)}), bf16[16,16,2048]{2,1,0:T(8,128)(2,1)S(1)}, u32[]{:S(2)}, u32[]{:S(2)}) async-start(bf16[16,16,2048]{2,1,0:T(8,128)(2,1)} %broadcast_in_dim.35), calls=%async_computation.4 | async-start | bytes 2097152 | tf_op jit(solution)/shard_map/all_to_all | solution.py:312
  229.4 11.6 %all-to-all-done.4 = bf16[16,16,2048]{2,1,0:T(8,128)(2,1)S(1)} async-done(((bf16[16,16,2048]{2,1,0:T(8,128)(2,1)}), bf16[16,16,2048]{2,1,0:T(8,128)(2,1)S(1)}, u32[]{:S(2)}, u32[]{:S(2)}) %all-to-all-start.4) | async-done | bytes 1048608 | tf_op jit(solution)/shard_map/all_to_all | solution.py:312
  242.1 3.7 %all-to-all-start.9 = ((bf16[16,16,2048]{2,1,0:T(8,128)(2,1)}), bf16[16,16,2048]{2,1,0:T(8,128)(2,1)S(1)}, u32[]{:S(2)}, u32[]{:S(2)}) async-start(bf16[16,16,2048]{2,1,0:T(8,128)(2,1)} %broadcast_in_dim.39), calls=%async_computation.9 | async-start | bytes 2097152 | tf_op jit(solution)/shard_map/all_to_all | solution.py:312
  245.8 13.3 %all-to-all-done.9 = bf16[16,16,2048]{2,1,0:T(8,128)(2,1)S(1)} async-done(((bf16[16,16,2048]{2,1,0:T(8,128)(2,1)}), bf16[16,16,2048]{2,1,0:T(8,128)(2,1)S(1)}, u32[]{:S(2)}, u32[]{:S(2)}) %all-to-all-start.9) | async-done | bytes 1048608 | tf_op jit(solution)/shard_map/all_to_all | solution.py:312
  261.7 25.1 %all-gather = bf16[8,304,171]{1,2,0:T(8,128)(2,1)S(1)} all-gather(bf16[1,304,171]{1,2,0:T(8,128)(2,1)S(1)} %bitcast.365), channel_id=1, replica_groups=mesh['seq'=8,'ch'=16] {'seq'}, dimensions={0}, use_global_device_ids=true | all-gather | bytes 935712 | tf_op jit(solution)/shard_map/all_gather | solution.py:321
  295.7 3.3 convert_bitcast_fusion.1
  299.0 26.1 %all-gather.6.cloned.1.call-done = bf16[2048,1152]{0,1:T(8,128)(2,1)} async-done(((bf16[256,1152]{0,1:T(8,128)(2,1)}), bf16[2048,1152]{0,1:T(8,128)(2,1)}) %all-gather.6.cloned.1.call-update) | async-done | bytes 4718608 | tf_op jit(solution)/shard_map/all_gather | solution.py:321
  325.1 6.5 %convert_bitcast_fusion = (f32[384,2048]{1,0:T(8,128)}, f32[2048,384]{0,1:T(8,128)}, f32[2048,384]{0,1:T(8,128)}) fusion(bf16[2048,1152]{0,1:T(8,128)(2,1)} %all-gather.6.cloned.1.call-done), kind=kLoop, calls=%fused_computation.1 | loop fusion | flops 2359296 | bytes 14155776 | tf_op jit(solution)/shard_map/transpose | solution.py:552
  331.6 3.5 %copy.182 = f32[2048,384]{1,0:T(8,128)} copy(f32[2048,384]{0,1:T(8,128)} %get-tuple-element.198) | data formatting | bytes 6291456
  335.1 3.7 %copy.183 = f32[2048,384]{1,0:T(8,128)} copy(f32[2048,384]{0,1:T(8,128)} %get-tuple-element.197) | data formatting | bytes 6291456
  (195 shorter events, 63.4 us)
Async XLA Ops:
  7.2 76.7 %copy-start = (bf16[384,2048]{1,0:T(8,128)(2,1)S(1)}, bf16[384,2048]{1,0:T(8,128)(2,1)}, u32[]{:S(2)}) copy-start(bf16[384,2048]{1,0:T(8,128)(2,1)} %param.37) | copy-start | bytes 4718596
  8.9 7.7 %copy-start.2 = (bf16[1,171,171]{2,1,0:T(8,128)(2,1)S(1)}, bf16[1,171,171]{2,1,0:T(8,128)(2,1)}, u32[]{:S(2)}) copy-start(bf16[1,171,171]{2,1,0:T(8,128)(2,1)} %gate_a_ref.3) | copy-start | bytes 175450
  8.9 7.7 %copy-start.3 = (bf16[1,171,171]{2,1,0:T(8,128)(2,1)S(1)}, bf16[1,171,171]{2,1,0:T(8,128)(2,1)}, u32[]{:S(2)}) copy-start(bf16[1,171,171]{2,1,0:T(8,128)(2,1)} %gate_x_ref.3) | copy-start | bytes 175450
  9.3 19.5 %copy-start.40 = (f32[2,128]{1,0:T(2,128)}, f32[2,128]{1,0:T(2,128)S(1)}, u32[]{:S(2)}) copy-start(f32[2,128]{1,0:T(2,128)S(1)} %get-tuple-element.220) | copy-start | bytes 3076
  10.9 5.7 %collective-permute-start = (bf16[2,3,171]{2,1,0:T(4,128)(2,1)S(1)}, bf16[2,3,171]{2,1,0:T(4,128)(2,1)S(1)}, u32[]{:S(2)}, u32[]{:S(2)}) collective-permute-start(bf16[2,3,171]{2,1,0:T(4,128)(2,1)S(1)} %slice.248), channel_id=1, source_target_pairs={{0,16},{16,32},{32,48},{48,64},{64,80},{80,96},{96,112},{1,17},{17... | collective-permute-start | bytes 6164 | tf_op jit(solution)/shard_map/ppermute | solution.py:277
  20.8 10.8 %all-to-all-start = ((f32[8,2,2,171]{3,2,1,0:T(2,128)}), f32[8,2,2,171]{3,2,1,0:T(2,128)S(1)}, u32[]{:S(2)}, u32[]{:S(2)}) async-start(f32[8,2,2,171]{3,2,1,0:T(2,128)} %broadcast_in_dim.33), calls=%async_computation | async-start | bytes 65536 | tf_op jit(solution)/shard_map/all_to_all | solution.py:282
  35.9 26.1 %copy-start.38 = (f32[2048]{0:T(1024)S(1)}, f32[2048]{0:T(1024)}, u32[]{:S(2)}) copy-start(f32[2048]{0:T(1024)} %param.24) | copy-start | bytes 24580
  35.9 22.9 %all-to-all-start.1 = ((bf16[16,16,2048]{2,1,0:T(8,128)(2,1)}), bf16[16,16,2048]{2,1,0:T(8,128)(2,1)}, u32[]{:S(2)}, u32[]{:S(2)}) async-start(bf16[16,16,2048]{2,1,0:T(8,128)(2,1)} %bitcast.358), calls=%async_computation.1 | async-start | bytes 2097152 | tf_op jit(solution)/shard_map/all_to_all | solution.py:303
  60.2 22.1 %copy-start.17 = (bf16[2048,384]{1,0:T(8,128)(2,1)S(1)}, bf16[2048,384]{1,0:T(8,128)(2,1)}, u32[]{:S(2)}) copy-start(bf16[2048,384]{1,0:T(8,128)(2,1)} %param.35) | copy-start | bytes 4718596
  62.0 51.6 %copy-start.39 = (f32[16]{0:T(128)}, f32[16]{0:T(128)S(1)}, u32[]{:S(2)}) copy-start(f32[16]{0:T(128)S(1)} %get-tuple-element.230) | copy-start | bytes 196
  62.3 20.8 %copy-start.18 = (bf16[2048,384]{1,0:T(8,128)(2,1)S(1)}, bf16[2048,384]{1,0:T(8,128)(2,1)}, u32[]{:S(2)}) copy-start(bf16[2048,384]{1,0:T(8,128)(2,1)} %param.36) | copy-start | bytes 4718596
  88.4 19.2 %all-to-all-start.5 = ((bf16[16,16,2048]{2,1,0:T(8,128)(2,1)}), bf16[16,16,2048]{2,1,0:T(8,128)(2,1)}, u32[]{:S(2)}, u32[]{:S(2)}) async-start(bf16[16,16,2048]{2,1,0:T(8,128)(2,1)} %bitcast.355), calls=%async_computation.5 | async-start | bytes 2097152 | tf_op jit(solution)/shard_map/all_to_all | solution.py:303
  95.3 18.3 %copy-start.24 = (f32[16,2048]{1,0:T(8,128)S(1)}, f32[16,2048]{1,0:T(8,128)}, u32[]{:S(2)}) copy-start(f32[16,2048]{1,0:T(8,128)} %copy-done.23) | copy-start | bytes 393220
  107.6 19.4 %all-to-all-start.3 = ((bf16[16,16,2048]{2,1,0:T(8,128)(2,1)}), bf16[16,16,2048]{2,1,0:T(8,128)(2,1)S(1)}, u32[]{:S(2)}, u32[]{:S(2)}) async-start(bf16[16,16,2048]{2,1,0:T(8,128)(2,1)} %bitcast.359), calls=%async_computation.3 | async-start | bytes 2097152 | tf_op jit(solution)/shard_map/all_to_all | solution.py:303
  112.2 99.3 %reduce-scatter.6.cloned.1.call-start = ((), (), s32[]{:S(2)}) async-start(), calls=%async_computation.14 | async-start | bytes 1585152 | tf_op jit(solution)/shard_map/reduce_scatter | solution.py:317
  127.1 18.8 %copy-start.28 = (bf16[2,128,171]{2,1,0:T(8,128)(2,1)S(1)}, bf16[2,128,171]{2,1,0:T(8,128)(2,1)}, u32[]{:S(2)}) copy-start(bf16[2,128,171]{2,1,0:T(8,128)(2,1)} %copy-done.27) | copy-start | bytes 262660
  128.3 18.1 %copy-start.21 = (bf16[171,2048]{1,0:T(8,128)(2,1)S(1)}, bf16[171,2048]{1,0:T(8,128)(2,1)}, u32[]{:S(2)}) copy-start(bf16[171,2048]{1,0:T(8,128)(2,1)} %param.34) | copy-start | bytes 2101252
  149.6 70.0 %reduce-scatter.8.cloned.1.call-start = ((), (), s32[]{:S(2)}) async-start(), calls=%async_computation.16 | async-start | bytes 5308416 | tf_op jit(solution)/shard_map/reduce_scatter | solution.py:317
  158.3 12.2 %all-to-all-start.7 = ((f32[8,2,2,171]{3,2,1,0:T(2,128)}), f32[8,2,2,171]{3,2,1,0:T(2,128)S(1)}, u32[]{:S(2)}, u32[]{:S(2)}) async-start(f32[8,2,2,171]{3,2,1,0:T(2,128)} %broadcast_in_dim.37), calls=%async_computation.7 | async-start | bytes 65536 | tf_op jit(solution)/shard_map/all_to_all | solution.py:282
  172.6 8.2 %copy-start.16 = (bf16[2,128,2048]{2,1,0:T(8,128)(2,1)S(1)}, bf16[2,128,2048]{2,1,0:T(8,128)(2,1)}, u32[]{:S(2)}) copy-start(bf16[2,128,2048]{2,1,0:T(8,128)(2,1)} %param.19) | copy-start | bytes 3145732
  172.6 8.2 %copy-start.34 = (bf16[2048,171]{0,1:T(8,128)(2,1)S(1)}, bf16[2048,171]{0,1:T(8,128)(2,1)}, u32[]{:S(2)}) copy-start(bf16[2048,171]{0,1:T(8,128)(2,1)} %param.25) | copy-start | bytes 2101252
  172.6 6.5 %collective-permute-start.1 = (f32[2,3,171]{2,1,0:T(4,128)S(1)}, f32[2,3,171]{2,1,0:T(4,128)S(1)}, u32[]{:S(2)}, u32[]{:S(2)}) collective-permute-start(f32[2,3,171]{2,1,0:T(4,128)S(1)} %get-tuple-element.44), channel_id=1, source_target_pairs={{16,0},{32,16},{48,32},{64,48},{80,64},{96,80},{112,96},{17,1},{33... | collective-permute-start | bytes 12320 | tf_op jit(solution)/shard_map/ppermute | solution.py:277
  175.7 9.8 %all-to-all-start.10 = ((f32[16,1,128]{2,1,0:T(1,128)}), f32[16,1,128]{2,1,0:T(1,128)S(1)}, u32[]{:S(2)}, u32[]{:S(2)}) async-start(f32[16,1,128]{2,1,0:T(1,128)} %bitcast.69), calls=%async_computation.10 | async-start | bytes 16384 | tf_op jit(solution)/shard_map/all_to_all | solution.py:509
  182.6 7.7 %copy-start.37 = (f32[2048]{0:T(1024)S(1)}, f32[2048]{0:T(1024)}, u32[]{:S(2)}) copy-start(f32[2048]{0:T(1024)} %param.23) | copy-start | bytes 24580
  182.6 7.7 %copy-start.42 = (f32[2,128]{1,0:T(2,128)S(1)}, f32[2,128]{1,0:T(2,128)}, u32[]{:S(2)}) copy-start(f32[2,128]{1,0:T(2,128)} %copy-done.40) | copy-start | bytes 3076
  185.4 21.8 %all-to-all-start.8 = ((bf16[16,16,2176]{2,1,0:T(8,128)(2,1)}), bf16[16,16,2176]{2,1,0:T(8,128)(2,1)}, u32[]{:S(2)}, u32[]{:S(2)}) async-start(bf16[16,16,2176]{2,1,0:T(8,128)(2,1)} %fusion.5), calls=%async_computation.8 | async-start | bytes 2228224 | tf_op jit(solution)/shard_map/all_to_all | solution.py:303
  189.8 70.9 %reduce-scatter.10.cloned.1.call-start = ((), (), s32[]{:S(2)}) async-start(), calls=%async_computation.18 | async-start | bytes 1400832
  211.4 84.3 %all-gather.4.cloned.1.call-start = ((), (), s32[]{:S(2)}) async-start(), calls=%async_computation.15 | async-start | bytes 1585152 | tf_op jit(solution)/shard_map/all_gather | solution.py:321
  212.0 113.1 %all-gather.6.cloned.1.call-start = ((), (), s32[]{:S(2)}) async-start(), calls=%async_computation.17 | async-start | bytes 5308416 | tf_op jit(solution)/shard_map/all_gather | solution.py:321
  220.7 20.2 %all-to-all-start.4 = ((bf16[16,16,2048]{2,1,0:T(8,128)(2,1)}), bf16[16,16,2048]{2,1,0:T(8,128)(2,1)S(1)}, u32[]{:S(2)}, u32[]{:S(2)}) async-start(bf16[16,16,2048]{2,1,0:T(8,128)(2,1)} %broadcast_in_dim.35), calls=%async_computation.4 | async-start | bytes 2097152 | tf_op jit(solution)/shard_map/all_to_all | solution.py:312
  240.9 19.8 %copy-start.19 = (bf16[16,16,2048]{2,1,0:T(8,128)(2,1)}, bf16[16,16,2048]{2,1,0:T(8,128)(2,1)S(1)}, u32[]{:S(2)}) copy-start(bf16[16,16,2048]{2,1,0:T(8,128)(2,1)S(1)} %all-to-all-done.4) | copy-start | bytes 3145732
  242.1 17.0 %all-to-all-start.9 = ((bf16[16,16,2048]{2,1,0:T(8,128)(2,1)}), bf16[16,16,2048]{2,1,0:T(8,128)(2,1)S(1)}, u32[]{:S(2)}, u32[]{:S(2)}) async-start(bf16[16,16,2048]{2,1,0:T(8,128)(2,1)} %broadcast_in_dim.39), calls=%async_computation.9 | async-start | bytes 2097152 | tf_op jit(solution)/shard_map/all_to_all | solution.py:312
  (28 other events, 91.6 us)
Sparse Core Ops, SparseCore 0:
  149.7 28.7 reduce-scatter.5
  180.9 38.6 reduce-scatter.7
  222.5 31.4 reduce-scatter.9
  255.6 28.6 all-gather.3
  285.8 39.2 all-gather.5

commit v2 on v1

--- a/solution.py
+++ b/solution.py
@@ -1,4 +1,4 @@
-from functools import partial
+import math
 
 import jax
 import jax.numpy as jnp
@@ -11,6 +11,13 @@
 F32 = jnp.float32
 BF16 = jnp.bfloat16
 TAPS = 4
+VMEM_LIMIT = 16 * 1024 * 1024
+LANES = 256
+GATE_ROWS = 24
+SMALL_ROWS = 64
+WIDE = 512
+GAIN_ROWS = 16
+HBM_PER_US = 3_600_000
 HALO = 8
 
 
@@ -162,6 +169,7 @@
 
 
 def gates_back_kernel(
+    midway,
     start_ref,
     short_ref,
     long_ref,
@@ -183,15 +191,14 @@
     lam_slope_ref,
     d_conv_head_ref,
     d_input_ref,
-    g_gate_a_ref,
-    g_gate_x_ref,
-    g_rows_ref,
+    small_ref,
     ext,
     prior,
     d_ext,
 ):
     groups, rows, chans = adj_ref.shape
     sums = [jnp.zeros((1, chans), F32) for _ in range(8)]
+    grad_a = grad_x = jnp.zeros((chans, chans), F32)
     for g in range(groups):
         length_ref = (short_ref, long_ref)[g]
         count = length_ref.shape[0]
@@ -218,14 +225,8 @@
         low = conv_out.astype(BF16)
         low_a = d_rate_pre.astype(BF16)
         low_x = d_inlet_pre.astype(BF16)
-        grad_a = dot(low, low_a, ((0,), (0,)))
-        grad_x = dot(low, low_x, ((0,), (0,)))
-        if g == 0:
-            g_gate_a_ref[...] = grad_a
-            g_gate_x_ref[...] = grad_x
-        else:
-            g_gate_a_ref[...] += grad_a
-            g_gate_x_ref[...] += grad_x
+        grad_a = grad_a + dot(low, low_a, ((0,), (0,)))
+        grad_x = grad_x + dot(low, low_x, ((0,), (0,)))
         d_conv = (
             adjoint * root * inlet
             + dot(low_a, gate_a_ref[0], ((1,), (1,)))
@@ -246,28 +247,70 @@
             d_input = d_input + conv_w_ref[k : k + 1, :] * d_ext[k : k + rows, :]
         d_input_ref[g] = d_input
         d_conv_head_ref[g] = d_conv[: TAPS - 1, :]
+        if g == 0:
+            midway()
     sums[2] = sums[2] * lam_slope_ref[...]
+    small_ref[...] = jnp.zeros(small_ref.shape, F32)
     for i, total in enumerate(sums):
-        g_rows_ref[i : i + 1, :] = total
+        lanes = slice(LANES * i, LANES * i + chans)
+        first, last = GATE_ROWS * i, min(GATE_ROWS * (i + 1), chans)
+        small_ref[: last - first, lanes] = grad_a[first:last]
+        small_ref[GATE_ROWS : GATE_ROWS + last - first, lanes] = grad_x[first:last]
+        small_ref[2 * GATE_ROWS : 2 * GATE_ROWS + 1, lanes] = total
 
 
 def sds(shape, dtype=F32):
     return jax.ShapeDtypeStruct(shape, dtype)
 
 
-def run_kernel(kernel, name, outs, ins, scratch=(), flops=0, smem=0):
+def in_hbm(array):
+    return pltpu.with_memory_space_constraint(array, pltpu.HBM)
+
+
+def run_kernel(kernel, name, outs, ins, scratch=(), flops=0, smem=0, after=(), passed=None, waits=0):
     vmem = pl.BlockSpec(memory_space=pltpu.VMEM)
     scalar = pl.BlockSpec(memory_space=pltpu.SMEM)
+    anywhere = pl.BlockSpec(memory_space=pl.ANY)
     moved = sum(a.size * a.dtype.itemsize for a in list(ins) + list(outs))
+    count, skip = len(ins), len(after)
+    ins = [*ins, *[in_hbm(a) for a in after]]
+    in_specs = [scalar] * smem + [vmem] * (count - smem) + [anywhere] * skip
+    out_specs = [vmem] * len(outs)
+    outs, scratch = list(outs), list(scratch)
+    if passed is not None:
+        ins.append(in_hbm(passed))
+        in_specs.append(anywhere)
+        outs.append(pltpu.HBM(passed.shape, passed.dtype))
+        out_specs.append(anywhere)
+        scratch += [pltpu.VMEM(passed.shape, passed.dtype), pltpu.SemaphoreType.DMA((2,))]
+
+    def run(*refs):
+        if passed is None:
+            kernel(*refs[:count], *refs[count + skip :])
+            return
+        in_ref, out_ref = refs[count + skip], refs[count + skip + len(outs)]
+        held, sems = refs[-2:]
+        fetch = pltpu.make_async_copy(in_ref, held, sems.at[0])
+        store = pltpu.make_async_copy(held, out_ref, sems.at[1])
+        fetch.start()
+
+        def midway():
+            fetch.wait()
+            store.start()
+
+        kept = refs[count + skip + 1 : count + skip + len(outs)]
+        kernel(midway, *refs[:count], *kept, *refs[count + skip + len(outs) + 1 : -2])
+        store.wait()
+
     return pl.pallas_call(
-        kernel,
+        run,
         name=name,
         out_shape=outs,
-        in_specs=[scalar] * smem + [vmem] * (len(ins) - smem),
-        out_specs=[vmem] * len(outs),
-        scratch_shapes=list(scratch),
-        cost_estimate=pl.CostEstimate(flops=flops, bytes_accessed=moved, transcendentals=0),
-        compiler_params=pltpu.CompilerParams(vmem_limit_bytes=32 * 1024 * 1024),
+        in_specs=in_specs,
+        out_specs=out_specs,
+        scratch_shapes=scratch,
+        cost_estimate=pl.CostEstimate(flops=flops, bytes_accessed=moved + waits * HBM_PER_US, transcendentals=0),
+        compiler_params=pltpu.CompilerParams(vmem_limit_bytes=VMEM_LIMIT),
     )(*ins)
 
 
@@ -277,58 +320,278 @@
     return lax.ppermute(block, axis, route)
 
 
-def gather_small(value, axis):
-    count = lax.axis_size(axis)
-    return lax.all_to_all(jnp.broadcast_to(value[None], (count,) + value.shape), axis, 0, 0)
-
-
-def carried_in(value, axis, backward):
-    count, mine = lax.axis_size(axis), lax.axis_index(axis)
-    pieces = gather_small(value, axis)
+def carried_in(value, backward):
+    count, mine = lax.axis_size("seq"), lax.axis_index("seq")
+    pieces = lax.all_to_all(jnp.broadcast_to(value[None], (count,) + value.shape), "seq", 0, 0)
     total = jnp.zeros(value.shape[1:], F32)
-    order = range(count - 1, 0, -1) if backward else range(count - 1)
-    for j in order:
+    for j in range(count - 1, 0, -1) if backward else range(count - 1):
         longer = pieces[j, 1] + pieces[j, 0] * total
         total = jnp.where((j > mine) if backward else (j < mine), longer, total)
     return total
 
 
-def scatter_rows(partial_sum, extra=None):
+def sum_parts(got_ref):
+    total = got_ref[0].astype(F32)
+    for j in range(1, got_ref.shape[0]):
+        total = total + got_ref[j].astype(F32)
+    return total
+
+
+def send_to_all(out_ref, share):
+    share = share.astype(BF16)
+    for j in range(out_ref.shape[0]):
+        out_ref[j] = share
+
+
+def norm_back(features, gain, grad):
+    scale = rms(features)
+    gained = gain * grad
+    mean = jnp.mean(gained * features, axis=-1, keepdims=True)
+    back = scale * gained - features * (scale * scale * scale) * mean
+    return back, jnp.sum(grad * (features * scale), axis=0, keepdims=True)
+
+
+def mid_kernel(got_ref, tokens_ref, gain_ref, resid_ref, normed_ref):
+    resid = tokens_ref[...].astype(F32) + sum_parts(got_ref)
+    resid_ref[...] = resid
+    send_to_all(normed_ref, resid * rms(resid) * gain_ref[...])
+
+
+def mid_back_kernel(got_ref, resid_ref, cotangent_ref, gain_ref, d_mid_ref, g_gain_ref, d_mix_ref):
+    back, g_gain = norm_back(resid_ref[...], gain_ref[...], sum_parts(got_ref))
+    d_mid = cotangent_ref[...].astype(F32) + back
+    d_mid_ref[...] = d_mid
+    g_gain_ref[...] = g_gain
+    send_to_all(d_mix_ref, d_mid)
+
+
+def tokens_back_kernel(got_ref, tokens_ref, resid_ref, d_mid_ref, gain_ref, *refs):
+    *chunk_refs, both_ref, sent_ref = refs
+    width = tokens_ref.shape[1]
+    total = sum_parts(got_ref)
+    rows, lanes = chunk_refs[0].shape
+    chunk = chunk_refs[0][...].astype(F32)
+    for chunk_ref in chunk_refs[1:]:
+        chunk = chunk + chunk_ref[...].astype(F32)
+    gains = total[:GAIN_ROWS, 2 * width :]
+    sent_ref[:rows, :] = chunk.astype(BF16)
+    sent_ref[rows:, : gains.shape[1]] = gains.astype(BF16)
+    sent_ref[rows:, gains.shape[1] :] = jnp.zeros((GAIN_ROWS, lanes - gains.shape[1]), BF16)
+    back, _ = norm_back(tokens_ref[...].astype(F32), gain_ref[...], total[:, :width])
+    d_tokens = (d_mid_ref[...] + back).astype(BF16)
+    layer_out = (resid_ref[...] + total[:, width : 2 * width]).astype(BF16)
+    for j in range(both_ref.shape[0]):
+        both_ref[j, 0] = d_tokens
+        both_ref[j, 1] = layer_out
+
+
+def split_both(both, after):
+    owners, _, share, width = both.shape
+
+    def run(both_ref, after_ref, d_tokens_ref, layer_ref):
+        d_tokens_ref[...] = both_ref[:, 0].astype(F32)
+        layer_ref[...] = both_ref[:, 1]
+
+    part = pl.BlockSpec((owners, share, WIDE), lambda i: (0, 0, i))
+    return pl.pallas_call(
+        run,
+        name="split_both",
+        grid=(width // WIDE,),
+        in_specs=[
+            pl.BlockSpec((owners, 2, share, WIDE), lambda i: (0, 0, 0, i)),
+            pl.BlockSpec(memory_space=pl.ANY),
+        ],
+        out_specs=[part, part],
+        out_shape=[pltpu.HBM((owners, share, width), F32), pltpu.HBM((owners, share, width), BF16)],
+        cost_estimate=pl.CostEstimate(flops=0, bytes_accessed=5 * both.size, transcendentals=0),
+        compiler_params=pltpu.CompilerParams(vmem_limit_bytes=VMEM_LIMIT),
+    )(both, in_hbm(after))
+
+
+def exchange(pieces):
+    return lax.all_to_all(pieces, "ch", 0, 0)
+
+
+def by_owner(partial_sum):
     count = lax.axis_size("ch")
     rows, width = partial_sum.shape
-    pieces = partial_sum.astype(BF16).reshape(count, rows // count, width)
-    if extra is not None:
-        extra = jnp.pad(extra.astype(BF16).reshape(count, 1, -1), ((0, 0), (0, rows // count - 1), (0, 0)))
-        pieces = jnp.concatenate([pieces, extra], axis=-1)
-    got = lax.all_to_all(pieces, "ch", 0, 0)
-    total = jnp.sum(got.astype(F32), axis=0)
-    if extra is not None:
-        return total[:, :width], total[0, width:]
-    return total
-
-
-def gather_rows(share):
-    count = lax.axis_size("ch")
-    got = lax.all_to_all(jnp.broadcast_to(share[None], (count,) + share.shape), "ch", 0, 0)
-    return got.reshape(count * share.shape[0], share.shape[1])
-
-
-def seq_scatter(bundle):
-    return lax.psum_scatter(bundle.astype(BF16), "seq", scatter_dimension=0, tiled=True)
-
-
-def seq_gather(share):
-    return lax.all_gather(share, "seq", axis=0, tiled=True)
+    return partial_sum.astype(BF16).reshape(count, rows // count, width)
+
+
+def with_gains(pieces, gains):
+    count, share, width = pieces[0].shape
+    more = gains.astype(BF16).reshape(-1, count, width // count).swapaxes(0, 1)
+    more = jnp.pad(more, ((0, 0), (0, share - gains.shape[0]), (0, 0)))
+    return jnp.concatenate([*pieces, more], axis=-1)
+
+
+def seq_route(fn):
+    count = lax.axis_size("seq")
+    return [(i, fn(i) % count) for i in range(count)]
+
+
+def swap_core(value):
+    return lax.ppermute(value, "seq", seq_route(lambda i: i ^ 1))
+
+
+def shift_z(value, hops):
+    return lax.ppermute(value, "seq", seq_route(lambda i: i + 2 * hops))
+
+
+def half_of(array, axis, other):
+    core = lax.axis_index("seq") % 2
+    size = array.shape[axis] // 2
+    return lax.dynamic_slice_in_dim(array, ((1 - core) if other else core) * size, size, axis)
+
+
+def reduce_chunk(kept, sent, axis):
+    z = lax.axis_index("seq") // 2
+    got = swap_core(sent.astype(BF16))
+    size = kept.shape[axis] // 4
+
+    def piece(hops):
+        at = ((z + hops) % 4) * size
+        cut = lambda a: lax.dynamic_slice_in_dim(a, at, size, axis).astype(F32)
+        return (cut(kept) + cut(got)).astype(BF16)
+
+    return [piece(0)] + [shift_z(piece(hops), hops) for hops in (1, 3, 2)]
+
+
+def assemble(kernel, name, chunks, outs, specs, after):
+    def out_spec(block, dim):
+        return pl.BlockSpec(
+            block, lambda i: tuple(i % 2 * 4 + i // 2 if d == dim else 0 for d in range(len(block)))
+        )
+
+    def run(chunks_ref, *refs):
+        kernel(chunks_ref[0], *refs[len(after) :])
+
+    return pl.pallas_call(
+        run,
+        name=name,
+        grid=(chunks.shape[0],),
+        in_specs=[pl.BlockSpec((1,) + chunks.shape[1:], lambda i: (i, 0, 0))]
+        + [pl.BlockSpec(memory_space=pl.ANY)] * len(after),
+        out_specs=[out_spec(*spec) for spec in specs],
+        out_shape=outs,
+        cost_estimate=pl.CostEstimate(
+            flops=0, bytes_accessed=2 * chunks.size + sum(4 * math.prod(o.shape) for o in outs), transcendentals=0
+        ),
+        compiler_params=pltpu.CompilerParams(vmem_limit_bytes=VMEM_LIMIT),
+    )(chunks, *[in_hbm(a) for a in after])
+
+
+def place_chunk(piece, y_ref, out_ref, x_ref, gate_a_ref, gate_x_ref, rows_ref, gains_ref):
+    chans = x_ref.shape[0]
+    piece = piece.astype(F32)
+    size = (piece.shape[0] - SMALL_ROWS - GAIN_ROWS) // 3
+    y_ref[...] = piece[:chans]
+    out_ref[...] = piece[size : size + chans]
+    x_ref[...] = piece[2 * size : 2 * size + chans]
+    at = 3 * size
+    gate_a_ref[0] = piece[at : at + GATE_ROWS, :chans]
+    gate_x_ref[0] = piece[at + GATE_ROWS : at + 2 * GATE_ROWS, :chans]
+    rows_ref[0] = piece[at + 2 * GATE_ROWS : at + 2 * GATE_ROWS + 8]
+    gains = piece[at + SMALL_ROWS : at + SMALL_ROWS + 8]
+
+    @pl.when(pl.program_id(0) == 0)
+    def _():
+        gains_ref[...] = gains
+
+    @pl.when(pl.program_id(0) > 0)
+    def _():
+        gains_ref[...] += gains
+
+
+def mlp_kernel(normed_ref, d_hidden_ref, one_hbm, two_hbm, cot_hbm, parts_ref, hidden_ref, grads_hbm, one, two, cot, grads, sems):
+    owners, share, width = parts_ref.shape
+    units = one.shape[1]
+    fetches = [
+        pltpu.make_async_copy(source, held, sems.at[n])
+        for n, (source, held) in enumerate(((one_hbm, one), (two_hbm, two), (cot_hbm, cot)))
+    ]
+    for fetch in fetches:
+        fetch.start()
+    normed = normed_ref[...]
+    fetches[0].wait()
+    value, slope = gelu_parts(dot(normed, one[...], ((1,), (0,))))
+    fetches[1].wait()
+    up = dot(normed, two[...], ((1,), (0,)))
+    d_hidden = d_hidden_ref[...]
+    hidden = (value * up).astype(BF16)
+    d_gate = (d_hidden * up * slope).astype(BF16)
+    d_up = (d_hidden * value).astype(BF16)
+    hidden_ref[...] = hidden
+    for at in range(0, width, WIDE):
+        cols = slice(at, at + WIDE)
+        back = dot(d_gate, one[cols, :], ((1,), (1,))) + dot(d_up, two[cols, :], ((1,), (1,)))
+        parts_ref[:, :, cols] = back.astype(BF16).reshape(owners, share, WIDE)
+    fetches[2].wait()
+    stores = []
+    for n, at in enumerate(range(0, width, WIDE)):
+        cols = slice(at, at + WIDE)
+        part = normed_ref[:, cols]
+        grads[cols, :units] = dot(part, d_gate, ((0,), (0,))).astype(BF16)
+        grads[cols, units : 2 * units] = dot(part, d_up, ((0,), (0,))).astype(BF16)
+        grads[cols, 2 * units :] = dot(cot[:, cols], hidden, ((0,), (0,))).astype(BF16)
+        stores.append(pltpu.make_async_copy(grads.at[cols], grads_hbm.at[cols], sems.at[3 + n]))
+        stores[-1].start()
+    for store in stores:
+        store.wait()
+
+
+def mlp_back(normed, d_hidden, w_one, w_two, cotangent, owners):
+    rows, width = normed.shape
+    units = w_one.shape[1]
+    vmem = pl.BlockSpec(memory_space=pltpu.VMEM)
+    anywhere = pl.BlockSpec(memory_space=pl.ANY)
+    return pl.pallas_call(
+        mlp_kernel,
+        name="mlp",
+        in_specs=[vmem, vmem, anywhere, anywhere, anywhere],
+        out_specs=[vmem, vmem, anywhere],
+        out_shape=[
+            sds((owners, rows // owners, width), BF16),
+            sds((rows, units), BF16),
+            pltpu.HBM((width, 3 * units), BF16),
+        ],
+        scratch_shapes=[
+            pltpu.VMEM((width, units), BF16),
+            pltpu.VMEM((width, units), BF16),
+            pltpu.VMEM((rows, width), BF16),
+            pltpu.VMEM((width, 3 * units), BF16),
+            pltpu.SemaphoreType.DMA((3 + width // WIDE,)),
+        ],
+        cost_estimate=pl.CostEstimate(
+            flops=14 * rows * width * units, bytes_accessed=14 * width * units, transcendentals=0
+        ),
+        compiler_params=pltpu.CompilerParams(vmem_limit_bytes=2 * VMEM_LIMIT),
+    )(normed, d_hidden, in_hbm(w_one), in_hbm(w_two), in_hbm(cotangent))
+
+
+def place_mlp(bundle, units):
+    width = bundle.shape[0]
+
+    def run(piece_ref, one_ref, two_ref, three_ref):
+        one_ref[...] = piece_ref[:, :units].astype(F32)
+        two_ref[...] = piece_ref[:, units : 2 * units].astype(F32)
+        three_ref[...] = piece_ref[:, 2 * units :].astype(F32).T
+
+    block = pl.BlockSpec((LANES, units), lambda i: (i, 0))
+    return pl.pallas_call(
+        run,
+        name="place_mlp",
+        grid=(width // LANES,),
+        in_specs=[pl.BlockSpec((LANES, 3 * units), lambda i: (i, 0))],
+        out_specs=[block, block, pl.BlockSpec((units, LANES), lambda i: (0, i))],
+        out_shape=[sds((width, units)), sds((width, units)), sds((units, width))],
+        cost_estimate=pl.CostEstimate(flops=0, bytes_accessed=18 * width * units, transcendentals=0),
+        compiler_params=pltpu.CompilerParams(vmem_limit_bytes=VMEM_LIMIT),
+    )(in_hbm(bundle))
 
 
 def rms(features):
     return lax.rsqrt(jnp.mean(features * features, axis=-1, keepdims=True) + EPS_NORM)
-
-
-def norm_back(features, scale, gain, grad):
-    gained = gain * grad
-    mean = jnp.mean(gained * features, axis=-1, keepdims=True)
-    return scale * gained - features * (scale * scale * scale) * mean
 
 
 def body(
@@ -367,6 +630,7 @@
     tokens = tokens.reshape(total_rows, width)
     cotangent = cotangent.reshape(total_rows, width)
     tokens_f = tokens.astype(F32)
+    tokens_share = mine(tokens)
     scale_one = rms(tokens_f)
     normed_one = (tokens_f * scale_one * gain_one).astype(BF16)
     conv_input = grouped(dot(normed_one, w_x, ((1,), (0,))).astype(BF16))
@@ -399,38 +663,34 @@
         flops=2 * flops,
         smem=3,
     )
-    state_in = carried_in(carry, "seq", False)
+    state_in = carried_in(carry, False)
     hidden = local_state + decay_run * state_in[:, None]
     mixed_in = (hidden * jax.nn.gelu(gate_pre, approximate=True)).astype(BF16)
     mixed_in = mixed_in.reshape(total_rows, chans)
-    mix_share = scatter_rows(dot(mixed_in, w_out, ((1,), (0,))))
-    resid_share = mine(tokens_f) + mix_share
-    scale_two = rms(resid_share)
-    normed_two = gather_rows((resid_share * scale_two * gain_two).astype(BF16))
-
-    mlp_gate = dot(normed_two, w_one, ((1,), (0,)))
-    mlp_up = dot(normed_two, w_two, ((1,), (0,)))
-    gate_value, gate_slope = gelu_parts(mlp_gate)
-    mlp_hidden = (gate_value * mlp_up).astype(BF16)
+    share = sds((share_rows, width))
+    to_all = sds((ch_count, share_rows, width), BF16)
+    resid_share, normed_two = run_kernel(
+        mid_kernel,
+        "resid_mid_norm",
+        [share, to_all],
+        [exchange(by_owner(dot(mixed_in, w_out, ((1,), (0,))))), tokens_share, gain_two[None]],
+        waits=20,
+    )
+    normed_two = exchange(normed_two).reshape(total_rows, width)
+
     d_hidden = dot(cotangent, w_three, ((1,), (1,)))
-    d_gate = (d_hidden * mlp_up * gate_slope).astype(BF16)
-    d_up = (d_hidden * gate_value).astype(BF16)
-    partial_two = dot(d_gate, w_one, ((1,), (1,))) + dot(d_up, w_two, ((1,), (1,)))
-    gain_two_share = resid_share * scale_two
-    sum_two = scatter_rows(partial_two)
-    gain_two_part = jnp.sum(sum_two * gain_two_share, axis=0)
-    d_mid = mine(cotangent.astype(F32)) + norm_back(resid_share, scale_two, gain_two, sum_two)
-    d_mix = gather_rows(d_mid.astype(BF16))
-
-    g_mlp = jnp.concatenate(
-        [
-            dot(normed_two, d_gate, ((0,), (0,))).astype(BF16),
-            dot(normed_two, d_up, ((0,), (0,))).astype(BF16),
-            dot(cotangent, mlp_hidden, ((0,), (0,))).astype(BF16),
-        ],
-        axis=1,
-    )
-    g_mlp = seq_gather(seq_scatter(g_mlp))
+    two_parts, mlp_hidden, g_mlp = mlp_back(normed_two, d_hidden, w_one, w_two, cotangent, ch_count)
+    partial_out = lax.optimization_barrier(by_owner(dot(mlp_hidden, w_three, ((1,), (0,)))))
+    d_mid, gain_two_part, d_mix = run_kernel(
+        mid_back_kernel,
+        "d_mid",
+        [share, sds((1, width)), to_all],
+        [exchange(two_parts), resid_share, mine(cotangent), gain_two[None]],
+        after=[g_mlp, partial_out],
+        waits=20,
+    )
+    d_mix = exchange(d_mix).reshape(total_rows, width)
+    g_mlp = lax.psum_scatter(g_mlp, "seq", scatter_dimension=0, tiled=True)
 
     d_mixed = grouped(dot(d_mix, w_out, ((1,), (1,))))
     d_gate_pre, reach, local_adjoint, carry_back = run_kernel(
@@ -438,18 +698,13 @@
         "adjoint_scan",
         [sds((groups, rows, chans), BF16), big, big, sds((2, groups, chans))],
         [d_mixed, gate_pre, hidden, keep],
-    )
-    beyond = carried_in(carry_back, "seq", True)
-    d_conv_head, d_input, g_gate_a, g_gate_x, g_rows = run_kernel(
+        waits=20,
+    )
+    beyond = carried_in(carry_back, True)
+    d_conv_head, d_input, small, g_mlp = run_kernel(
         gates_back_kernel,
         "gates_back",
-        [
-            sds((groups, TAPS - 1, chans)),
-            big,
-            sds((chans, chans)),
-            sds((chans, chans)),
-            sds((8, chans)),
-        ],
+        [sds((groups, TAPS - 1, chans)), big, sds((SMALL_ROWS, width))],
         [
             start,
             short_lengths,
@@ -478,7 +733,10 @@
         ],
         flops=4 * flops,
         smem=3,
-    )
+        passed=g_mlp,
+        waits=10,
+    )
+    g_mlp = lax.all_gather(g_mlp, "seq", axis=0, tiled=True)
     lead = shifted(d_conv_head, "seq", -1)
     ahead = start[0] + rows + jnp.arange(TAPS - 1, dtype=jnp.int32)
     lead_masks = []
@@ -500,56 +758,83 @@
     d_gate_pre = d_gate_pre.reshape(total_rows, chans)
 
     partial_one = dot(d_input, w_x, ((1,), (1,))) + dot(d_gate_pre, w_y, ((1,), (1,)))
-    gain_one_part = jnp.sum(partial_one * (tokens_f * scale_one), axis=0)
-    sum_one, g_gain_one = scatter_rows(partial_one, gain_one_part)
-    tokens_share = mine(tokens_f)
-    d_tokens = d_mid + norm_back(tokens_share, mine(scale_one), gain_one, sum_one)
-    d_tokens = grouped(gather_rows(d_tokens.astype(BF16)).astype(F32))
-
-    gain_two_got = lax.all_to_all(gain_two_part.reshape(ch_count, share_width), "ch", 0, 0)
-    g_gain_two = jnp.sum(gain_two_got, axis=0)
-
-    partial_out = dot(mlp_hidden, w_three, ((1,), (0,)))
-    out_share = resid_share + scatter_rows(partial_out)
-    layer_out = grouped(gather_rows(out_share.astype(BF16)))
-
-    g_mid = jnp.concatenate(
+    gain_one_part = jnp.sum(partial_one * (tokens_f * scale_one), axis=0, keepdims=True)
+    gain_parts = jnp.concatenate([gain_one_part, gain_two_part], axis=0)
+    back_pieces = exchange(with_gains([by_owner(partial_one), partial_out], gain_parts))
+
+    padded = lambda a: jnp.pad(a, ((0, 0), (0, -chans % 16)))
+    d_gate_wide, mixed_wide = padded(d_gate_pre + 0.0 * d_input), padded(mixed_in + 0.0 * d_input)
+    d_input_wide = padded(d_input)
+
+    def terms(other):
+        normed_half = half_of(normed_one, 1, other)
+        return jnp.concatenate(
+            [
+                dot(d_gate_wide, normed_half, ((0,), (0,))),
+                dot(mixed_wide, half_of(d_mix, 1, other), ((0,), (0,))),
+                dot(d_input_wide, normed_half, ((0,), (0,))),
+                half_of(small, 1, other),
+            ],
+            axis=0,
+        )
+
+    chunk_parts = reduce_chunk(terms(False), terms(True), 1)
+
+    g_w_one, g_w_two, g_w_three = place_mlp(g_mlp, hidden_units)
+    both, chunk = run_kernel(
+        tokens_back_kernel,
+        "d_tokens",
+        [sds((ch_count, 2, share_rows, width), BF16), sds((chunk_parts[0].shape[0] + GAIN_ROWS, LANES), BF16)],
+        [back_pieces, tokens_share, resid_share, d_mid, gain_one[None], *chunk_parts],
+        after=[g_w_one],
+        waits=30,
+    )
+    g_w_y, g_w_out, g_w_x, g_gate_a, g_gate_x, g_rows, gains = assemble(
+        place_chunk,
+        "place_chunk",
+        lax.all_gather(chunk, "seq"),
         [
-            dot(normed_one, d_gate_pre, ((0,), (0,))).astype(BF16),
-            dot(d_mix, mixed_in, ((0,), (0,))).astype(BF16),
+            sds((chans, width)),
+            sds((chans, width)),
+            sds((chans, width)),
+            sds((1, chans, chans)),
+            sds((1, chans, chans)),
+            sds((8, 8, LANES)),
+            sds((8, LANES)),
         ],
-        axis=1,
-    )
-    g_mid = seq_gather(seq_scatter(g_mid))
-
-    g_w_x = dot(normed_one, d_input, ((0,), (0,)))
-    gains = jnp.pad(jnp.stack([g_gain_one, g_gain_two]), ((0, 0), (0, chans - share_width)))
-    tail = jnp.concatenate([g_w_x, g_gate_a, g_gate_x, g_rows, gains], axis=0).astype(BF16)
-    tail_rows = tail.shape[0]
-    tail = jnp.pad(tail, ((0, -tail_rows % (16 * seq_count)), (0, 0)))
-    tail = seq_gather(seq_scatter(tail)).astype(F32)
-    at = width
-    g_gate_a = tail[at : at + chans][None]
-    g_gate_x = tail[at + chans : at + 2 * chans][None]
-    at = at + 2 * chans
+        [
+            ((chans, LANES), 1),
+            ((chans, LANES), 1),
+            ((chans, LANES), 1),
+            ((1, GATE_ROWS, chans), 1),
+            ((1, GATE_ROWS, chans), 1),
+            ((1, 8, LANES), 0),
+            ((8, LANES), None),
+        ],
+        [],
+    )
+    g_rows = g_rows[:, 0, :chans]
+    d_tokens, layer_out = split_both(exchange(both), g_w_y)
+    d_tokens = d_tokens.reshape(groups, rows, width)
+    layer_out = layer_out.reshape(groups, rows, width)
     return (
         layer_out,
         d_tokens,
-        tail[at + 8, :share_width],
-        tail[at + 9, :share_width],
-        g_mid[:, :chans].astype(F32),
-        tail[:width],
-        tail[at + 4 : at + 8],
-        tail[at + 3],
+        gains[0, :share_width],
+        gains[1, :share_width],
+        g_w_y.T,
+        g_w_x.T,
+        g_rows[4:],
+        g_rows[3],
         g_gate_a,
         g_gate_x,
-        tail[at],
-        tail[at + 1],
-        tail[at + 2],
-        g_mid[:, chans:].astype(F32).T,
-        g_mlp[:, :hidden_units].astype(F32),
-        g_mlp[:, hidden_units : 2 * hidden_units].astype(F32),
-        g_mlp[:, 2 * hidden_units :].astype(F32).T,
+        g_rows[0],
+        g_rows[1],
+        g_rows[2],
+        g_w_out,
+        g_w_one,
+        g_w_two,
+        g_w_three,
     )
 
 

time: 348 us -> 251 us (0.72)
  blocking collectives: 62.9 us -> 19.7 us
  waiting for transfers between devices: 127 us -> 86.7 us
  Pallas kernels: 5.04 us -> 30.8 us
  other arithmetic: 32.6 us -> 11.7 us
  starting transfers between devices: 55.5 us -> 46.7 us
  local copies, waits for them, and re-layouts: 27.2 us -> 22.1 us
  matrix products: 21.5 us -> 16.9 us
    all_to_all x9 -> x7, waiting for transfers between devices: 92 us -> 57.4 us  [the longest x5 49.9 us: exchange(): return lax.all_to_all(pieces, 'ch', 0, 0)]
    pallas_call x3 -> x10, Pallas kernels: 5.04 us -> 30.8 us  [the longest x6 8.53 us: run_kernel(): pl.pallas_call(run, name=name, out_shape=outs, in_specs=in_specs, out_spe...]
    all_gather x1 -> x0, blocking collectives: 25.1 us -> none  [seq_gather(): return lax.all_gather(share, 'seq', axis=0, tiled=True)]
    all_to_all x2 -> x1, blocking collectives: 37.7 us -> 19.7 us  [exchange(): return lax.all_to_all(pieces, 'ch', 0, 0)]
    all_to_all x9 -> x7, starting transfers between devices: 47.4 us -> 36.2 us  [the longest x5 24 us: exchange(): return lax.all_to_all(pieces, 'ch', 0, 0)]
    transpose x2 -> x1, other arithmetic: 9.77 us -> 0.03 us  [with_gains(): more = gains.astype(BF16).reshape(-1, count, width // count).swapaxes(0, 1)]
    reduce_scatter x2 -> x1, waiting for transfers between devices: 7.53 us -> 0.02 us  [body(): g_mlp = lax.psum_scatter(g_mlp, 'seq', scatter_dimension=0, tiled=True)]
    reduce_sum x7 -> x0, other arithmetic: 6.11 us -> none  [the longest x4 4.34 us: scatter_rows(): total = jnp.sum(got.astype(F32), axis=0)]
  transfers between devices with their start and end apart: 16 -> 16, of which waited for: 12 -> 14; matrix products, arithmetic and copies ran while one was open for 13% -> 12% of each run, Pallas kernels for 1% -> 5%
where the time goes in v2:
time: 251 us; the launch traced here: 249 us
  waiting for transfers between devices  86.7 us (35%)
  starting transfers between devices  46.7 us (19%)
  Pallas kernels  30.8 us (12%)
  local copies, waits for them, and re-layouts  22.1 us (9%)
  blocking collectives  19.7 us (8%)
  matrix products  16.9 us (7%)
  between operations  14.8 us (6%)
  other arithmetic  11.7 us (5%)
    all_to_all x5, waiting for transfers between devices, exchange(): return lax.all_to_all(pieces, 'ch', 0, 0)  49.9 us
    all_to_all x5, starting transfers between devices, exchange(): return lax.all_to_all(pieces, 'ch', 0, 0)  24 us
    all_to_all x1, blocking collectives, exchange(): return lax.all_to_all(pieces, 'ch', 0, 0)  19.7 us
    all_gather x1, waiting for transfers between devices, body(): lax.all_gather(chunk, 'seq')  19.4 us
    dot_general x14, matrix products, dot(): lax.dot_general(left, right, (contract, ((), ())), preferred_element_type...  16.9 us
    unnamed x129, local copies, waits for them, and re-layouts  16 us
    all_to_all x2, starting transfers between devices, carried_in(): lax.all_to_all(jnp.broadcast_to(value[None], (count,) + value.shape), 'se...  12.3 us
    pallas_call x6, Pallas kernels, run_kernel(): pl.pallas_call(run, name=name, out_shape=outs, in_specs=in_specs, out_spe...  8.53 us
  transfers between devices with their start and end apart: 16, of which 14 were waited for; matrix products, arithmetic and copies ran while one was open for 12% of the time, Pallas kernels for 5%

profile of v2, /device:TPU:1, one launch (start us, length us, event | category | flops | bytes accessed | tf_op | source)
XLA Modules:
  0.0 249.2 jit_solution(8213920699807331496)
XLA Ops:
  11.3 4.9 %collective-permute-start = (bf16[2,3,171]{2,1,0:T(4,128)(2,1)S(1)}, bf16[2,3,171]{2,1,0:T(4,128)(2,1)S(1)}, u32[]{:S(2)}, u32[]{:S(2)}) collective-permute-start(bf16[2,3,171]{2,1,0:T(4,128)(2,1)S(1)} %slice.221), channel_id=1, source_target_pairs={{0,16},{16,32},{32,48},{48,64},{64,80},{80,96},{96,112},{1,17},{17... | collective-permute-start | bytes 6164 | tf_op jit(solution)/shard_map/ppermute | solution.py:320
  17.1 2.1 conv_gates_scan.1
  22.0 6.1 %all-to-all-start = ((f32[8,2,2,171]{3,2,1,0:T(2,128)}), f32[8,2,2,171]{3,2,1,0:T(2,128)S(1)}, u32[]{:S(2)}, u32[]{:S(2)}) async-start(f32[8,2,2,171]{3,2,1,0:T(2,128)} %broadcast_in_dim.25), calls=%async_computation | async-start | bytes 65536 | tf_op jit(solution)/shard_map/all_to_all | solution.py:325
  28.0 1.9 fusion.5.refs_1_
  30.0 2.8 %all-to-all-done = f32[8,2,2,171]{3,2,1,0:T(2,128)S(1)} async-done(((f32[8,2,2,171]{3,2,1,0:T(2,128)}), f32[8,2,2,171]{3,2,1,0:T(2,128)S(1)}, u32[]{:S(2)}, u32[]{:S(2)}) %all-to-all-start) | async-done | bytes 21920 | tf_op jit(solution)/shard_map/all_to_all | solution.py:325
  33.5 2.6 %convolution_convert_fusion.1 = bf16[256,2048]{1,0:T(8,128)(2,1)} fusion(bf16[256,171]{1,0:T(8,128)(2,1)S(1)} %bitcast.338, bf16[171,2048]{1,0:T(8,128)(2,1)} %param.34), kind=kOutput, calls=%fused_computation.6 | convolution fusion | flops 179830784 | bytes 1836544 | tf_op jit(solution)/shard_map/dot_general | solution.py:25
  36.1 6.8 %all-to-all-start.1 = ((bf16[16,16,2048]{2,1,0:T(8,128)(2,1)}), bf16[16,16,2048]{2,1,0:T(8,128)(2,1)S(1)}, u32[]{:S(2)}, u32[]{:S(2)}) async-start(bf16[16,16,2048]{2,1,0:T(8,128)(2,1)} %bitcast.329), calls=%async_computation.1 | async-start | bytes 2097152 | tf_op jit(solution)/shard_map/all_to_all | solution.py:412
  44.3 14.4 %all-to-all-done.1.refs_0_ = bf16[16,16,2048]{2,1,0:T(8,128)(2,1)S(1)} async-done(((bf16[16,16,2048]{2,1,0:T(8,128)(2,1)}), bf16[16,16,2048]{2,1,0:T(8,128)(2,1)S(1)}, u32[]{:S(2)}, u32[]{:S(2)}) %all-to-all-start.1) | async-done | bytes 1048608 | tf_op jit(solution)/shard_map/all_to_all | solution.py:412
  61.5 4.2 %all-to-all-start.2 = ((bf16[16,16,2048]{2,1,0:T(8,128)(2,1)}), bf16[16,16,2048]{2,1,0:T(8,128)(2,1)S(1)}, u32[]{:S(2)}, u32[]{:S(2)}) async-start(bf16[16,16,2048]{2,1,0:T(8,128)(2,1)} %copy-done.5), calls=%async_computation.2 | async-start | bytes 2097152 | tf_op jit(solution)/shard_map/all_to_all | solution.py:412
  65.8 2.7 %fusion.115.d_hidden_ref = f32[256,384]{1,0:T(8,128)} fusion(bf16[256,2048]{1,0:T(8,128)(2,1)} %bitcast.335, bf16[384,2048]{1,0:T(8,128)(2,1)S(1)} %copy-done), kind=kOutput, calls=%fused_computation.213 | convolution fusion | flops 402653184 | bytes 3014656 | tf_op jit(solution)/shard_map/dot_general | solution.py:25
  68.5 12.2 %all-to-all-done.2 = bf16[16,16,2048]{2,1,0:T(8,128)(2,1)S(1)} async-done(((bf16[16,16,2048]{2,1,0:T(8,128)(2,1)}), bf16[16,16,2048]{2,1,0:T(8,128)(2,1)S(1)}, u32[]{:S(2)}, u32[]{:S(2)}) %all-to-all-start.2) | async-done | bytes 1048608 | tf_op jit(solution)/shard_map/all_to_all | solution.py:412
  81.7 7.1 %mlp.1 = (bf16[16,16,2048]{2,1,0:T(8,128)(2,1)S(1)}, bf16[256,384]{1,0:T(8,128)(2,1)S(1)}, bf16[2048,1152]{1,0:T(8,128)(2,1)}) custom-call(bf16[256,2048]{1,0:T(8,128)(2,1)S(1)} %bitcast.310, f32[256,384]{1,0:T(8,128)S(1)} %copy-done.11, bf16[2048,384]{1,0:T(8,128)(2,1)} %one_hbm.1, bf16[2048,384]{1,0:T(8,128)(2,1)} %two_hbm.1, bf16[256,2048]{1,0:T(8,128)(2,1)} %bitcast.336), custom_call_target="tpu_custom_call" | custom-call | flops 2818572288 | bytes 11010048 | tf_op jit(solution)/shard_map/mlp/pallas_call | solution.py:548
  90.5 4.7 %all-to-all-start.3 = ((bf16[16,16,2048]{2,1,0:T(8,128)(2,1)}), bf16[16,16,2048]{2,1,0:T(8,128)(2,1)S(1)}, u32[]{:S(2)}, u32[]{:S(2)}) async-start(bf16[16,16,2048]{2,1,0:T(8,128)(2,1)} %copy-done.4), calls=%async_computation.3 | async-start | bytes 2097152 | tf_op jit(solution)/shard_map/all_to_all | solution.py:412
  96.7 2.6 %convolution_convert_fusion = bf16[256,2048]{1,0:T(8,128)(2,1)} fusion(bf16[256,384]{1,0:T(8,128)(2,1)} %copy-done.25, bf16[384,2048]{1,0:T(8,128)(2,1)S(1)} %copy-done), kind=kOutput, calls=%fused_computation.5 | convolution fusion | flops 403177472 | bytes 2818048 | tf_op jit(solution)/shard_map/dot_general | solution.py:25
  99.3 10.9 %all-to-all-done.3.refs_0_ = bf16[16,16,2048]{2,1,0:T(8,128)(2,1)S(1)} async-done(((bf16[16,16,2048]{2,1,0:T(8,128)(2,1)}), bf16[16,16,2048]{2,1,0:T(8,128)(2,1)S(1)}, u32[]{:S(2)}, u32[]{:S(2)}) %all-to-all-start.3) | async-done | bytes 1048608 | tf_op jit(solution)/shard_map/all_to_all | solution.py:412
  112.3 19.7 %all_to_all.40 = bf16[16,16,2048]{2,1,0:T(8,128)(2,1)S(1)} all-to-all(bf16[16,16,2048]{2,1,0:T(8,128)(2,1)S(1)} %get-tuple-element.62), channel_id=1, replica_groups=mesh['seq'=8,'ch'=16] {'ch'}, dimensions={0} | all-to-all | bytes 2097152 | tf_op jit(solution)/shard_map/all_to_all | solution.py:412
  134.3 6.2 %all-to-all-start.5 = ((f32[8,2,2,171]{3,2,1,0:T(2,128)}), f32[8,2,2,171]{3,2,1,0:T(2,128)S(1)}, u32[]{:S(2)}, u32[]{:S(2)}) async-start(f32[8,2,2,171]{3,2,1,0:T(2,128)} %broadcast_in_dim.27), calls=%async_computation.5 | async-start | bytes 65536 | tf_op jit(solution)/shard_map/all_to_all | solution.py:325
  140.5 4.7 %all-to-all-done.5 = f32[8,2,2,171]{3,2,1,0:T(2,128)S(1)} async-done(((f32[8,2,2,171]{3,2,1,0:T(2,128)}), f32[8,2,2,171]{3,2,1,0:T(2,128)S(1)}, u32[]{:S(2)}, u32[]{:S(2)}) %all-to-all-start.5) | async-done | bytes 21920 | tf_op jit(solution)/shard_map/all_to_all | solution.py:325
  145.4 2.8 %gates_back.1 = (f32[2,3,171]{2,1,0:T(4,128)S(1)}, f32[2,128,171]{2,1,0:T(8,128)S(1)}, f32[64,2048]{1,0:T(8,128)S(1)}, bf16[256,1152]{1,0:T(8,128)(2,1)}) custom-call(s32[1]{0:T(128)} %bitcast.refs_0_, s32[8]{0:T(128)S(1)} %copy-done.44, s32[3]{0:T(128)S(1)} %copy-done.42, f32[2,128,171]{2,1,0:T(8,128)S(1)} %get-tuple-element.64.refs_3_, ...), custom_call_target="tpu_custom_call" | custom-call | flops 59885568 | bytes 38142680 | tf_op jit(solution)/shard_map/gates_back/pallas_call | solution.py:305
  149.4 2.6 %collective-permute-start.1 = (f32[2,3,171]{2,1,0:T(4,128)S(1)}, f32[2,3,171]{2,1,0:T(4,128)S(1)}, u32[]{:S(2)}, u32[]{:S(2)}) collective-permute-start(f32[2,3,171]{2,1,0:T(4,128)S(1)} %get-tuple-element.71), channel_id=1, source_target_pairs={{16,0},{32,16},{48,32},{64,48},{80,64},{96,80},{112,96},{17,1},{33... | collective-permute-start | bytes 12320 | tf_op jit(solution)/shard_map/ppermute | solution.py:320
  158.9 3.9 %all-to-all-start.6 = ((bf16[16,16,4224]{2,1,0:T(8,128)(2,1)}), bf16[16,16,4224]{2,1,0:T(8,128)(2,1)S(1)}, u32[]{:S(2)}, u32[]{:S(2)}) async-start(bf16[16,16,4224]{2,1,0:T(8,128)(2,1)} %fusion.1), calls=%async_computation.7 | async-start | bytes 4325376 | tf_op jit(solution)/shard_map/all_to_all | solution.py:412
  170.2 2.5 %add_convert_fusion = (bf16[592,256]{1,0:T(8,128)(2,1)}, bf16[592,256]{1,0:T(8,128)(2,1)}, bf16[592,256]{1,0:T(8,128)(2,1)}, bf16[592,256]{1,0:T(8,128)(2,1)S(1)}) fusion(f32[592,1024]{1,0:T(8,128)S(1)} %pad_maximum_fusion, s32[]{:T(128)S(6)} %select_n.230, bf16[592,1024]{1,0:T(8,128)(2,1)} %collective-permute-done.2, s32[]{:T(128)S(6)} %select_n.228, ...), kind=kLoop, calls=%fused_computation.26 | loop fusion | flops 1818624 | bytes 4849680 | tf_op jit(solution)/shard_map/convert_element_type | solution.py:455
  175.5 3.7 %all-gather.4.cloned.1.call-done.piece_ref = bf16[2048,1152]{1,0:T(8,128)(2,1)} async-done(((bf16[256,1152]{1,0:T(8,128)(2,1)}), bf16[2048,1152]{1,0:T(8,128)(2,1)}) %all-gather.4.cloned.1.call-update) | async-done | bytes 4718608 | tf_op jit(solution)/shard_map/all_gather | solution.py:739
  179.2 7.7 %place_mlp.1 = (f32[2048,384]{1,0:T(8,128)}, f32[2048,384]{1,0:T(8,128)}, f32[384,2048]{1,0:T(8,128)}) custom-call(bf16[2048,1152]{1,0:T(8,128)(2,1)} %all-gather.4.cloned.1.call-done.piece_ref), custom_call_target="tpu_custom_call" | custom-call | bytes 14155776 | tf_op jit(solution)/shard_map/place_mlp/pallas_call | solution.py:581
  186.9 2.0 collective-permute-done.4.refs_7_
  190.2 6.6 %all-to-all-done.6.refs_0_ = bf16[16,16,4224]{2,1,0:T(8,128)(2,1)S(1)} async-done(((bf16[16,16,4224]{2,1,0:T(8,128)(2,1)}), bf16[16,16,4224]{2,1,0:T(8,128)(2,1)S(1)}, u32[]{:S(2)}, u32[]{:S(2)}) %all-to-all-start.6) | async-done | bytes 2162720 | tf_op jit(solution)/shard_map/all_to_all | solution.py:412
  196.9 2.3 d_tokens.1
  200.5 4.4 %all-to-all-start.7 = ((bf16[16,2,16,2048]{3,2,1,0:T(8,128)(2,1)}), bf16[16,2,16,2048]{3,2,1,0:T(8,128)(2,1)}, u32[]{:S(2)}, u32[]{:S(2)}) async-start(bf16[16,2,16,2048]{3,2,1,0:T(8,128)(2,1)} %copy-done.3), calls=%async_computation.8 | async-start | bytes 4194304 | tf_op jit(solution)/shard_map/all_to_all | solution.py:412
  204.9 19.4 %all-gather.6.cloned.1.call-done = bf16[4864,256]{1,0:T(8,128)(2,1)} async-done(((bf16[608,256]{1,0:T(8,128)(2,1)}), bf16[4864,256]{1,0:T(8,128)(2,1)}) %all-gather.6.cloned.1.call-update) | async-done | bytes 2490384 | tf_op jit(solution)/shard_map/all_gather | solution.py:795
  226.0 3.5 %place_chunk.1 = (f32[171,2048]{1,0:T(8,128)}, f32[171,2048]{1,0:T(8,128)}, f32[171,2048]{1,0:T(8,128)}, f32[1,171,171]{2,1,0:T(8,128)S(1)}, f32[1,171,171]{2,1,...) custom-call(bf16[8,608,256]{2,1,0:T(8,128)(2,1)S(1)} %bitcast.306), custom_call_target="tpu_custom_call" | custom-call | bytes 7000520 | tf_op jit(solution)/shard_map/place_chunk/pallas_call | solution.py:469
  232.9 5.7 %all-to-all-done.7.both_ref = bf16[16,2,16,2048]{3,2,1,0:T(8,128)(2,1)} async-done(((bf16[16,2,16,2048]{3,2,1,0:T(8,128)(2,1)}), bf16[16,2,16,2048]{3,2,1,0:T(8,128)(2,1)}, u32[]{:S(2)}, u32[]{:S(2)}) %all-to-all-start.7) | async-done | bytes 2097184 | tf_op jit(solution)/shard_map/all_to_all | solution.py:412
  238.7 4.0 %split_both.1 = (f32[16,16,2048]{2,1,0:T(8,128)}, bf16[16,16,2048]{2,1,0:T(8,128)(2,1)}) custom-call(bf16[16,2,16,2048]{3,2,1,0:T(8,128)(2,1)} %all-to-all-done.7.both_ref, f32[171,2048]{1,0:T(8,128)} %get-tuple-element.80.after_ref), custom_call_target="tpu_custom_call" | custom-call | bytes 5242880 | tf_op jit(solution)/shard_map/split_both/pallas_call | solution.py:396
  (197 shorter events, 46.8 us)
Async XLA Ops:
  7.2 58.6 %copy-start = (bf16[384,2048]{1,0:T(8,128)(2,1)S(1)}, bf16[384,2048]{1,0:T(8,128)(2,1)}, u32[]{:S(2)}) copy-start(bf16[384,2048]{1,0:T(8,128)(2,1)} %param.37) | copy-start | bytes 4718596
  9.0 19.0 %copy-start.29 = (f32[2048]{0:T(1024)S(1)}, f32[2048]{0:T(1024)}, u32[]{:S(2)}) copy-start(f32[2048]{0:T(1024)} %param.23) | copy-start | bytes 24580
  11.3 5.7 %collective-permute-start = (bf16[2,3,171]{2,1,0:T(4,128)(2,1)S(1)}, bf16[2,3,171]{2,1,0:T(4,128)(2,1)S(1)}, u32[]{:S(2)}, u32[]{:S(2)}) collective-permute-start(bf16[2,3,171]{2,1,0:T(4,128)(2,1)S(1)} %slice.221), channel_id=1, source_target_pairs={{0,16},{16,32},{32,48},{48,64},{64,80},{80,96},{96,112},{1,17},{17... | collective-permute-start | bytes 6164 | tf_op jit(solution)/shard_map/ppermute | solution.py:320
  22.0 10.8 %all-to-all-start = ((f32[8,2,2,171]{3,2,1,0:T(2,128)}), f32[8,2,2,171]{3,2,1,0:T(2,128)S(1)}, u32[]{:S(2)}, u32[]{:S(2)}) async-start(f32[8,2,2,171]{3,2,1,0:T(2,128)} %broadcast_in_dim.25), calls=%async_computation | async-start | bytes 65536 | tf_op jit(solution)/shard_map/all_to_all | solution.py:325
  33.5 25.3 %copy-start.28 = (f32[2048]{0:T(1024)S(1)}, f32[2048]{0:T(1024)}, u32[]{:S(2)}) copy-start(f32[2048]{0:T(1024)} %param.24) | copy-start | bytes 24580
  36.1 22.7 %all-to-all-start.1 = ((bf16[16,16,2048]{2,1,0:T(8,128)(2,1)}), bf16[16,16,2048]{2,1,0:T(8,128)(2,1)S(1)}, u32[]{:S(2)}, u32[]{:S(2)}) async-start(bf16[16,16,2048]{2,1,0:T(8,128)(2,1)} %bitcast.329), calls=%async_computation.1 | async-start | bytes 2097152 | tf_op jit(solution)/shard_map/all_to_all | solution.py:412
  61.5 19.2 %all-to-all-start.2 = ((bf16[16,16,2048]{2,1,0:T(8,128)(2,1)}), bf16[16,16,2048]{2,1,0:T(8,128)(2,1)S(1)}, u32[]{:S(2)}, u32[]{:S(2)}) async-start(bf16[16,16,2048]{2,1,0:T(8,128)(2,1)} %copy-done.5), calls=%async_computation.2 | async-start | bytes 2097152 | tf_op jit(solution)/shard_map/all_to_all | solution.py:412
  65.7 79.6 %reduce-scatter.2.cloned.1.call-start = ((), (), s32[]{:S(2)}) async-start(), calls=%async_computation.9 | async-start | bytes 5308416 | tf_op jit(solution)/shard_map/reduce_scatter | solution.py:693
  90.5 19.7 %all-to-all-start.3 = ((bf16[16,16,2048]{2,1,0:T(8,128)(2,1)}), bf16[16,16,2048]{2,1,0:T(8,128)(2,1)S(1)}, u32[]{:S(2)}, u32[]{:S(2)}) async-start(bf16[16,16,2048]{2,1,0:T(8,128)(2,1)} %copy-done.4), calls=%async_computation.3 | async-start | bytes 2097152 | tf_op jit(solution)/shard_map/all_to_all | solution.py:412
  112.2 19.7 %copy-start.38 = (f32[1,2048]{1,0:T(1,128)}, f32[1,2048]{1,0:T(1,128)S(1)}, u32[]{:S(2)}) copy-start(f32[1,2048]{1,0:T(1,128)S(1)} %get-tuple-element.73) | copy-start | bytes 24580
  112.2 21.5 %copy-start.26 = (f32[16,2048]{1,0:T(8,128)}, f32[16,2048]{1,0:T(8,128)S(1)}, u32[]{:S(2)}) copy-start(f32[16,2048]{1,0:T(8,128)S(1)} %get-tuple-element.74.refs_3_) | copy-start | bytes 393220
  112.2 19.8 %copy-start.56 = (bf16[171,2048]{1,0:T(8,128)(2,1)S(1)}, bf16[171,2048]{1,0:T(8,128)(2,1)}, u32[]{:S(2)}) copy-start(bf16[171,2048]{1,0:T(8,128)(2,1)} %param.34) | copy-start | bytes 2101252
  131.9 13.4 %copy-start.15 = (bf16[1,171,171]{2,1,0:T(8,128)(2,1)S(1)}, bf16[1,171,171]{2,1,0:T(8,128)(2,1)}, u32[]{:S(2)}) copy-start(bf16[1,171,171]{2,1,0:T(8,128)(2,1)} %refs_16_.1) | copy-start | bytes 175450
  131.9 13.4 %copy-start.20 = (f32[2,128,171]{2,1,0:T(8,128)S(1)}, f32[2,128,171]{2,1,0:T(8,128)}, u32[]{:S(2)}) copy-start(f32[2,128,171]{2,1,0:T(8,128)} %copy-done.19) | copy-start | bytes 525316
  131.9 13.4 %copy-start.22 = (f32[2,128,171]{2,1,0:T(8,128)S(1)}, f32[2,128,171]{2,1,0:T(8,128)}, u32[]{:S(2)}) copy-start(f32[2,128,171]{2,1,0:T(8,128)} %copy-done.21) | copy-start | bytes 525316
  132.0 13.4 %copy-start.24 = (f32[2,128,171]{2,1,0:T(8,128)S(1)}, f32[2,128,171]{2,1,0:T(8,128)}, u32[]{:S(2)}) copy-start(f32[2,128,171]{2,1,0:T(8,128)} %copy-done.23) | copy-start | bytes 525316
  132.0 13.4 %copy-start.31 = (f32[4,171]{1,0:T(4,128)S(1)}, f32[4,171]{1,0:T(4,128)}, u32[]{:S(2)}) copy-start(f32[4,171]{1,0:T(4,128)} %refs_14_.1) | copy-start | bytes 8212
  132.0 13.4 %copy-start.33 = (f32[2,171]{1,0:T(2,128)S(1)}, f32[2,171]{1,0:T(2,128)}, u32[]{:S(2)}) copy-start(f32[2,171]{1,0:T(2,128)} %copy-done.32) | copy-start | bytes 4108
  132.9 16.5 %copy-start.39 = (f32[1,2048]{1,0:T(1,128)S(1)}, f32[1,2048]{1,0:T(1,128)}, u32[]{:S(2)}) copy-start(f32[1,2048]{1,0:T(1,128)} %copy-done.38) | copy-start | bytes 24580
  134.3 10.9 %all-to-all-start.5 = ((f32[8,2,2,171]{3,2,1,0:T(2,128)}), f32[8,2,2,171]{3,2,1,0:T(2,128)S(1)}, u32[]{:S(2)}, u32[]{:S(2)}) async-start(f32[8,2,2,171]{3,2,1,0:T(2,128)} %broadcast_in_dim.27), calls=%async_computation.5 | async-start | bytes 65536 | tf_op jit(solution)/shard_map/all_to_all | solution.py:325
  140.5 38.7 %all-gather.4.cloned.1.call-start = ((), (), s32[]{:S(2)}) async-start(), calls=%async_computation.10 | async-start | bytes 5308416 | tf_op jit(solution)/shard_map/all_gather | solution.py:739
  149.4 5.0 %collective-permute-start.1 = (f32[2,3,171]{2,1,0:T(4,128)S(1)}, f32[2,3,171]{2,1,0:T(4,128)S(1)}, u32[]{:S(2)}, u32[]{:S(2)}) collective-permute-start(f32[2,3,171]{2,1,0:T(4,128)S(1)} %get-tuple-element.71), channel_id=1, source_target_pairs={{16,0},{32,16},{48,32},{64,48},{80,64},{96,80},{112,96},{17,1},{33... | collective-permute-start | bytes 12320 | tf_op jit(solution)/shard_map/ppermute | solution.py:320
  158.9 37.9 %all-to-all-start.6 = ((bf16[16,16,4224]{2,1,0:T(8,128)(2,1)}), bf16[16,16,4224]{2,1,0:T(8,128)(2,1)S(1)}, u32[]{:S(2)}, u32[]{:S(2)}) async-start(bf16[16,16,4224]{2,1,0:T(8,128)(2,1)} %fusion.1), calls=%async_computation.7 | async-start | bytes 4325376 | tf_op jit(solution)/shard_map/all_to_all | solution.py:412
  162.8 61.6 %all-gather.6.cloned.1.call-start = ((), (), s32[]{:S(2)}) async-start(), calls=%async_computation.11 | async-start | bytes 2801664 | tf_op jit(solution)/shard_map/all_gather | solution.py:795
  167.0 3.2 %collective-permute-start.2 = (bf16[592,1024]{1,0:T(8,128)(2,1)}, bf16[592,1024]{1,0:T(8,128)(2,1)}, u32[]{:S(2)}, u32[]{:S(2)}) collective-permute-start(bf16[592,1024]{1,0:T(8,128)(2,1)} %pad_maximum_fusion.1), channel_id=1, source_target_pairs={{0,16},{16,0},{32,48},{48,32},{64,80},{80,64},{96,112},{112,96},{1... | collective-permute-start | bytes 3637256 | tf_op jit(solution)/shard_map/ppermute | solution.py:434
  172.8 14.1 %collective-permute-start.5 = (bf16[592,256]{1,0:T(8,128)(2,1)}, bf16[592,256]{1,0:T(8,128)(2,1)S(1)}, u32[]{:S(2)}, u32[]{:S(2)}) collective-permute-start(bf16[592,256]{1,0:T(8,128)(2,1)} %get-tuple-element.175), channel_id=1, source_target_pairs={{0,64},{16,80},{32,96},{48,112},{64,0},{80,16},{96,32},{112,48},{1... | collective-permute-start | bytes 909320 | tf_op jit(solution)/shard_map/ppermute | solution.py:438
  173.9 15.0 %collective-permute-start.4 = (bf16[592,256]{1,0:T(8,128)(2,1)}, bf16[592,256]{1,0:T(8,128)(2,1)S(1)}, u32[]{:S(2)}, u32[]{:S(2)}) collective-permute-start(bf16[592,256]{1,0:T(8,128)(2,1)} %get-tuple-element.176), channel_id=1, source_target_pairs={{0,96},{16,112},{32,0},{48,16},{64,32},{80,48},{96,64},{112,80},{1... | collective-permute-start | bytes 909320 | tf_op jit(solution)/shard_map/ppermute | solution.py:438
  175.5 21.4 %copy-start.7 = (bf16[16,2048]{1,0:T(8,128)(2,1)S(1)}, bf16[16,2048]{1,0:T(8,128)(2,1)}, u32[]{:S(2)}) copy-start(bf16[16,2048]{1,0:T(8,128)(2,1)} %constant_dynamic-slice_fusion.2.refs_1_) | copy-start | bytes 196612
  175.5 21.4 %copy-start.10 = (f32[16,2048]{1,0:T(8,128)S(1)}, f32[16,2048]{1,0:T(8,128)}, u32[]{:S(2)}) copy-start(f32[16,2048]{1,0:T(8,128)} %copy-done.8) | copy-start | bytes 393220
  175.5 21.4 %copy-start.27 = (f32[16,2048]{1,0:T(8,128)S(1)}, f32[16,2048]{1,0:T(8,128)}, u32[]{:S(2)}) copy-start(f32[16,2048]{1,0:T(8,128)} %copy-done.26) | copy-start | bytes 393220
  175.5 14.7 %collective-permute-start.3 = (bf16[592,256]{1,0:T(8,128)(2,1)}, bf16[592,256]{1,0:T(8,128)(2,1)}, u32[]{:S(2)}, u32[]{:S(2)}) collective-permute-start(bf16[592,256]{1,0:T(8,128)(2,1)} %get-tuple-element.177), channel_id=1, source_target_pairs={{0,32},{16,48},{32,64},{48,80},{64,96},{80,112},{96,0},{112,16},{1... | collective-permute-start | bytes 909320 | tf_op jit(solution)/shard_map/ppermute | solution.py:438
  200.5 38.2 %all-to-all-start.7 = ((bf16[16,2,16,2048]{3,2,1,0:T(8,128)(2,1)}), bf16[16,2,16,2048]{3,2,1,0:T(8,128)(2,1)}, u32[]{:S(2)}, u32[]{:S(2)}) async-start(bf16[16,2,16,2048]{3,2,1,0:T(8,128)(2,1)} %copy-done.3), calls=%async_computation.8 | async-start | bytes 4194304 | tf_op jit(solution)/shard_map/all_to_all | solution.py:412
  (47 other events, 262.4 us)
Sparse Core Ops, SparseCore 0:
  90.6 34.9 reduce-scatter.1
  148.4 30.7 all-gather.3
  200.6 23.6 all-gather.5

commit v3 on v2

--- a/solution.py
+++ b/solution.py
@@ -57,6 +57,19 @@
         total = total + length_ref[j]
         ends.append(total)
     return ends
+
+
+def gates(ext, conv_in, edge, masks, conv_w_ref, conv_b_ref, gate_a_ref, gate_x_ref, bias_a_ref, bias_x_ref):
+    rows, chans = conv_in.shape
+    ext[HALO - TAPS + 1 : HALO, :] = edge.astype(F32)
+    ext[HALO:, :] = conv_in.astype(F32)
+    conv_out = jnp.broadcast_to(conv_b_ref[...], (rows, chans))
+    for k in range(TAPS):
+        conv_out = conv_out + conv_w_ref[k : k + 1, :] * ext[HALO - k : HALO - k + rows, :] * masks[k]
+    low = conv_out.astype(BF16)
+    rate = jax.nn.sigmoid(dot(low, gate_a_ref[0], ((1,), (0,))) + bias_a_ref[...])
+    inlet = jax.nn.sigmoid(dot(low, gate_x_ref[0], ((1,), (0,))) + bias_x_ref[...])
+    return conv_out, rate, inlet
 
 
 def forward_kernel(
@@ -72,9 +85,6 @@
     bias_a_ref,
     bias_x_ref,
     decay_ref,
-    conv_out_ref,
-    rate_ref,
-    inlet_ref,
     keep_ref,
     run_ref,
     state_ref,
@@ -86,19 +96,9 @@
         length_ref = (short_ref, long_ref)[g]
         count = length_ref.shape[0]
         masks = doc_masks(row_ends(length_ref, count), count, start_ref[0], rows)
-        ext[g, HALO - TAPS + 1 : HALO, :] = edge_ref[g].astype(F32)
-        ext[g, HALO:, :] = conv_in_ref[g].astype(F32)
-        conv_out = jnp.broadcast_to(conv_b_ref[...], (rows, chans))
-        for k in range(TAPS):
-            conv_out = (
-                conv_out + conv_w_ref[k : k + 1, :] * ext[g, HALO - k : HALO - k + rows, :] * masks[k]
-            )
-        conv_out_ref[g] = conv_out
-        low = conv_out.astype(BF16)
-        rate = jax.nn.sigmoid(dot(low, gate_a_ref[0], ((1,), (0,))) + bias_a_ref[...])
-        inlet = jax.nn.sigmoid(dot(low, gate_x_ref[0], ((1,), (0,))) + bias_x_ref[...])
-        rate_ref[g] = rate
-        inlet_ref[g] = inlet
+        conv_out, rate, inlet = gates(
+            ext, conv_in_ref[g], edge_ref[g], masks, conv_w_ref, conv_b_ref, gate_a_ref, gate_x_ref, bias_a_ref, bias_x_ref
+        )
         log_decay = decay_ref[...] * rate
         keep_ref[g] = jnp.exp(log_decay) * masks[1]
         state_ref[g] = jnp.sqrt(-expm1_neg(2.0 * log_decay)) * inlet * conv_out
@@ -118,8 +118,9 @@
     first = tuple((jnp.ones((1, chans), F32), jnp.zeros((1, chans), F32)) for _ in range(groups))
     last = lax.fori_loop(0, rows, step, first, unroll=8)
     for g in range(groups):
-        carry_ref[0, g : g + 1, :] = last[g][0]
-        carry_ref[1, g : g + 1, :] = last[g][1]
+        for j in range(carry_ref.shape[0]):
+            carry_ref[j, 0, g : g + 1, :] = last[g][0]
+            carry_ref[j, 1, g : g + 1, :] = last[g][1]
 
 
 def gelu_parts(x):
@@ -164,8 +165,9 @@
     first = tuple((jnp.ones((1, chans), F32), jnp.zeros((1, chans), F32)) for _ in range(groups))
     last = lax.fori_loop(0, rows, step, first, unroll=8)
     for g in range(groups):
-        carry_ref[0, g : g + 1, :] = last[g][0]
-        carry_ref[1, g : g + 1, :] = last[g][1]
+        for j in range(carry_ref.shape[0]):
+            carry_ref[j, 0, g : g + 1, :] = last[g][0]
+            carry_ref[j, 1, g : g + 1, :] = last[g][1]
 
 
 def gates_back_kernel(
@@ -179,14 +181,14 @@
     state_in_ref,
     hidden_ref,
     keep_ref,
-    rate_ref,
-    inlet_ref,
-    conv_out_ref,
     conv_in_ref,
     edge_ref,
     conv_w_ref,
+    conv_b_ref,
     gate_a_ref,
     gate_x_ref,
+    bias_a_ref,
+    bias_x_ref,
     decay_ref,
     lam_slope_ref,
     d_conv_head_ref,
@@ -208,9 +210,9 @@
         prior[HALO - 1 : HALO, :] = state_in_ref[g : g + 1, :]
         prior[HALO:, :] = hidden_ref[g]
         d_keep = adjoint * prior[HALO - 1 : HALO - 1 + rows, :]
-        rate = rate_ref[g]
-        inlet = inlet_ref[g]
-        conv_out = conv_out_ref[g]
+        conv_out, rate, inlet = gates(
+            ext, conv_in_ref[g], edge_ref[g], masks, conv_w_ref, conv_b_ref, gate_a_ref, gate_x_ref, bias_a_ref, bias_x_ref
+        )
         decay = decay_ref[...]
         log_decay = decay * rate
         square = -expm1_neg(2.0 * log_decay)
@@ -233,8 +235,6 @@
             + dot(low_x, gate_x_ref[0], ((1,), (1,)))
         )
         sums[3] = sums[3] + jnp.sum(d_conv, axis=0, keepdims=True)
-        ext[HALO - TAPS + 1 : HALO, :] = edge_ref[g].astype(F32)
-        ext[HALO:, :] = conv_in_ref[g].astype(F32)
         d_input = conv_w_ref[0:1, :] * d_conv
         sums[4] = sums[4] + jnp.sum(d_conv * ext[HALO:, :], axis=0, keepdims=True)
         d_ext[rows:, :] = jnp.zeros((HALO, chans), F32)
@@ -267,14 +267,37 @@
     return pltpu.with_memory_space_constraint(array, pltpu.HBM)
 
 
+class Late:
+    def __init__(self, array):
+        self.array = in_hbm(array)
+
+
+class Arriving:
+    def __init__(self, copy, ref):
+        self.copy, self.ref, self.shape = copy, ref, ref.shape
+        copy.start()
+
+    def wait(self):
+        if self.copy is not None:
+            self.copy.wait()
+            self.copy = None
+
+    def __getitem__(self, index):
+        self.wait()
+        return self.ref[index]
+
+
 def run_kernel(kernel, name, outs, ins, scratch=(), flops=0, smem=0, after=(), passed=None, waits=0):
     vmem = pl.BlockSpec(memory_space=pltpu.VMEM)
     scalar = pl.BlockSpec(memory_space=pltpu.SMEM)
     anywhere = pl.BlockSpec(memory_space=pl.ANY)
+    late = [isinstance(a, Late) for a in ins]
+    ins = [a.array if isinstance(a, Late) else a for a in ins]
     moved = sum(a.size * a.dtype.itemsize for a in list(ins) + list(outs))
     count, skip = len(ins), len(after)
+    in_specs = [scalar] * smem + [anywhere if l else vmem for l in late[smem:]] + [anywhere] * skip
+    held = [pltpu.VMEM(a.shape, a.dtype) for a, l in zip(ins, late) if l]
     ins = [*ins, *[in_hbm(a) for a in after]]
-    in_specs = [scalar] * smem + [vmem] * (count - smem) + [anywhere] * skip
     out_specs = [vmem] * len(outs)
     outs, scratch = list(outs), list(scratch)
     if passed is not None:
@@ -285,13 +308,20 @@
         scratch += [pltpu.VMEM(passed.shape, passed.dtype), pltpu.SemaphoreType.DMA((2,))]
 
     def run(*refs):
+        if held:
+            refs, arrived, sems = list(refs[: -len(held) - 1]), refs[-len(held) - 1 : -1], refs[-1]
+            for n, i in enumerate([i for i in range(count) if late[i]]):
+                refs[i] = Arriving(pltpu.make_async_copy(refs[i], arrived[n], sems.at[n]), arrived[n])
         if passed is None:
             kernel(*refs[:count], *refs[count + skip :])
+            for ref in refs[:count]:
+                if isinstance(ref, Arriving):
+                    ref.wait()
             return
         in_ref, out_ref = refs[count + skip], refs[count + skip + len(outs)]
-        held, sems = refs[-2:]
-        fetch = pltpu.make_async_copy(in_ref, held, sems.at[0])
-        store = pltpu.make_async_copy(held, out_ref, sems.at[1])
+        buffer, both_sems = refs[-2:]
+        fetch = pltpu.make_async_copy(in_ref, buffer, both_sems.at[0])
+        store = pltpu.make_async_copy(buffer, out_ref, both_sems.at[1])
         fetch.start()
 
         def midway():
@@ -308,10 +338,83 @@
         out_shape=outs,
         in_specs=in_specs,
         out_specs=out_specs,
-        scratch_shapes=scratch,
+        scratch_shapes=scratch + ([*held, pltpu.SemaphoreType.DMA((len(held),))] if held else []),
         cost_estimate=pl.CostEstimate(flops=flops, bytes_accessed=moved + waits * HBM_PER_US, transcendentals=0),
         compiler_params=pltpu.CompilerParams(vmem_limit_bytes=VMEM_LIMIT),
     )(*ins)
+
+
+def front(tokens, gain, w_x, w_y, groups):
+    total, width = tokens.shape
+    chans = w_x.shape[0]
+    rows = total // groups
+    step = total // 4
+
+    def run(gain_ref, *refs):
+        sources, outs, held, kept, sems = refs[:3], refs[3:8], refs[8:10], refs[10:13], refs[13]
+        normed_out, scale_ref, conv_in_ref, edge_ref, gate_out = outs
+        tokens_ref, normed_ref, gate_ref = kept
+        reads = []
+        for n in range(4):
+            part = pl.ds(n * step, step)
+            reads.append(pltpu.make_async_copy(sources[0].at[part], tokens_ref.at[part], sems.at[n]))
+            reads[-1].start()
+        w_x_ref, w_y_ref = [
+            Arriving(pltpu.make_async_copy(source, ref, sems.at[4 + n]), ref)
+            for n, (source, ref) in enumerate(zip(sources[1:], held))
+        ]
+        stores = []
+        for n in range(4):
+            reads[n].wait()
+            for at in range(n * step, (n + 1) * step, 32):
+                part = slice(at, at + 32)
+                features = tokens_ref[part, :].astype(F32)
+                scale = rms(features)
+                scale_ref[part, :] = scale
+                normed_ref[part, :] = (features * scale * gain_ref[...]).astype(BF16)
+            part = pl.ds(n * step, step)
+            stores.append(pltpu.make_async_copy(normed_ref.at[part], normed_out.at[part], sems.at[6 + n]))
+            stores[-1].start()
+        for g in range(groups):
+            part = normed_ref[g * rows : (g + 1) * rows, :]
+            gate_ref[g] = dot(part, w_y_ref[...], ((1,), (1,)))
+        stores.append(pltpu.make_async_copy(gate_ref, gate_out, sems.at[10]))
+        stores[-1].start()
+        for g in range(groups):
+            part = normed_ref[g * rows : (g + 1) * rows, :]
+            conv_in = dot(part, w_x_ref[...], ((1,), (1,))).astype(BF16)
+            conv_in_ref[g] = conv_in
+            edge_ref[g] = conv_in[rows - TAPS + 1 :, :]
+        for store in stores:
+            store.wait()
+
+    vmem = pl.BlockSpec(memory_space=pltpu.VMEM)
+    anywhere = pl.BlockSpec(memory_space=pl.ANY)
+    return pl.pallas_call(
+        run,
+        name="front",
+        in_specs=[vmem] + [anywhere] * 3,
+        out_specs=[anywhere, vmem, vmem, vmem, anywhere],
+        out_shape=[
+            pltpu.HBM((total, width), BF16),
+            sds((total, 1)),
+            sds((groups, rows, chans), BF16),
+            sds((groups, TAPS - 1, chans), BF16),
+            pltpu.HBM((groups, rows, chans), F32),
+        ],
+        scratch_shapes=[
+            pltpu.VMEM(w_x.shape, BF16),
+            pltpu.VMEM(w_y.shape, BF16),
+            pltpu.VMEM((total, width), BF16),
+            pltpu.VMEM((total, width), BF16),
+            pltpu.VMEM((groups, rows, chans), F32),
+            pltpu.SemaphoreType.DMA((11,)),
+        ],
+        cost_estimate=pl.CostEstimate(
+            flops=4 * total * chans * width, bytes_accessed=4 * total * width, transcendentals=0
+        ),
+        compiler_params=pltpu.CompilerParams(vmem_limit_bytes=VMEM_LIMIT),
+    )(gain[None], in_hbm(tokens), in_hbm(w_x), in_hbm(w_y))
 
 
 def shifted(block, axis, distance):
@@ -322,8 +425,8 @@
 
 def carried_in(value, backward):
     count, mine = lax.axis_size("seq"), lax.axis_index("seq")
-    pieces = lax.all_to_all(jnp.broadcast_to(value[None], (count,) + value.shape), "seq", 0, 0)
-    total = jnp.zeros(value.shape[1:], F32)
+    pieces = lax.all_to_all(value, "seq", 0, 0)
+    total = jnp.zeros(value.shape[2:], F32)
     for j in range(count - 1, 0, -1) if backward else range(count - 1):
         longer = pieces[j, 1] + pieces[j, 0] * total
         total = jnp.where((j > mine) if backward else (j < mine), longer, total)
@@ -387,25 +490,41 @@
 
 def split_both(both, after):
     owners, _, share, width = both.shape
-
-    def run(both_ref, after_ref, d_tokens_ref, layer_ref):
-        d_tokens_ref[...] = both_ref[:, 0].astype(F32)
-        layer_ref[...] = both_ref[:, 1]
-
-    part = pl.BlockSpec((owners, share, WIDE), lambda i: (0, 0, i))
+    parts = 8
+    step = owners // parts
+
+    def run(both_hbm, after_ref, d_tokens_hbm, layer_hbm, held, wide, sems):
+        reads, stores = [], []
+        for n in range(parts):
+            part = pl.ds(n * step, step)
+            reads.append(pltpu.make_async_copy(both_hbm.at[part], held.at[part], sems.at[n]))
+            reads[-1].start()
+        for n in range(parts):
+            part = pl.ds(n * step, step)
+            reads[n].wait()
+            stores.append(pltpu.make_async_copy(held.at[part, 1], layer_hbm.at[part], sems.at[parts + n]))
+            stores[-1].start()
+            wide[n * step : (n + 1) * step] = held[n * step : (n + 1) * step, 0].astype(F32)
+            stores.append(pltpu.make_async_copy(wide.at[part], d_tokens_hbm.at[part], sems.at[2 * parts + n]))
+            stores[-1].start()
+        for store in stores:
+            store.wait()
+
+    anywhere = pl.BlockSpec(memory_space=pl.ANY)
     return pl.pallas_call(
         run,
         name="split_both",
-        grid=(width // WIDE,),
-        in_specs=[
-            pl.BlockSpec((owners, 2, share, WIDE), lambda i: (0, 0, 0, i)),
-            pl.BlockSpec(memory_space=pl.ANY),
+        in_specs=[anywhere] * 2,
+        out_specs=[anywhere] * 2,
+        out_shape=[pltpu.HBM((owners, share, width), F32), pltpu.HBM((owners, share, width), BF16)],
+        scratch_shapes=[
+            pltpu.VMEM(both.shape, BF16),
+            pltpu.VMEM((owners, share, width), F32),
+            pltpu.SemaphoreType.DMA((3 * parts,)),
         ],
-        out_specs=[part, part],
-        out_shape=[pltpu.HBM((owners, share, width), F32), pltpu.HBM((owners, share, width), BF16)],
         cost_estimate=pl.CostEstimate(flops=0, bytes_accessed=5 * both.size, transcendentals=0),
         compiler_params=pltpu.CompilerParams(vmem_limit_bytes=VMEM_LIMIT),
-    )(both, in_hbm(after))
+    )(in_hbm(both), in_hbm(after))
 
 
 def exchange(pieces):
@@ -503,70 +622,62 @@
         gains_ref[...] += gains
 
 
-def mlp_kernel(normed_ref, d_hidden_ref, one_hbm, two_hbm, cot_hbm, parts_ref, hidden_ref, grads_hbm, one, two, cot, grads, sems):
-    owners, share, width = parts_ref.shape
-    units = one.shape[1]
-    fetches = [
-        pltpu.make_async_copy(source, held, sems.at[n])
-        for n, (source, held) in enumerate(((one_hbm, one), (two_hbm, two), (cot_hbm, cot)))
-    ]
-    for fetch in fetches:
-        fetch.start()
-    normed = normed_ref[...]
-    fetches[0].wait()
-    value, slope = gelu_parts(dot(normed, one[...], ((1,), (0,))))
-    fetches[1].wait()
-    up = dot(normed, two[...], ((1,), (0,)))
-    d_hidden = d_hidden_ref[...]
-    hidden = (value * up).astype(BF16)
-    d_gate = (d_hidden * up * slope).astype(BF16)
-    d_up = (d_hidden * value).astype(BF16)
-    hidden_ref[...] = hidden
-    for at in range(0, width, WIDE):
-        cols = slice(at, at + WIDE)
-        back = dot(d_gate, one[cols, :], ((1,), (1,))) + dot(d_up, two[cols, :], ((1,), (1,)))
-        parts_ref[:, :, cols] = back.astype(BF16).reshape(owners, share, WIDE)
-    fetches[2].wait()
-    stores = []
-    for n, at in enumerate(range(0, width, WIDE)):
-        cols = slice(at, at + WIDE)
-        part = normed_ref[:, cols]
-        grads[cols, :units] = dot(part, d_gate, ((0,), (0,))).astype(BF16)
-        grads[cols, units : 2 * units] = dot(part, d_up, ((0,), (0,))).astype(BF16)
-        grads[cols, 2 * units :] = dot(cot[:, cols], hidden, ((0,), (0,))).astype(BF16)
-        stores.append(pltpu.make_async_copy(grads.at[cols], grads_hbm.at[cols], sems.at[3 + n]))
-        stores[-1].start()
-    for store in stores:
-        store.wait()
-
-
 def mlp_back(normed, d_hidden, w_one, w_two, cotangent, owners):
     rows, width = normed.shape
     units = w_one.shape[1]
-    vmem = pl.BlockSpec(memory_space=pltpu.VMEM)
+    share = rows // owners
+    steps = range(0, width, WIDE)
+
+    def run(*refs):
+        ins, (parts_out, hidden_out, grads_out) = refs[:5], refs[5:8]
+        held, parts, kept_hidden, grads, sems = refs[8:13], refs[13], refs[14], refs[15], refs[16]
+        normed, one, two, d_hidden, cot = [
+            Arriving(pltpu.make_async_copy(source, ref, sems.at[n]), ref) for n, (source, ref) in enumerate(zip(ins, held))
+        ]
+        stores = []
+
+        def store(source, target):
+            stores.append(pltpu.make_async_copy(source, target, sems.at[len(ins) + len(stores)]))
+            stores[-1].start()
+
+        value, slope = gelu_parts(dot(normed[...], one[...], ((1,), (0,))))
+        up = dot(normed[...], two[...], ((1,), (0,)))
+        hidden = (value * up).astype(BF16)
+        kept_hidden[...] = hidden
+        store(kept_hidden, hidden_out)
+        d_gate = (d_hidden[...] * up * slope).astype(BF16)
+        d_up = (d_hidden[...] * value).astype(BF16)
+        for at in steps:
+            cols = slice(at, at + WIDE)
+            back = dot(d_gate, one[cols, :], ((1,), (1,))) + dot(d_up, two[cols, :], ((1,), (1,)))
+            parts[:, :, cols] = back.astype(BF16).reshape(owners, share, WIDE)
+        store(parts, parts_out)
+        for at in steps:
+            cols = slice(at, at + WIDE)
+            grads[cols, :units] = dot(normed[:, cols], d_gate, ((0,), (0,))).astype(BF16)
+            grads[cols, units : 2 * units] = dot(normed[:, cols], d_up, ((0,), (0,))).astype(BF16)
+            grads[cols, 2 * units :] = dot(cot[:, cols], hidden, ((0,), (0,))).astype(BF16)
+            store(grads.at[cols], grads_out.at[cols])
+        for copy in stores:
+            copy.wait()
+
+    ins = [in_hbm(a) for a in (normed, w_one, w_two, d_hidden, cotangent)]
+    outs = [((owners, share, width), BF16), ((rows, units), BF16), ((width, 3 * units), BF16)]
     anywhere = pl.BlockSpec(memory_space=pl.ANY)
     return pl.pallas_call(
-        mlp_kernel,
+        run,
         name="mlp",
-        in_specs=[vmem, vmem, anywhere, anywhere, anywhere],
-        out_specs=[vmem, vmem, anywhere],
-        out_shape=[
-            sds((owners, rows // owners, width), BF16),
-            sds((rows, units), BF16),
-            pltpu.HBM((width, 3 * units), BF16),
-        ],
-        scratch_shapes=[
-            pltpu.VMEM((width, units), BF16),
-            pltpu.VMEM((width, units), BF16),
-            pltpu.VMEM((rows, width), BF16),
-            pltpu.VMEM((width, 3 * units), BF16),
-            pltpu.SemaphoreType.DMA((3 + width // WIDE,)),
-        ],
+        in_specs=[anywhere] * len(ins),
+        out_specs=[anywhere] * len(outs),
+        out_shape=[pltpu.HBM(*out) for out in outs],
+        scratch_shapes=[pltpu.VMEM(a.shape, a.dtype) for a in ins]
+        + [pltpu.VMEM(*out) for out in outs]
+        + [pltpu.SemaphoreType.DMA((len(ins) + 2 + len(steps),))],
         cost_estimate=pl.CostEstimate(
             flops=14 * rows * width * units, bytes_accessed=14 * width * units, transcendentals=0
         ),
         compiler_params=pltpu.CompilerParams(vmem_limit_bytes=2 * VMEM_LIMIT),
-    )(normed, d_hidden, in_hbm(w_one), in_hbm(w_two), in_hbm(cotangent))
+    )(*ins)
 
 
 def place_mlp(bundle, units):
@@ -631,20 +742,17 @@
     cotangent = cotangent.reshape(total_rows, width)
     tokens_f = tokens.astype(F32)
     tokens_share = mine(tokens)
-    scale_one = rms(tokens_f)
-    normed_one = (tokens_f * scale_one * gain_one).astype(BF16)
-    conv_input = grouped(dot(normed_one, w_x, ((1,), (0,))).astype(BF16))
-    edge = shifted(conv_input[:, rows - TAPS + 1 :], "seq", 1)
-    gate_pre = grouped(dot(normed_one, w_y, ((1,), (0,))))
+    normed_one, scale_one, conv_input, edge, gate_pre = front(tokens, gain_one, w_x.T, w_y.T, groups)
+    edge = shifted(edge, "seq", 1)
 
     decay = (-8.0 * jax.nn.softplus(-lam))[None]
     lam_slope = (8.0 * jax.nn.sigmoid(-lam))[None]
     big = sds((groups, rows, chans))
     flops = 2 * total_rows * chans * chans
-    conv_out, rate, inlet, keep, decay_run, local_state, carry = run_kernel(
+    keep, decay_run, local_state, carry = run_kernel(
         forward_kernel,
         "conv_gates_scan",
-        [big] * 6 + [sds((2, groups, chans))],
+        [big] * 3 + [sds((seq_count, 2, groups, chans))],
         [
             start,
             short_lengths,
@@ -659,7 +767,7 @@
             bias_x[None],
             decay,
         ],
-        [pltpu.VMEM((groups, HALO + rows, chans), F32)],
+        [pltpu.VMEM((HALO + rows, chans), F32)],
         flops=2 * flops,
         smem=3,
     )
@@ -673,7 +781,7 @@
         mid_kernel,
         "resid_mid_norm",
         [share, to_all],
-        [exchange(by_owner(dot(mixed_in, w_out, ((1,), (0,))))), tokens_share, gain_two[None]],
+        [exchange(by_owner(dot(mixed_in, w_out, ((1,), (0,))))), Late(tokens_share), gain_two[None]],
         waits=20,
     )
     normed_two = exchange(normed_two).reshape(total_rows, width)
@@ -685,7 +793,7 @@
         mid_back_kernel,
         "d_mid",
         [share, sds((1, width)), to_all],
-        [exchange(two_parts), resid_share, mine(cotangent), gain_two[None]],
+        [exchange(two_parts), Late(resid_share), Late(mine(cotangent)), gain_two[None]],
         after=[g_mlp, partial_out],
         waits=20,
     )
@@ -696,7 +804,7 @@
     d_gate_pre, reach, local_adjoint, carry_back = run_kernel(
         adjoint_kernel,
         "adjoint_scan",
-        [sds((groups, rows, chans), BF16), big, big, sds((2, groups, chans))],
+        [sds((groups, rows, chans), BF16), big, big, sds((seq_count, 2, groups, chans))],
         [d_mixed, gate_pre, hidden, keep],
         waits=20,
     )
@@ -715,14 +823,14 @@
             state_in,
             hidden,
             keep,
-            rate,
-            inlet,
-            conv_out,
             conv_input,
             edge,
             conv_w,
+            conv_b[None],
             gate_a,
             gate_x,
+            bias_a[None],
+            bias_x[None],
             decay,
             lam_slope,
         ],
@@ -785,7 +893,7 @@
         tokens_back_kernel,
         "d_tokens",
         [sds((ch_count, 2, share_rows, width), BF16), sds((chunk_parts[0].shape[0] + GAIN_ROWS, LANES), BF16)],
-        [back_pieces, tokens_share, resid_share, d_mid, gain_one[None], *chunk_parts],
+        [back_pieces, Late(tokens_share), Late(resid_share), Late(d_mid), gain_one[None], *chunk_parts],
         after=[g_w_one],
         waits=30,
     )

time: 251 us -> 241 us (0.960)
  local copies, waits for them, and re-layouts: 22.1 us -> 13.1 us
  Pallas kernels: 30.8 us -> 36 us
  other arithmetic: 11.7 us -> 7.94 us
  blocking collectives: 19.7 us -> 17 us
    unnamed x129 -> x75, local copies, waits for them, and re-layouts: 16 us -> 8.38 us
    pallas_call x6, Pallas kernels: 8.53 us -> 11.2 us  [run_kernel(): pl.pallas_call(run, name=name, out_shape=outs, in_specs=in_specs, out_spe...]
    all_to_all x1, blocking collectives: 19.7 us -> 17 us  [exchange(): return lax.all_to_all(pieces, 'ch', 0, 0)]
    pallas_call x2 -> x3, Pallas kernels: 11 us -> 13.6 us  [the longest x1 7.67 us: mlp_back(): pl.pallas_call(run, name='mlp', in_specs=[anywhere] * len(ins), out_specs...]
    dot_general x14 -> x12, matrix products: 16.9 us -> 14.7 us  [dot(): lax.dot_general(left, right, (contract, ((), ())), preferred_element_type...]
  transfers between devices with their start and end apart: 16 -> 16, of which waited for: 14 -> 14; matrix products, arithmetic and copies ran while one was open for 12% -> 11% of each run, Pallas kernels for 5% -> 6%
where the time goes in v3:
time: 241 us; the launch traced here: 240 us
  waiting for transfers between devices  88.4 us (37%)
  starting transfers between devices  48.3 us (20%)
  Pallas kernels  36 us (15%)
  blocking collectives  17 us (7%)
  matrix products  14.7 us (6%)
  between operations  14.4 us (6%)
  local copies, waits for them, and re-layouts  13.1 us (5%)
  other arithmetic  7.94 us (3%)
    all_to_all x5, waiting for transfers between devices, exchange(): return lax.all_to_all(pieces, 'ch', 0, 0)  49.4 us
    all_to_all x5, starting transfers between devices, exchange(): return lax.all_to_all(pieces, 'ch', 0, 0)  23.2 us
    all_gather x1, waiting for transfers between devices, body(): lax.all_gather(chunk, 'seq')  19.5 us
    all_to_all x1, blocking collectives, exchange(): return lax.all_to_all(pieces, 'ch', 0, 0)  17 us
    dot_general x12, matrix products, dot(): lax.dot_general(left, right, (contract, ((), ())), preferred_element_type...  14.7 us
    all_to_all x2, starting transfers between devices, carried_in(): pieces = lax.all_to_all(value, 'seq', 0, 0)  14.4 us
    pallas_call x6, Pallas kernels, run_kernel(): pl.pallas_call(run, name=name, out_shape=outs, in_specs=in_specs, out_spe...  11.2 us
    all_to_all x2, waiting for transfers between devices, carried_in(): pieces = lax.all_to_all(value, 'seq', 0, 0)  9.45 us
  transfers between devices with their start and end apart: 16, of which 14 were waited for; matrix products, arithmetic and copies ran while one was open for 11% of the time, Pallas kernels for 6%

profile of v3, /device:TPU:1, one launch (start us, length us, event | category | flops | bytes accessed | tf_op | source)
XLA Modules:
  0.0 239.9 jit_solution(7699009988292486114)
XLA Ops:
  8.1 3.1 %front.1 = (bf16[256,2048]{1,0:T(8,128)(2,1)}, f32[256,1]{1,0:T(8,128)S(1)}, bf16[2,128,171]{2,1,0:T(8,128)(2,1)S(1)}, bf16[2,3,171]{2,1,0:T(4,128)(2,1)S(1)}, f32[2,128,171]{2,1,0:T(8,128)}) custom-call(f32[1,2048]{1,0:T(1,128)S(1)} %bitcast.303, bf16[256,2048]{1,0:T(8,128)(2,1)} %bitcast.321, bf16[171,2048]{1,0:T(8,128)(2,1)} %bitcast.329, ...), custom_call_target="tpu_custom_call" | custom-call | flops 358612992 | bytes 2097152 | tf_op jit(solution)/shard_map/front/pallas_call | solution.py:393
  11.2 4.9 %collective-permute-start = (bf16[2,3,171]{2,1,0:T(4,128)(2,1)S(1)}, bf16[2,3,171]{2,1,0:T(4,128)(2,1)S(1)}, u32[]{:S(2)}, u32[]{:S(2)}) collective-permute-start(bf16[2,3,171]{2,1,0:T(4,128)(2,1)S(1)} %get-tuple-element.57), channel_id=1, source_target_pairs={{0,16},{16,32},{32,48},{48,64},{64,80},{80,96},{96,112},{1,17},{17... | collective-permute-start | bytes 6164 | tf_op jit(solution)/shard_map/ppermute | solution.py:423
  17.0 2.8 %conv_gates_scan.1 = (f32[2,128,171]{2,1,0:T(8,128)S(1)}, f32[2,128,171]{2,1,0:T(8,128)S(1)}, f32[2,128,171]{2,1,0:T(8,128)S(1)}, f32[8,2,2,171]{3,2,1,0:T(2,128)}) custom-call(s32[1]{0:T(128)} %bitcast.refs_0_, s32[8]{0:T(128)S(1)} %copy-done.24, s32[3]{0:T(128)S(1)} %copy-done.23, bf16[2,128,171]{2,1,0:T(8,128)(2,1)S(1)} %get-tuple-element.56.refs_3_.refs_9_, ...), custom_call_target="tpu_custom_call" | custom-call | flops 29942784 | bytes 759288 | tf_op jit(solution)/shard_map/conv_gates_scan/pallas_call | solution.py:335
  19.8 6.1 %all-to-all-start = ((f32[8,2,2,171]{3,2,1,0:T(2,128)}), f32[8,2,2,171]{3,2,1,0:T(2,128)S(1)}, u32[]{:S(2)}, u32[]{:S(2)}) async-start(f32[8,2,2,171]{3,2,1,0:T(2,128)} %get-tuple-element.60), calls=%async_computation | async-start | bytes 65536 | tf_op jit(solution)/shard_map/all_to_all | solution.py:428
  25.9 4.7 %all-to-all-done = f32[8,2,2,171]{3,2,1,0:T(2,128)S(1)} async-done(((f32[8,2,2,171]{3,2,1,0:T(2,128)}), f32[8,2,2,171]{3,2,1,0:T(2,128)S(1)}, u32[]{:S(2)}, u32[]{:S(2)}) %all-to-all-start) | async-done | bytes 21920 | tf_op jit(solution)/shard_map/all_to_all | solution.py:428
  31.7 2.6 %convolution_convert_fusion.1 = bf16[256,2048]{1,0:T(8,128)(2,1)} fusion(bf16[256,171]{1,0:T(8,128)(2,1)S(1)} %bitcast.334, bf16[171,2048]{1,0:T(8,128)(2,1)} %param.34), kind=kOutput, calls=%fused_computation.4 | convolution fusion | flops 179830784 | bytes 1836544 | tf_op jit(solution)/shard_map/dot_general | solution.py:25
  34.3 6.8 %all-to-all-start.1 = ((bf16[16,16,2048]{2,1,0:T(8,128)(2,1)}), bf16[16,16,2048]{2,1,0:T(8,128)(2,1)S(1)}, u32[]{:S(2)}, u32[]{:S(2)}) async-start(bf16[16,16,2048]{2,1,0:T(8,128)(2,1)} %bitcast.323), calls=%async_computation.1 | async-start | bytes 2097152 | tf_op jit(solution)/shard_map/all_to_all | solution.py:531
  42.5 14.4 %all-to-all-done.1.refs_0_ = bf16[16,16,2048]{2,1,0:T(8,128)(2,1)S(1)} async-done(((bf16[16,16,2048]{2,1,0:T(8,128)(2,1)}), bf16[16,16,2048]{2,1,0:T(8,128)(2,1)S(1)}, u32[]{:S(2)}, u32[]{:S(2)}) %all-to-all-start.1) | async-done | bytes 1048608 | tf_op jit(solution)/shard_map/all_to_all | solution.py:531
  59.1 4.5 %all-to-all-start.2 = ((bf16[16,16,2048]{2,1,0:T(8,128)(2,1)}), bf16[16,16,2048]{2,1,0:T(8,128)(2,1)}, u32[]{:S(2)}, u32[]{:S(2)}) async-start(bf16[16,16,2048]{2,1,0:T(8,128)(2,1)} %copy-done.4), calls=%async_computation.2 | async-start | bytes 2097152 | tf_op jit(solution)/shard_map/all_to_all | solution.py:531
  65.1 13.2 %all-to-all-done.2 = bf16[16,16,2048]{2,1,0:T(8,128)(2,1)} async-done(((bf16[16,16,2048]{2,1,0:T(8,128)(2,1)}), bf16[16,16,2048]{2,1,0:T(8,128)(2,1)}, u32[]{:S(2)}, u32[]{:S(2)}) %all-to-all-start.2) | async-done | bytes 1048608 | tf_op jit(solution)/shard_map/all_to_all | solution.py:531
  78.3 7.7 %mlp.1 = (bf16[16,16,2048]{2,1,0:T(8,128)(2,1)}, bf16[256,384]{1,0:T(8,128)(2,1)}, bf16[2048,1152]{1,0:T(8,128)(2,1)}) custom-call(bf16[256,2048]{1,0:T(8,128)(2,1)} %bitcast.25.refs_0_, bf16[2048,384]{1,0:T(8,128)(2,1)} %refs_1_.4, bf16[2048,384]{1,0:T(8,128)(2,1)} %refs_2_.4, f32[256,384]{1,0:T(8,128)} %fusion.106.refs_3_, bf16[256,2048]{1,0:T(8,128)(2,1)} %bitcast.331), custom_call_target="tpu_custom_call" | custom-call | flops 2818572288 | bytes 11010048 | tf_op jit(solution)/shard_map/mlp/pallas_call | solution.py:667
  86.0 3.7 %all-to-all-start.3 = ((bf16[16,16,2048]{2,1,0:T(8,128)(2,1)}), bf16[16,16,2048]{2,1,0:T(8,128)(2,1)S(1)}, u32[]{:S(2)}, u32[]{:S(2)}) async-start(bf16[16,16,2048]{2,1,0:T(8,128)(2,1)} %get-tuple-element.63), calls=%async_computation.3 | async-start | bytes 2097152 | tf_op jit(solution)/shard_map/all_to_all | solution.py:531
  91.2 2.6 %convolution_convert_fusion = bf16[256,2048]{1,0:T(8,128)(2,1)} fusion(bf16[256,384]{1,0:T(8,128)(2,1)} %get-tuple-element.66, bf16[384,2048]{1,0:T(8,128)(2,1)S(1)} %copy-done), kind=kOutput, calls=%fused_computation.3 | convolution fusion | flops 403177472 | bytes 2818048 | tf_op jit(solution)/shard_map/dot_general | solution.py:25
  93.8 9.6 %all-to-all-done.3.refs_0_ = bf16[16,16,2048]{2,1,0:T(8,128)(2,1)S(1)} async-done(((bf16[16,16,2048]{2,1,0:T(8,128)(2,1)}), bf16[16,16,2048]{2,1,0:T(8,128)(2,1)S(1)}, u32[]{:S(2)}, u32[]{:S(2)}) %all-to-all-start.3) | async-done | bytes 1048608 | tf_op jit(solution)/shard_map/all_to_all | solution.py:531
  105.5 17.0 %all_to_all.40 = bf16[16,16,2048]{2,1,0:T(8,128)(2,1)S(1)} all-to-all(bf16[16,16,2048]{2,1,0:T(8,128)(2,1)S(1)} %get-tuple-element.67), channel_id=1, replica_groups=mesh['seq'=8,'ch'=16] {'ch'}, dimensions={0} | all-to-all | bytes 2097152 | tf_op jit(solution)/shard_map/all_to_all | solution.py:531
  124.9 8.3 %all-to-all-start.5 = ((f32[8,2,2,171]{3,2,1,0:T(2,128)}), f32[8,2,2,171]{3,2,1,0:T(2,128)S(1)}, u32[]{:S(2)}, u32[]{:S(2)}) async-start(f32[8,2,2,171]{3,2,1,0:T(2,128)} %get-tuple-element.71), calls=%async_computation.5 | async-start | bytes 65536 | tf_op jit(solution)/shard_map/all_to_all | solution.py:428
  133.2 4.7 %all-to-all-done.5 = f32[8,2,2,171]{3,2,1,0:T(2,128)S(1)} async-done(((f32[8,2,2,171]{3,2,1,0:T(2,128)}), f32[8,2,2,171]{3,2,1,0:T(2,128)S(1)}, u32[]{:S(2)}, u32[]{:S(2)}) %all-to-all-start.5) | async-done | bytes 21920 | tf_op jit(solution)/shard_map/all_to_all | solution.py:428
  138.1 2.7 %gates_back.1 = (f32[2,3,171]{2,1,0:T(4,128)S(1)}, f32[2,128,171]{2,1,0:T(8,128)S(1)}, f32[64,2048]{1,0:T(8,128)S(1)}, bf16[256,1152]{1,0:T(8,128)(2,1)}) custom-call(s32[1]{0:T(128)} %bitcast.refs_0_, s32[8]{0:T(128)S(1)} %copy-done.24, s32[3]{0:T(128)S(1)} %copy-done.23, f32[2,128,171]{2,1,0:T(8,128)S(1)} %get-tuple-element.69.refs_3_, ...), custom_call_target="tpu_custom_call" | custom-call | flops 59885568 | bytes 37619420 | tf_op jit(solution)/shard_map/gates_back/pallas_call | solution.py:335
  142.0 2.6 %collective-permute-start.1 = (f32[2,3,171]{2,1,0:T(4,128)S(1)}, f32[2,3,171]{2,1,0:T(4,128)S(1)}, u32[]{:S(2)}, u32[]{:S(2)}) collective-permute-start(f32[2,3,171]{2,1,0:T(4,128)S(1)} %get-tuple-element.73), channel_id=1, source_target_pairs={{16,0},{32,16},{48,32},{64,48},{80,64},{96,80},{112,96},{17,1},{33... | collective-permute-start | bytes 12320 | tf_op jit(solution)/shard_map/ppermute | solution.py:423
  147.6 2.2 fusion.103
  151.4 3.9 %all-to-all-start.6 = ((bf16[16,16,4224]{2,1,0:T(8,128)(2,1)}), bf16[16,16,4224]{2,1,0:T(8,128)(2,1)S(1)}, u32[]{:S(2)}, u32[]{:S(2)}) async-start(bf16[16,16,4224]{2,1,0:T(8,128)(2,1)} %fusion.1), calls=%async_computation.7 | async-start | bytes 4325376 | tf_op jit(solution)/shard_map/all_to_all | solution.py:531
  162.8 2.5 %add_convert_fusion = (bf16[592,256]{1,0:T(8,128)(2,1)}, bf16[592,256]{1,0:T(8,128)(2,1)}, bf16[592,256]{1,0:T(8,128)(2,1)}, bf16[592,256]{1,0:T(8,128)(2,1)S(1)}) fusion(f32[592,1024]{1,0:T(8,128)S(1)} %pad_maximum_fusion, s32[]{:T(128)S(6)} %select_n.230, bf16[592,1024]{1,0:T(8,128)(2,1)} %collective-permute-done.2, s32[]{:T(128)S(6)} %select_n.228, ...), kind=kLoop, calls=%fused_computation.14 | loop fusion | flops 1818624 | bytes 4849680 | tf_op jit(solution)/shard_map/convert_element_type | solution.py:574
  168.3 3.3 %all-gather.4.cloned.1.call-done.piece_ref = bf16[2048,1152]{1,0:T(8,128)(2,1)} async-done(((bf16[256,1152]{1,0:T(8,128)(2,1)}), bf16[2048,1152]{1,0:T(8,128)(2,1)}) %all-gather.4.cloned.1.call-update) | async-done | bytes 4718608 | tf_op jit(solution)/shard_map/all_gather | solution.py:847
  171.6 7.7 %place_mlp.1 = (f32[2048,384]{1,0:T(8,128)}, f32[2048,384]{1,0:T(8,128)}, f32[384,2048]{1,0:T(8,128)}) custom-call(bf16[2048,1152]{1,0:T(8,128)(2,1)} %all-gather.4.cloned.1.call-done.piece_ref), custom_call_target="tpu_custom_call" | custom-call | bytes 14155776 | tf_op jit(solution)/shard_map/place_mlp/pallas_call | solution.py:692
  179.3 2.1 collective-permute-done.4.refs_7_
  182.7 6.6 %all-to-all-done.6.refs_0_ = bf16[16,16,4224]{2,1,0:T(8,128)(2,1)S(1)} async-done(((bf16[16,16,4224]{2,1,0:T(8,128)(2,1)}), bf16[16,16,4224]{2,1,0:T(8,128)(2,1)S(1)}, u32[]{:S(2)}, u32[]{:S(2)}) %all-to-all-start.6) | async-done | bytes 2162720 | tf_op jit(solution)/shard_map/all_to_all | solution.py:531
  189.3 1.8 d_tokens.1
  192.5 4.5 %all-to-all-start.7 = ((bf16[16,2,16,2048]{3,2,1,0:T(8,128)(2,1)}), bf16[16,2,16,2048]{3,2,1,0:T(8,128)(2,1)}, u32[]{:S(2)}, u32[]{:S(2)}) async-start(bf16[16,2,16,2048]{3,2,1,0:T(8,128)(2,1)} %copy-done.3), calls=%async_computation.8 | async-start | bytes 4194304 | tf_op jit(solution)/shard_map/all_to_all | solution.py:531
  196.9 19.5 %all-gather.6.cloned.1.call-done = bf16[4864,256]{1,0:T(8,128)(2,1)} async-done(((bf16[608,256]{1,0:T(8,128)(2,1)}), bf16[4864,256]{1,0:T(8,128)(2,1)}) %all-gather.6.cloned.1.call-update) | async-done | bytes 2490384 | tf_op jit(solution)/shard_map/all_gather | solution.py:903
  218.1 3.5 %place_chunk.1 = (f32[171,2048]{1,0:T(8,128)}, f32[171,2048]{1,0:T(8,128)}, f32[171,2048]{1,0:T(8,128)}, f32[1,171,171]{2,1,0:T(8,128)S(1)}, f32[1,171,171]{2,1,...) custom-call(bf16[8,608,256]{2,1,0:T(8,128)(2,1)S(1)} %bitcast.299), custom_call_target="tpu_custom_call" | custom-call | bytes 7000520 | tf_op jit(solution)/shard_map/place_chunk/pallas_call | solution.py:588
  225.0 5.5 %all-to-all-done.7.both_hbm = bf16[16,2,16,2048]{3,2,1,0:T(8,128)(2,1)} async-done(((bf16[16,2,16,2048]{3,2,1,0:T(8,128)(2,1)}), bf16[16,2,16,2048]{3,2,1,0:T(8,128)(2,1)}, u32[]{:S(2)}, u32[]{:S(2)}) %all-to-all-start.7) | async-done | bytes 2097184 | tf_op jit(solution)/shard_map/all_to_all | solution.py:531
  230.6 2.8 %split_both.1 = (f32[16,16,2048]{2,1,0:T(8,128)}, bf16[16,16,2048]{2,1,0:T(8,128)(2,1)}) custom-call(bf16[16,2,16,2048]{3,2,1,0:T(8,128)(2,1)} %all-to-all-done.7.both_hbm, f32[171,2048]{1,0:T(8,128)} %get-tuple-element.84.after_ref), custom_call_target="tpu_custom_call" | custom-call | bytes 5242880 | tf_op jit(solution)/shard_map/split_both/pallas_call | solution.py:514
  (136 shorter events, 37.6 us)
Async XLA Ops:
  7.2 56.4 %copy-start = (bf16[384,2048]{1,0:T(8,128)(2,1)S(1)}, bf16[384,2048]{1,0:T(8,128)(2,1)}, u32[]{:S(2)}) copy-start(bf16[384,2048]{1,0:T(8,128)(2,1)} %param.37) | copy-start | bytes 4718596
  7.2 9.7 %copy-start.11 = (bf16[1,171,171]{2,1,0:T(8,128)(2,1)S(1)}, bf16[1,171,171]{2,1,0:T(8,128)(2,1)}, u32[]{:S(2)}) copy-start(bf16[1,171,171]{2,1,0:T(8,128)(2,1)} %refs_14_.1) | copy-start | bytes 175450
  7.2 9.7 %copy-start.9 = (bf16[1,171,171]{2,1,0:T(8,128)(2,1)S(1)}, bf16[1,171,171]{2,1,0:T(8,128)(2,1)}, u32[]{:S(2)}) copy-start(bf16[1,171,171]{2,1,0:T(8,128)(2,1)} %refs_13_.1) | copy-start | bytes 175450
  8.1 8.9 %copy-start.22 = (f32[171]{0:T(256)S(1)}, f32[171]{0:T(256)}, u32[]{:S(2)}) copy-start(f32[171]{0:T(256)} %param.32) | copy-start | bytes 2056
  11.2 19.4 %copy-start.6 = (bf16[2,128,171]{2,1,0:T(8,128)(2,1)}, bf16[2,128,171]{2,1,0:T(8,128)(2,1)S(1)}, u32[]{:S(2)}) copy-start(bf16[2,128,171]{2,1,0:T(8,128)(2,1)S(1)} %get-tuple-element.56.refs_3_.refs_9_) | copy-start | bytes 262660
  11.2 19.4 %copy-start.13 = (f32[256,1]{1,0:T(8,128)}, f32[256,1]{1,0:T(8,128)S(1)}, u32[]{:S(2)}) copy-start(f32[256,1]{1,0:T(8,128)S(1)} %get-tuple-element.75) | copy-start | bytes 3076
  11.2 5.7 %collective-permute-start = (bf16[2,3,171]{2,1,0:T(4,128)(2,1)S(1)}, bf16[2,3,171]{2,1,0:T(4,128)(2,1)S(1)}, u32[]{:S(2)}, u32[]{:S(2)}) collective-permute-start(bf16[2,3,171]{2,1,0:T(4,128)(2,1)S(1)} %get-tuple-element.57), channel_id=1, source_target_pairs={{0,16},{16,32},{32,48},{48,64},{64,80},{80,96},{96,112},{1,17},{17... | collective-permute-start | bytes 6164 | tf_op jit(solution)/shard_map/ppermute | solution.py:423
  19.8 10.8 %all-to-all-start = ((f32[8,2,2,171]{3,2,1,0:T(2,128)}), f32[8,2,2,171]{3,2,1,0:T(2,128)S(1)}, u32[]{:S(2)}, u32[]{:S(2)}) async-start(f32[8,2,2,171]{3,2,1,0:T(2,128)} %get-tuple-element.60), calls=%async_computation | async-start | bytes 65536 | tf_op jit(solution)/shard_map/all_to_all | solution.py:428
  31.7 25.3 %copy-start.16 = (f32[2048]{0:T(1024)S(1)}, f32[2048]{0:T(1024)}, u32[]{:S(2)}) copy-start(f32[2048]{0:T(1024)} %param.24) | copy-start | bytes 24580
  34.3 22.7 %all-to-all-start.1 = ((bf16[16,16,2048]{2,1,0:T(8,128)(2,1)}), bf16[16,16,2048]{2,1,0:T(8,128)(2,1)S(1)}, u32[]{:S(2)}, u32[]{:S(2)}) async-start(bf16[16,16,2048]{2,1,0:T(8,128)(2,1)} %bitcast.323), calls=%async_computation.1 | async-start | bytes 2097152 | tf_op jit(solution)/shard_map/all_to_all | solution.py:531
  59.1 19.3 %all-to-all-start.2 = ((bf16[16,16,2048]{2,1,0:T(8,128)(2,1)}), bf16[16,16,2048]{2,1,0:T(8,128)(2,1)}, u32[]{:S(2)}, u32[]{:S(2)}) async-start(bf16[16,16,2048]{2,1,0:T(8,128)(2,1)} %copy-done.4), calls=%async_computation.2 | async-start | bytes 2097152 | tf_op jit(solution)/shard_map/all_to_all | solution.py:531
  63.6 74.5 %reduce-scatter.2.cloned.1.call-start = ((), (), s32[]{:S(2)}) async-start(), calls=%async_computation.9 | async-start | bytes 5308416 | tf_op jit(solution)/shard_map/reduce_scatter | solution.py:801
  86.0 17.4 %all-to-all-start.3 = ((bf16[16,16,2048]{2,1,0:T(8,128)(2,1)}), bf16[16,16,2048]{2,1,0:T(8,128)(2,1)S(1)}, u32[]{:S(2)}, u32[]{:S(2)}) async-start(bf16[16,16,2048]{2,1,0:T(8,128)(2,1)} %get-tuple-element.63), calls=%async_computation.3 | async-start | bytes 2097152 | tf_op jit(solution)/shard_map/all_to_all | solution.py:531
  103.5 19.0 %copy-start.29 = (bf16[171,2048]{1,0:T(8,128)(2,1)S(1)}, bf16[171,2048]{1,0:T(8,128)(2,1)}, u32[]{:S(2)}) copy-start(bf16[171,2048]{1,0:T(8,128)(2,1)} %param.34) | copy-start | bytes 2101252
  105.5 18.0 %copy-start.5 = (f32[2,128,171]{2,1,0:T(8,128)S(1)}, f32[2,128,171]{2,1,0:T(8,128)}, u32[]{:S(2)}) copy-start(f32[2,128,171]{2,1,0:T(8,128)} %get-tuple-element.61.refs_1_) | copy-start | bytes 525316
  105.5 32.5 %copy-start.7 = (bf16[2,128,171]{2,1,0:T(8,128)(2,1)S(1)}, bf16[2,128,171]{2,1,0:T(8,128)(2,1)}, u32[]{:S(2)}) copy-start(bf16[2,128,171]{2,1,0:T(8,128)(2,1)} %copy-done.6) | copy-start | bytes 262660
  105.5 32.6 %copy-start.10 = (bf16[1,171,171]{2,1,0:T(8,128)(2,1)S(1)}, bf16[1,171,171]{2,1,0:T(8,128)(2,1)}, u32[]{:S(2)}) copy-start(bf16[1,171,171]{2,1,0:T(8,128)(2,1)} %refs_13_.1) | copy-start | bytes 175450
  105.5 32.6 %copy-start.12 = (bf16[1,171,171]{2,1,0:T(8,128)(2,1)S(1)}, bf16[1,171,171]{2,1,0:T(8,128)(2,1)}, u32[]{:S(2)}) copy-start(bf16[1,171,171]{2,1,0:T(8,128)(2,1)} %refs_14_.1) | copy-start | bytes 175450
  123.0 18.2 %copy-start.14 = (f32[256,1]{1,0:T(8,128)S(1)}, f32[256,1]{1,0:T(8,128)}, u32[]{:S(2)}) copy-start(f32[256,1]{1,0:T(8,128)} %copy-done.13) | copy-start | bytes 3076
  124.9 22.2 %copy-start.30 = (bf16[2048,171]{0,1:T(8,128)(2,1)S(1)}, bf16[2048,171]{0,1:T(8,128)(2,1)}, u32[]{:S(2)}) copy-start(bf16[2048,171]{0,1:T(8,128)(2,1)} %param.26) | copy-start | bytes 2101252
  124.9 13.1 %all-to-all-start.5 = ((f32[8,2,2,171]{3,2,1,0:T(2,128)}), f32[8,2,2,171]{3,2,1,0:T(2,128)S(1)}, u32[]{:S(2)}, u32[]{:S(2)}) async-start(f32[8,2,2,171]{3,2,1,0:T(2,128)} %get-tuple-element.71), calls=%async_computation.5 | async-start | bytes 65536 | tf_op jit(solution)/shard_map/all_to_all | solution.py:428
  133.2 38.4 %all-gather.4.cloned.1.call-start = ((), (), s32[]{:S(2)}) async-start(), calls=%async_computation.10 | async-start | bytes 5308416 | tf_op jit(solution)/shard_map/all_gather | solution.py:847
  142.0 5.0 %collective-permute-start.1 = (f32[2,3,171]{2,1,0:T(4,128)S(1)}, f32[2,3,171]{2,1,0:T(4,128)S(1)}, u32[]{:S(2)}, u32[]{:S(2)}) collective-permute-start(f32[2,3,171]{2,1,0:T(4,128)S(1)} %get-tuple-element.73), channel_id=1, source_target_pairs={{16,0},{32,16},{48,32},{64,48},{80,64},{96,80},{112,96},{17,1},{33... | collective-permute-start | bytes 12320 | tf_op jit(solution)/shard_map/ppermute | solution.py:423
  151.4 37.9 %all-to-all-start.6 = ((bf16[16,16,4224]{2,1,0:T(8,128)(2,1)}), bf16[16,16,4224]{2,1,0:T(8,128)(2,1)S(1)}, u32[]{:S(2)}, u32[]{:S(2)}) async-start(bf16[16,16,4224]{2,1,0:T(8,128)(2,1)} %fusion.1), calls=%async_computation.7 | async-start | bytes 4325376 | tf_op jit(solution)/shard_map/all_to_all | solution.py:531
  155.2 61.2 %all-gather.6.cloned.1.call-start = ((), (), s32[]{:S(2)}) async-start(), calls=%async_computation.11 | async-start | bytes 2801664 | tf_op jit(solution)/shard_map/all_gather | solution.py:903
  159.5 3.2 %collective-permute-start.2 = (bf16[592,1024]{1,0:T(8,128)(2,1)}, bf16[592,1024]{1,0:T(8,128)(2,1)}, u32[]{:S(2)}, u32[]{:S(2)}) collective-permute-start(bf16[592,1024]{1,0:T(8,128)(2,1)} %pad_maximum_fusion.1), channel_id=1, source_target_pairs={{0,16},{16,0},{32,48},{48,32},{64,80},{80,64},{96,112},{112,96},{1... | collective-permute-start | bytes 3637256 | tf_op jit(solution)/shard_map/ppermute | solution.py:553
  165.3 14.0 %collective-permute-start.5 = (bf16[592,256]{1,0:T(8,128)(2,1)}, bf16[592,256]{1,0:T(8,128)(2,1)S(1)}, u32[]{:S(2)}, u32[]{:S(2)}) collective-permute-start(bf16[592,256]{1,0:T(8,128)(2,1)} %get-tuple-element.179), channel_id=1, source_target_pairs={{0,64},{16,80},{32,96},{48,112},{64,0},{80,16},{96,32},{112,48},{1... | collective-permute-start | bytes 909320 | tf_op jit(solution)/shard_map/ppermute | solution.py:557
  166.5 15.0 %collective-permute-start.4 = (bf16[592,256]{1,0:T(8,128)(2,1)}, bf16[592,256]{1,0:T(8,128)(2,1)S(1)}, u32[]{:S(2)}, u32[]{:S(2)}) collective-permute-start(bf16[592,256]{1,0:T(8,128)(2,1)} %get-tuple-element.180), channel_id=1, source_target_pairs={{0,96},{16,112},{32,0},{48,16},{64,32},{80,48},{96,64},{112,80},{1... | collective-permute-start | bytes 909320 | tf_op jit(solution)/shard_map/ppermute | solution.py:557
  168.3 21.0 %copy-start.18 = (f32[2048]{0:T(1024)S(1)}, f32[2048]{0:T(1024)}, u32[]{:S(2)}) copy-start(f32[2048]{0:T(1024)} %param.23) | copy-start | bytes 24580
  168.3 14.4 %collective-permute-start.3 = (bf16[592,256]{1,0:T(8,128)(2,1)}, bf16[592,256]{1,0:T(8,128)(2,1)S(1)}, u32[]{:S(2)}, u32[]{:S(2)}) collective-permute-start(bf16[592,256]{1,0:T(8,128)(2,1)} %get-tuple-element.181), channel_id=1, source_target_pairs={{0,32},{16,48},{32,64},{48,80},{64,96},{80,112},{96,0},{112,16},{1... | collective-permute-start | bytes 909320 | tf_op jit(solution)/shard_map/ppermute | solution.py:557
  192.5 38.1 %all-to-all-start.7 = ((bf16[16,2,16,2048]{3,2,1,0:T(8,128)(2,1)}), bf16[16,2,16,2048]{3,2,1,0:T(8,128)(2,1)}, u32[]{:S(2)}, u32[]{:S(2)}) async-start(bf16[16,2,16,2048]{3,2,1,0:T(8,128)(2,1)} %copy-done.3), calls=%async_computation.8 | async-start | bytes 4194304 | tf_op jit(solution)/shard_map/all_to_all | solution.py:531
  221.6 11.7 %copy-start.1 = (bf16[384,2048]{1,0:T(8,128)(2,1)S(1)}, bf16[384,2048]{1,0:T(8,128)(2,1)}, u32[]{:S(2)}) copy-start(bf16[384,2048]{1,0:T(8,128)(2,1)} %param.37) | copy-start | bytes 4718596
  (20 other events, 87.2 us)
Sparse Core Ops, SparseCore 0:
  86.2 35.2 reduce-scatter.1
  140.9 30.6 all-gather.3
  192.6 23.7 all-gather.5

commit v4 on v3

--- a/solution.py
+++ b/solution.py
@@ -268,8 +268,15 @@
 
 
 class Late:
-    def __init__(self, array):
-        self.array = in_hbm(array)
+    def __init__(self, array, share=0):
+        self.array, self.share = in_hbm(array), share
+        self.held = pltpu.VMEM((share or array.shape[0],) + array.shape[1:], array.dtype)
+
+    def source(self, ref):
+        if not self.share:
+            return ref
+        at = pl.multiple_of(lax.axis_index("ch") * self.share, self.share)
+        return ref.at[pl.ds(at, self.share)]
 
 
 class Arriving:
@@ -291,12 +298,12 @@
     vmem = pl.BlockSpec(memory_space=pltpu.VMEM)
     scalar = pl.BlockSpec(memory_space=pltpu.SMEM)
     anywhere = pl.BlockSpec(memory_space=pl.ANY)
-    late = [isinstance(a, Late) for a in ins]
+    late = [a if isinstance(a, Late) else None for a in ins]
     ins = [a.array if isinstance(a, Late) else a for a in ins]
     moved = sum(a.size * a.dtype.itemsize for a in list(ins) + list(outs))
     count, skip = len(ins), len(after)
     in_specs = [scalar] * smem + [anywhere if l else vmem for l in late[smem:]] + [anywhere] * skip
-    held = [pltpu.VMEM(a.shape, a.dtype) for a, l in zip(ins, late) if l]
+    held = [l.held for l in late if l]
     ins = [*ins, *[in_hbm(a) for a in after]]
     out_specs = [vmem] * len(outs)
     outs, scratch = list(outs), list(scratch)
@@ -311,7 +318,8 @@
         if held:
             refs, arrived, sems = list(refs[: -len(held) - 1]), refs[-len(held) - 1 : -1], refs[-1]
             for n, i in enumerate([i for i in range(count) if late[i]]):
-                refs[i] = Arriving(pltpu.make_async_copy(refs[i], arrived[n], sems.at[n]), arrived[n])
+                source = late[i].source(refs[i])
+                refs[i] = Arriving(pltpu.make_async_copy(source, arrived[n], sems.at[n]), arrived[n])
         if passed is None:
             kernel(*refs[:count], *refs[count + skip :])
             for ref in refs[:count]:
@@ -344,16 +352,18 @@
     )(*ins)
 
 
-def front(tokens, gain, w_x, w_y, groups):
+def front(tokens, cotangent, gain, w_x, w_y, groups):
     total, width = tokens.shape
+    share = total // lax.axis_size("ch")
     chans = w_x.shape[0]
     rows = total // groups
     step = total // 4
 
-    def run(gain_ref, *refs):
-        sources, outs, held, kept, sems = refs[:3], refs[3:8], refs[8:10], refs[10:13], refs[13]
-        normed_out, scale_ref, conv_in_ref, edge_ref, gate_out = outs
-        tokens_ref, normed_ref, gate_ref = kept
+    def run(*refs):
+        gain_hbm, sources, outs, held, kept, sems = refs[0], refs[1:5], refs[5:12], refs[12:14], refs[14:18], refs[18]
+        normed_out, scale_ref, conv_in_ref, edge_ref, gate_out, tokens_share_ref, cot_share_ref = outs
+        gain_ref = Arriving(pltpu.make_async_copy(gain_hbm, kept[3], sems.at[12]), kept[3])
+        tokens_ref, normed_ref, gate_ref, _ = kept
         reads = []
         for n in range(4):
             part = pl.ds(n * step, step)
@@ -361,9 +371,12 @@
             reads[-1].start()
         w_x_ref, w_y_ref = [
             Arriving(pltpu.make_async_copy(source, ref, sems.at[4 + n]), ref)
-            for n, (source, ref) in enumerate(zip(sources[1:], held))
+            for n, (source, ref) in enumerate(zip(sources[1:3], held))
         ]
-        stores = []
+        mine = pl.ds(pl.multiple_of(lax.axis_index("ch") * share, share), share)
+        cot_share = pltpu.make_async_copy(sources[3].at[mine], cot_share_ref, sems.at[11])
+        cot_share.start()
+        stores = [cot_share]
         for n in range(4):
             reads[n].wait()
             for at in range(n * step, (n + 1) * step, 32):
@@ -375,6 +388,7 @@
             part = pl.ds(n * step, step)
             stores.append(pltpu.make_async_copy(normed_ref.at[part], normed_out.at[part], sems.at[6 + n]))
             stores[-1].start()
+        tokens_share_ref[...] = tokens_ref[mine, :]
         for g in range(groups):
             part = normed_ref[g * rows : (g + 1) * rows, :]
             gate_ref[g] = dot(part, w_y_ref[...], ((1,), (1,)))
@@ -393,14 +407,16 @@
     return pl.pallas_call(
         run,
         name="front",
-        in_specs=[vmem] + [anywhere] * 3,
-        out_specs=[anywhere, vmem, vmem, vmem, anywhere],
+        in_specs=[anywhere] * 5,
+        out_specs=[anywhere, vmem, vmem, vmem, anywhere, vmem, vmem],
         out_shape=[
             pltpu.HBM((total, width), BF16),
             sds((total, 1)),
             sds((groups, rows, chans), BF16),
             sds((groups, TAPS - 1, chans), BF16),
             pltpu.HBM((groups, rows, chans), F32),
+            sds((share, width), BF16),
+            sds((share, width), BF16),
         ],
         scratch_shapes=[
             pltpu.VMEM(w_x.shape, BF16),
@@ -408,13 +424,14 @@
             pltpu.VMEM((total, width), BF16),
             pltpu.VMEM((total, width), BF16),
             pltpu.VMEM((groups, rows, chans), F32),
-            pltpu.SemaphoreType.DMA((11,)),
+            pltpu.VMEM((1, width), F32),
+            pltpu.SemaphoreType.DMA((13,)),
         ],
         cost_estimate=pl.CostEstimate(
             flops=4 * total * chans * width, bytes_accessed=4 * total * width, transcendentals=0
         ),
         compiler_params=pltpu.CompilerParams(vmem_limit_bytes=VMEM_LIMIT),
-    )(gain[None], in_hbm(tokens), in_hbm(w_x), in_hbm(w_y))
+    )(in_hbm(gain[None]), in_hbm(tokens), in_hbm(w_x), in_hbm(w_y), in_hbm(cotangent))
 
 
 def shifted(block, axis, distance):
@@ -488,45 +505,6 @@
         both_ref[j, 1] = layer_out
 
 
-def split_both(both, after):
-    owners, _, share, width = both.shape
-    parts = 8
-    step = owners // parts
-
-    def run(both_hbm, after_ref, d_tokens_hbm, layer_hbm, held, wide, sems):
-        reads, stores = [], []
-        for n in range(parts):
-            part = pl.ds(n * step, step)
-            reads.append(pltpu.make_async_copy(both_hbm.at[part], held.at[part], sems.at[n]))
-            reads[-1].start()
-        for n in range(parts):
-            part = pl.ds(n * step, step)
-            reads[n].wait()
-            stores.append(pltpu.make_async_copy(held.at[part, 1], layer_hbm.at[part], sems.at[parts + n]))
-            stores[-1].start()
-            wide[n * step : (n + 1) * step] = held[n * step : (n + 1) * step, 0].astype(F32)
-            stores.append(pltpu.make_async_copy(wide.at[part], d_tokens_hbm.at[part], sems.at[2 * parts + n]))
-            stores[-1].start()
-        for store in stores:
-            store.wait()
-
-    anywhere = pl.BlockSpec(memory_space=pl.ANY)
-    return pl.pallas_call(
-        run,
-        name="split_both",
-        in_specs=[anywhere] * 2,
-        out_specs=[anywhere] * 2,
-        out_shape=[pltpu.HBM((owners, share, width), F32), pltpu.HBM((owners, share, width), BF16)],
-        scratch_shapes=[
-            pltpu.VMEM(both.shape, BF16),
-            pltpu.VMEM((owners, share, width), F32),
-            pltpu.SemaphoreType.DMA((3 * parts,)),
-        ],
-        cost_estimate=pl.CostEstimate(flops=0, bytes_accessed=5 * both.size, transcendentals=0),
-        compiler_params=pltpu.CompilerParams(vmem_limit_bytes=VMEM_LIMIT),
-    )(in_hbm(both), in_hbm(after))
-
-
 def exchange(pieces):
     return lax.all_to_all(pieces, "ch", 0, 0)
 
@@ -576,108 +554,132 @@
     return [piece(0)] + [shift_z(piece(hops), hops) for hops in (1, 3, 2)]
 
 
-def assemble(kernel, name, chunks, outs, specs, after):
-    def out_spec(block, dim):
-        return pl.BlockSpec(
-            block, lambda i: tuple(i % 2 * 4 + i // 2 if d == dim else 0 for d in range(len(block)))
-        )
-
-    def run(chunks_ref, *refs):
-        kernel(chunks_ref[0], *refs[len(after) :])
-
+def finish(both, chunks, chans):
+    owners, _, share, width = both.shape
+    count = chunks.shape[0]
+    wide = (chunks.shape[1] - SMALL_ROWS - GAIN_ROWS) // 3
+    step = owners // 4
+    gain_width = width // owners
+
+    def run(both_ref, chunks_hbm, *refs):
+        outs, kept, chunk_ref, sems = refs[:14], refs[14:27], refs[27], refs[28]
+        d_tokens_hbm, layer_hbm = outs[:2]
+        d_tokens_ref, y_ref, out_ref, x_ref, gate_a_ref, gate_x_ref, conv_w_ref, *rows_refs = kept
+        *rows_refs, gain_one_ref, gain_two_ref = rows_refs
+        reads, stores = [], []
+
+        def store(source, target):
+            stores.append(pltpu.make_async_copy(source, target, sems.at[count + len(stores)]))
+            stores[-1].start()
+
+        for i in range(count):
+            reads.append(pltpu.make_async_copy(chunks_hbm.at[i], chunk_ref.at[i], sems.at[i]))
+            reads[-1].start()
+        store(both_ref.at[:, 1], layer_hbm)
+        for n in range(4):
+            part = slice(n * step, (n + 1) * step)
+            d_tokens_ref[part] = both_ref[part, 0].astype(F32)
+            store(d_tokens_ref.at[pl.ds(n * step, step)], d_tokens_hbm.at[pl.ds(n * step, step)])
+        gains = jnp.zeros((8, LANES), F32)
+        for i in range(count):
+            chunk = i % 2 * 4 + i // 2
+            lanes = pl.ds(chunk * LANES, LANES)
+            reads[i].wait()
+            for n, (ref, hbm) in enumerate(zip((y_ref, out_ref, x_ref), outs[2:5])):
+                ref[:, chunk * LANES : (chunk + 1) * LANES] = chunk_ref[i, n * wide : n * wide + chans, :].astype(F32)
+                store(ref.at[:, lanes], hbm.at[:, lanes])
+            small = chunk_ref[i, 3 * wide :, :].astype(F32)
+            for n, ref in enumerate((gate_a_ref, gate_x_ref)):
+                for r in range(min(GATE_ROWS, chans - chunk * GATE_ROWS)):
+                    ref[chunk * GATE_ROWS + r] = small[n * GATE_ROWS + r : n * GATE_ROWS + r + 1, :chans]
+            total = small[2 * GATE_ROWS : 2 * GATE_ROWS + 1, :chans]
+            if chunk < 4:
+                rows_refs[chunk][...] = total
+            else:
+                conv_w_ref[chunk - 4 : chunk - 3, :] = total
+            gains = gains + small[SMALL_ROWS : SMALL_ROWS + 8]
+        gain_one_ref[...] = gains[0:1, :gain_width]
+        gain_two_ref[...] = gains[1:2, :gain_width]
+        for source, target in zip(kept[4:], outs[5:]):
+            store(source, target)
+        for copy in stores:
+            copy.wait()
+
+    weight = ((chans, width), F32)
+    gate = ((chans, 1, chans), F32)
+    row = ((1, chans), F32)
+    gain = ((1, gain_width), F32)
+    blocks = ((owners, share, width), F32)
+    small = [gate, gate, ((TAPS, chans), F32), row, row, row, row, gain, gain]
+    anywhere = pl.BlockSpec(memory_space=pl.ANY)
     return pl.pallas_call(
         run,
-        name=name,
-        grid=(chunks.shape[0],),
-        in_specs=[pl.BlockSpec((1,) + chunks.shape[1:], lambda i: (i, 0, 0))]
-        + [pl.BlockSpec(memory_space=pl.ANY)] * len(after),
-        out_specs=[out_spec(*spec) for spec in specs],
-        out_shape=outs,
+        name="finish",
+        in_specs=[pl.BlockSpec(memory_space=pltpu.VMEM), anywhere],
+        out_specs=[anywhere] * 14,
+        out_shape=[pltpu.HBM(*out) for out in (blocks, (blocks[0], BF16), weight, weight, weight, *small)],
+        scratch_shapes=[pltpu.VMEM(*out) for out in (blocks, weight, weight, weight, *small)]
+        + [pltpu.VMEM(chunks.shape, BF16), pltpu.SemaphoreType.DMA((count + 5 + 3 * count + len(small),))],
         cost_estimate=pl.CostEstimate(
-            flops=0, bytes_accessed=2 * chunks.size + sum(4 * math.prod(o.shape) for o in outs), transcendentals=0
+            flops=0, bytes_accessed=6 * both.size + 12 * width * chans, transcendentals=0
         ),
-        compiler_params=pltpu.CompilerParams(vmem_limit_bytes=VMEM_LIMIT),
-    )(chunks, *[in_hbm(a) for a in after])
-
-
-def place_chunk(piece, y_ref, out_ref, x_ref, gate_a_ref, gate_x_ref, rows_ref, gains_ref):
-    chans = x_ref.shape[0]
-    piece = piece.astype(F32)
-    size = (piece.shape[0] - SMALL_ROWS - GAIN_ROWS) // 3
-    y_ref[...] = piece[:chans]
-    out_ref[...] = piece[size : size + chans]
-    x_ref[...] = piece[2 * size : 2 * size + chans]
-    at = 3 * size
-    gate_a_ref[0] = piece[at : at + GATE_ROWS, :chans]
-    gate_x_ref[0] = piece[at + GATE_ROWS : at + 2 * GATE_ROWS, :chans]
-    rows_ref[0] = piece[at + 2 * GATE_ROWS : at + 2 * GATE_ROWS + 8]
-    gains = piece[at + SMALL_ROWS : at + SMALL_ROWS + 8]
-
-    @pl.when(pl.program_id(0) == 0)
-    def _():
-        gains_ref[...] = gains
-
-    @pl.when(pl.program_id(0) > 0)
-    def _():
-        gains_ref[...] += gains
-
-
-def mlp_back(normed, d_hidden, w_one, w_two, cotangent, owners):
+        compiler_params=pltpu.CompilerParams(vmem_limit_bytes=2 * VMEM_LIMIT),
+    )(both, in_hbm(chunks))
+
+
+def mlp_back(normed, w_one, w_two, w_three, cotangent, owners):
     rows, width = normed.shape
     units = w_one.shape[1]
     share = rows // owners
     steps = range(0, width, WIDE)
 
-    def run(*refs):
-        ins, (parts_out, hidden_out, grads_out) = refs[:5], refs[5:8]
-        held, parts, kept_hidden, grads, sems = refs[8:13], refs[13], refs[14], refs[15], refs[16]
-        normed, one, two, d_hidden, cot = [
-            Arriving(pltpu.make_async_copy(source, ref, sems.at[n]), ref) for n, (source, ref) in enumerate(zip(ins, held))
-        ]
+    def run(normed_ref, one, two, three, cot, parts, out_hbm, grads_hbm, out_parts, grads, sems):
         stores = []
 
         def store(source, target):
-            stores.append(pltpu.make_async_copy(source, target, sems.at[len(ins) + len(stores)]))
+            stores.append(pltpu.make_async_copy(source, target, sems.at[len(stores)]))
             stores[-1].start()
 
-        value, slope = gelu_parts(dot(normed[...], one[...], ((1,), (0,))))
-        up = dot(normed[...], two[...], ((1,), (0,)))
+        value, slope = gelu_parts(dot(normed_ref[...], one[...], ((1,), (0,))))
+        up = dot(normed_ref[...], two[...], ((1,), (0,)))
         hidden = (value * up).astype(BF16)
-        kept_hidden[...] = hidden
-        store(kept_hidden, hidden_out)
-        d_gate = (d_hidden[...] * up * slope).astype(BF16)
-        d_up = (d_hidden[...] * value).astype(BF16)
+        d_hidden = dot(cot[...], three[...], ((1,), (1,)))
+        d_gate = (d_hidden * up * slope).astype(BF16)
+        d_up = (d_hidden * value).astype(BF16)
+        for at in steps:
+            cols = slice(at, at + WIDE)
+            out = dot(hidden, three[:, cols], ((1,), (0,)))
+            out_parts[:, :, cols] = out.astype(BF16).reshape(owners, share, WIDE)
+        store(out_parts, out_hbm)
+        for at in steps:
+            cols = slice(at, at + WIDE)
+            grads[cols, :units] = dot(normed_ref[:, cols], d_gate, ((0,), (0,))).astype(BF16)
+            grads[cols, units : 2 * units] = dot(normed_ref[:, cols], d_up, ((0,), (0,))).astype(BF16)
+            grads[cols, 2 * units :] = dot(cot[:, cols], hidden, ((0,), (0,))).astype(BF16)
+            store(grads.at[cols], grads_hbm.at[cols])
         for at in steps:
             cols = slice(at, at + WIDE)
             back = dot(d_gate, one[cols, :], ((1,), (1,))) + dot(d_up, two[cols, :], ((1,), (1,)))
             parts[:, :, cols] = back.astype(BF16).reshape(owners, share, WIDE)
-        store(parts, parts_out)
-        for at in steps:
-            cols = slice(at, at + WIDE)
-            grads[cols, :units] = dot(normed[:, cols], d_gate, ((0,), (0,))).astype(BF16)
-            grads[cols, units : 2 * units] = dot(normed[:, cols], d_up, ((0,), (0,))).astype(BF16)
-            grads[cols, 2 * units :] = dot(cot[:, cols], hidden, ((0,), (0,))).astype(BF16)
-            store(grads.at[cols], grads_out.at[cols])
         for copy in stores:
             copy.wait()
 
-    ins = [in_hbm(a) for a in (normed, w_one, w_two, d_hidden, cotangent)]
-    outs = [((owners, share, width), BF16), ((rows, units), BF16), ((width, 3 * units), BF16)]
+    parts = ((owners, share, width), BF16)
+    grads = ((width, 3 * units), BF16)
+    vmem = pl.BlockSpec(memory_space=pltpu.VMEM)
     anywhere = pl.BlockSpec(memory_space=pl.ANY)
     return pl.pallas_call(
         run,
         name="mlp",
-        in_specs=[anywhere] * len(ins),
-        out_specs=[anywhere] * len(outs),
-        out_shape=[pltpu.HBM(*out) for out in outs],
-        scratch_shapes=[pltpu.VMEM(a.shape, a.dtype) for a in ins]
-        + [pltpu.VMEM(*out) for out in outs]
-        + [pltpu.SemaphoreType.DMA((len(ins) + 2 + len(steps),))],
+        in_specs=[vmem] * 5,
+        out_specs=[vmem, anywhere, anywhere],
+        out_shape=[sds(*parts), pltpu.HBM(*parts), pltpu.HBM(*grads)],
+        scratch_shapes=[pltpu.VMEM(*parts), pltpu.VMEM(*grads), pltpu.SemaphoreType.DMA((len(steps) + 1,))],
         cost_estimate=pl.CostEstimate(
-            flops=14 * rows * width * units, bytes_accessed=14 * width * units, transcendentals=0
+            flops=18 * rows * width * units, bytes_accessed=14 * width * units, transcendentals=0
         ),
         compiler_params=pltpu.CompilerParams(vmem_limit_bytes=2 * VMEM_LIMIT),
-    )(*ins)
+    )(normed, w_one, w_two, w_three, cotangent)
 
 
 def place_mlp(bundle, units):
@@ -736,13 +738,13 @@
     share_width = width // ch_count
     start = (seq_index * rows).astype(jnp.int32)[None]
     grouped = lambda a: a.reshape(groups, rows, a.shape[-1])
-    mine = lambda a: lax.dynamic_slice_in_dim(a, ch_index * share_rows, share_rows, 0)
 
     tokens = tokens.reshape(total_rows, width)
     cotangent = cotangent.reshape(total_rows, width)
     tokens_f = tokens.astype(F32)
-    tokens_share = mine(tokens)
-    normed_one, scale_one, conv_input, edge, gate_pre = front(tokens, gain_one, w_x.T, w_y.T, groups)
+    normed_one, scale_one, conv_input, edge, gate_pre, tokens_share, cotangent_share = front(
+        tokens, cotangent, gain_one, w_x.T, w_y.T, groups
+    )
     edge = shifted(edge, "seq", 1)
 
     decay = (-8.0 * jax.nn.softplus(-lam))[None]
@@ -781,19 +783,17 @@
         mid_kernel,
         "resid_mid_norm",
         [share, to_all],
-        [exchange(by_owner(dot(mixed_in, w_out, ((1,), (0,))))), Late(tokens_share), gain_two[None]],
+        [exchange(by_owner(dot(mixed_in, w_out, ((1,), (0,))))), tokens_share, gain_two[None]],
         waits=20,
     )
     normed_two = exchange(normed_two).reshape(total_rows, width)
 
-    d_hidden = dot(cotangent, w_three, ((1,), (1,)))
-    two_parts, mlp_hidden, g_mlp = mlp_back(normed_two, d_hidden, w_one, w_two, cotangent, ch_count)
-    partial_out = lax.optimization_barrier(by_owner(dot(mlp_hidden, w_three, ((1,), (0,)))))
+    two_parts, partial_out, g_mlp = mlp_back(normed_two, w_one, w_two, w_three, cotangent, ch_count)
     d_mid, gain_two_part, d_mix = run_kernel(
         mid_back_kernel,
         "d_mid",
         [share, sds((1, width)), to_all],
-        [exchange(two_parts), Late(resid_share), Late(mine(cotangent)), gain_two[None]],
+        [exchange(two_parts), resid_share, cotangent_share, gain_two[None]],
         after=[g_mlp, partial_out],
         waits=20,
     )
@@ -809,6 +809,8 @@
         waits=20,
     )
     beyond = carried_in(carry_back, True)
+    d_gate_pre = d_gate_pre.reshape(total_rows, chans)
+    partial_y = lax.optimization_barrier(dot(d_gate_pre, w_y, ((1,), (1,))))
     d_conv_head, d_input, small, g_mlp = run_kernel(
         gates_back_kernel,
         "gates_back",
@@ -841,6 +843,7 @@
         ],
         flops=4 * flops,
         smem=3,
+        after=[partial_y],
         passed=g_mlp,
         waits=10,
     )
@@ -863,9 +866,7 @@
         late.append(total)
     late = jnp.pad(jnp.stack(late, axis=1), ((0, 0), (rows - TAPS + 1, 0), (0, 0)))
     d_input = (d_input + late).astype(BF16).reshape(total_rows, chans)
-    d_gate_pre = d_gate_pre.reshape(total_rows, chans)
-
-    partial_one = dot(d_input, w_x, ((1,), (1,))) + dot(d_gate_pre, w_y, ((1,), (1,)))
+    partial_one = dot(d_input, w_x, ((1,), (1,))) + partial_y
     gain_one_part = jnp.sum(partial_one * (tokens_f * scale_one), axis=0, keepdims=True)
     gain_parts = jnp.concatenate([gain_one_part, gain_two_part], axis=0)
     back_pieces = exchange(with_gains([by_owner(partial_one), partial_out], gain_parts))
@@ -897,48 +898,36 @@
         after=[g_w_one],
         waits=30,
     )
-    g_w_y, g_w_out, g_w_x, g_gate_a, g_gate_x, g_rows, gains = assemble(
-        place_chunk,
-        "place_chunk",
-        lax.all_gather(chunk, "seq"),
-        [
-            sds((chans, width)),
-            sds((chans, width)),
-            sds((chans, width)),
-            sds((1, chans, chans)),
-            sds((1, chans, chans)),
-            sds((8, 8, LANES)),
-            sds((8, LANES)),
-        ],
-        [
-            ((chans, LANES), 1),
-            ((chans, LANES), 1),
-            ((chans, LANES), 1),
-            ((1, GATE_ROWS, chans), 1),
-            ((1, GATE_ROWS, chans), 1),
-            ((1, 8, LANES), 0),
-            ((8, LANES), None),
-        ],
-        [],
-    )
-    g_rows = g_rows[:, 0, :chans]
-    d_tokens, layer_out = split_both(exchange(both), g_w_y)
-    d_tokens = d_tokens.reshape(groups, rows, width)
-    layer_out = layer_out.reshape(groups, rows, width)
+    (
+        d_tokens,
+        layer_out,
+        g_w_y,
+        g_w_out,
+        g_w_x,
+        g_gate_a,
+        g_gate_x,
+        g_conv_w,
+        g_bias_a,
+        g_bias_x,
+        g_lam,
+        g_conv_b,
+        g_gain_one,
+        g_gain_two,
+    ) = finish(exchange(both), lax.all_gather(chunk, "seq"), chans)
     return (
-        layer_out,
-        d_tokens,
-        gains[0, :share_width],
-        gains[1, :share_width],
+        layer_out.reshape(groups, rows, width),
+        d_tokens.reshape(groups, rows, width),
+        g_gain_one[0],
+        g_gain_two[0],
         g_w_y.T,
         g_w_x.T,
-        g_rows[4:],
-        g_rows[3],
-        g_gate_a,
-        g_gate_x,
-        g_rows[0],
-        g_rows[1],
-        g_rows[2],
+        g_conv_w,
+        g_conv_b[0],
+        g_gate_a.transpose(1, 0, 2),
+        g_gate_x.transpose(1, 0, 2),
+        g_bias_a[0],
+        g_bias_x[0],
+        g_lam[0],
         g_w_out,
         g_w_one,
         g_w_two,

time: 241 us -> 229 us (0.950)
  blocking collectives: 17 us -> 89.9 us
  waiting for transfers between devices: 88.4 us -> 36.8 us
  starting transfers between devices: 48.3 us -> 32.5 us
  local copies, waits for them, and re-layouts: 13.1 us -> 4.35 us
  Pallas kernels: 36 us -> 31.3 us
  matrix products: 14.7 us -> 11.3 us
    all_to_all x1 -> x4, blocking collectives: 17 us -> 89.9 us  [exchange(): return lax.all_to_all(pieces, 'ch', 0, 0)]
    all_to_all x5 -> x2, waiting for transfers between devices: 49.4 us -> 19.1 us  [exchange(): return lax.all_to_all(pieces, 'ch', 0, 0)]
    all_gather x1, waiting for transfers between devices: 19.5 us -> 0.01 us  [body(): lax.all_gather(chunk, 'seq')]
    all_to_all x5 -> x2, starting transfers between devices: 23.2 us -> 7.51 us  [exchange(): return lax.all_to_all(pieces, 'ch', 0, 0)]
    unnamed x75 -> x58, local copies, waits for them, and re-layouts: 8.38 us -> 4.29 us
    pallas_call x4 -> x3, Pallas kernels: 17.1 us -> 13.3 us  [the longest x1 5.13 us: mlp_back(): pl.pallas_call(run, name='mlp', in_specs=[vmem] * 5, out_specs=[vmem, any...]
    dot_general x12 -> x10, matrix products: 14.7 us -> 11.3 us  [dot(): lax.dot_general(left, right, (contract, ((), ())), preferred_element_type...]
    dynamic_slice x2 -> x0, local copies, waits for them, and re-layouts: 2.95 us -> none  [body(): lax.dynamic_slice_in_dim(a, ch_index * share_rows, share_rows, 0)]
  transfers between devices with their start and end apart: 16 -> 13, of which waited for: 14 -> 10; matrix products, arithmetic and copies ran while one was open for 11% -> 8% of each run, Pallas kernels for 6% -> 5%
where the time goes in v4:
time: 229 us; the launch traced here: 228 us
  blocking collectives  89.9 us (39%)
  waiting for transfers between devices  36.8 us (16%)
  starting transfers between devices  32.5 us (14%)
  Pallas kernels  31.3 us (14%)
  between operations  14.4 us (6%)
  matrix products  11.3 us (5%)
  other arithmetic  7.96 us (3%)
  local copies, waits for them, and re-layouts  4.35 us (2%)
    all_to_all x4, blocking collectives, exchange(): return lax.all_to_all(pieces, 'ch', 0, 0)  89.9 us
    all_to_all x2, waiting for transfers between devices, exchange(): return lax.all_to_all(pieces, 'ch', 0, 0)  19.1 us
    all_to_all x2, starting transfers between devices, carried_in(): pieces = lax.all_to_all(value, 'seq', 0, 0)  14.4 us
    dot_general x10, matrix products, dot(): lax.dot_general(left, right, (contract, ((), ())), preferred_element_type...  11.3 us
    pallas_call x6, Pallas kernels, run_kernel(): pl.pallas_call(run, name=name, out_shape=outs, in_specs=in_specs, out_spe...  10.3 us
    pallas_call x1, Pallas kernels, place_mlp(): pl.pallas_call(run, name='place_mlp', grid=(width // LANES,), in_specs=[p...  7.68 us
    ppermute x2, starting transfers between devices, shifted(): return lax.ppermute(block, axis, route)  7.58 us
    all_to_all x2, starting transfers between devices, exchange(): return lax.all_to_all(pieces, 'ch', 0, 0)  7.51 us
  transfers between devices with their start and end apart: 13, of which 10 were waited for; matrix products, arithmetic and copies ran while one was open for 8% of the time, Pallas kernels for 5%

profile of v4, /device:TPU:1, one launch (start us, length us, event | category | flops | bytes accessed | tf_op | source)
XLA Modules:
  0.0 228.4 jit_solution(18236866795550545916)
XLA Ops:
  7.3 3.3 %front.1 = (bf16[256,2048]{1,0:T(8,128)(2,1)}, f32[256,1]{1,0:T(8,128)S(1)}, bf16[2,128,171]{2,1,0:T(8,128)(2,1)S(1)}, bf16[2,3,171]{2,1,0:T(4,128)(2,1)S(1)}, f...) custom-call(f32[1,2048]{1,0:T(1,128)} %bitcast.297, ...), custom_call_target="tpu_custom_call" | custom-call | flops 358612992 | bytes 2097152 | tf_op jit(solution)/shard_map/front/pallas_call | solution.py:407
  10.6 4.9 %collective-permute-start = (bf16[2,3,171]{2,1,0:T(4,128)(2,1)S(1)}, bf16[2,3,171]{2,1,0:T(4,128)(2,1)S(1)}, u32[]{:S(2)}, u32[]{:S(2)}) collective-permute-start(bf16[2,3,171]{2,1,0:T(4,128)(2,1)S(1)} %get-tuple-element.64), channel_id=1, source_target_pairs={{0,16},{16,32},{32,48},{48,64},{64,80},{80,96},{96,112},{1,17},{17... | collective-permute-start | bytes 6164 | tf_op jit(solution)/shard_map/ppermute | solution.py:440
  16.4 2.8 %conv_gates_scan.1 = (f32[2,128,171]{2,1,0:T(8,128)S(1)}, f32[2,128,171]{2,1,0:T(8,128)S(1)}, f32[2,128,171]{2,1,0:T(8,128)S(1)}, f32[8,2,2,171]{3,2,1,0:T(2,128)}) custom-call(s32[1]{0:T(128)} %bitcast.refs_0_, s32[8]{0:T(128)S(1)} %copy-done.19, s32[3]{0:T(128)S(1)} %copy-done.18, bf16[2,128,171]{2,1,0:T(8,128)(2,1)S(1)} %get-tuple-element.63.refs_3_.refs_9_, ...), custom_call_target="tpu_custom_call" | custom-call | flops 29942784 | bytes 759288 | tf_op jit(solution)/shard_map/conv_gates_scan/pallas_call | solution.py:343
  19.2 6.1 %all-to-all-start = ((f32[8,2,2,171]{3,2,1,0:T(2,128)}), f32[8,2,2,171]{3,2,1,0:T(2,128)S(1)}, u32[]{:S(2)}, u32[]{:S(2)}) async-start(f32[8,2,2,171]{3,2,1,0:T(2,128)} %get-tuple-element.67), calls=%async_computation | async-start | bytes 65536 | tf_op jit(solution)/shard_map/all_to_all | solution.py:445
  25.2 4.7 %all-to-all-done = f32[8,2,2,171]{3,2,1,0:T(2,128)S(1)} async-done(((f32[8,2,2,171]{3,2,1,0:T(2,128)}), f32[8,2,2,171]{3,2,1,0:T(2,128)S(1)}, u32[]{:S(2)}, u32[]{:S(2)}) %all-to-all-start) | async-done | bytes 21920 | tf_op jit(solution)/shard_map/all_to_all | solution.py:445
  31.5 23.0 %all_to_all.40.refs_0_ = bf16[16,16,2048]{2,1,0:T(8,128)(2,1)S(1)} all-to-all(bf16[16,16,2048]{2,1,0:T(8,128)(2,1)S(1)} %bitcast.315), channel_id=1, replica_groups=mesh['seq'=8,'ch'=16] {'ch'}, dimensions={0} | all-to-all | bytes 2097152 | tf_op jit(solution)/shard_map/all_to_all | solution.py:509
  54.9 18.4 %all_to_all.41 = bf16[16,16,2048]{2,1,0:T(8,128)(2,1)S(1)} all-to-all(bf16[16,16,2048]{2,1,0:T(8,128)(2,1)S(1)} %get-tuple-element.70), channel_id=1, replica_groups=mesh['seq'=8,'ch'=16] {'ch'}, dimensions={0} | all-to-all | bytes 2097152 | tf_op jit(solution)/shard_map/all_to_all | solution.py:509
  73.3 5.1 %mlp.1 = (bf16[16,16,2048]{2,1,0:T(8,128)(2,1)S(1)}, bf16[16,16,2048]{2,1,0:T(8,128)(2,1)}, bf16[2048,1152]{1,0:T(8,128)(2,1)}) custom-call(bf16[256,2048]{1,0:T(8,128)(2,1)S(1)} %bitcast.293, bf16[2048,384]{1,0:T(8,128)(2,1)S(1)} %copy-done.20, bf16[2048,384]{1,0:T(8,128)(2,1)S(1)} %copy-done.21, bf16[384,2048]{1,0:T(8,128)(2,1)S(1)} %copy-done.22, ...), custom_call_target="tpu_custom_call" | custom-call | flops 3623878656 | bytes 11010048 | tf_op jit(solution)/shard_map/mlp/pallas_call | solution.py:671
  78.4 16.6 %all_to_all.42.refs_0_ = bf16[16,16,2048]{2,1,0:T(8,128)(2,1)S(1)} all-to-all(bf16[16,16,2048]{2,1,0:T(8,128)(2,1)S(1)} %get-tuple-element.71), channel_id=1, replica_groups=mesh['seq'=8,'ch'=16] {'ch'}, dimensions={0} | all-to-all | bytes 2097152 | tf_op jit(solution)/shard_map/all_to_all | solution.py:509
  96.9 3.8 %all-to-all-start.4 = ((bf16[16,16,2048]{2,1,0:T(8,128)(2,1)}), bf16[16,16,2048]{2,1,0:T(8,128)(2,1)S(1)}, u32[]{:S(2)}, u32[]{:S(2)}) async-start(bf16[16,16,2048]{2,1,0:T(8,128)(2,1)} %get-tuple-element.76), calls=%async_computation.4 | async-start | bytes 2097152 | tf_op jit(solution)/shard_map/all_to_all | solution.py:509
  100.7 13.5 %all-to-all-done.4 = bf16[16,16,2048]{2,1,0:T(8,128)(2,1)S(1)} async-done(((bf16[16,16,2048]{2,1,0:T(8,128)(2,1)}), bf16[16,16,2048]{2,1,0:T(8,128)(2,1)S(1)}, u32[]{:S(2)}, u32[]{:S(2)}) %all-to-all-start.4) | async-done | bytes 1048608 | tf_op jit(solution)/shard_map/all_to_all | solution.py:509
  115.2 1.5 adjoint_scan.1
  116.7 8.4 %all-to-all-start.5 = ((f32[8,2,2,171]{3,2,1,0:T(2,128)}), f32[8,2,2,171]{3,2,1,0:T(2,128)S(1)}, u32[]{:S(2)}, u32[]{:S(2)}) async-start(f32[8,2,2,171]{3,2,1,0:T(2,128)} %get-tuple-element.80), calls=%async_computation.5 | async-start | bytes 65536 | tf_op jit(solution)/shard_map/all_to_all | solution.py:445
  125.1 2.9 %fusion.105.refs_19_ = f32[256,2048]{1,0:T(8,128)} fusion(bf16[256,171]{1,0:T(8,128)(2,1)S(1)} %bitcast.294, bf16[2048,171]{0,1:T(8,128)(2,1)} %param.25), kind=kOutput, calls=%fused_computation.192 | convolution fusion | flops 179306496 | bytes 2885120 | tf_op jit(solution)/shard_map/dot_general | solution.py:25
  127.9 1.9 all-to-all-done.5
  129.8 2.7 %gates_back.1 = (f32[2,3,171]{2,1,0:T(4,128)S(1)}, f32[2,128,171]{2,1,0:T(8,128)S(1)}, f32[64,2048]{1,0:T(8,128)S(1)}, bf16[256,1152]{1,0:T(8,128)(2,1)}) custom-call(s32[1]{0:T(128)} %bitcast.refs_0_, s32[8]{0:T(128)S(1)} %copy-done.19, s32[3]{0:T(128)S(1)} %copy-done.18, f32[2,128,171]{2,1,0:T(8,128)S(1)} %get-tuple-element.78.refs_3_, ...), custom_call_target="tpu_custom_call" | custom-call | flops 59885568 | bytes 37619420 | tf_op jit(solution)/shard_map/gates_back/pallas_call | solution.py:343
  133.8 2.6 %collective-permute-start.1 = (f32[2,3,171]{2,1,0:T(4,128)S(1)}, f32[2,3,171]{2,1,0:T(4,128)S(1)}, u32[]{:S(2)}, u32[]{:S(2)}) collective-permute-start(f32[2,3,171]{2,1,0:T(4,128)S(1)} %get-tuple-element.83), channel_id=1, source_target_pairs={{16,0},{32,16},{48,32},{64,48},{80,64},{96,80},{112,96},{17,1},{33... | collective-permute-start | bytes 12320 | tf_op jit(solution)/shard_map/ppermute | solution.py:440
  136.5 2.3 %collective-permute-done.1 = f32[2,3,171]{2,1,0:T(4,128)S(1)} collective-permute-done((f32[2,3,171]{2,1,0:T(4,128)S(1)}, f32[2,3,171]{2,1,0:T(4,128)S(1)}, u32[]{:S(2)}, u32[]{:S(2)}) %collective-permute-start.1) | collective-permute-done | bytes 4136 | tf_op jit(solution)/shard_map/ppermute | solution.py:440
  138.9 2.6 %fusion.103 = (bf16[256,2048]{1,0:T(8,128)(2,1)S(1)}, bf16[2048]{0:T(1024)(128)(2,1)S(1)}) fusion(f32[256]{0:T(256)S(1)} %reduce.6, bf16[2,128,2048]{2,1,0:T(8,128)(2,1)S(1)} %copy-done.25, f32[256,2048]{1,0:T(8,128)} %fusion.105.refs_19_, bf16[256,171]{1,0:T(8,128)(2,1)S(1)} %bitcast.316, bf16[2048,171]{0,1:T(8,128)(2,1)} %param.26), kind=kOutput, calls=%fused_computation.190 | convolution fusion | flops 182450176 | bytes 4987392 | tf_op jit(solution)/shard_map/dot_general | solution.py:25
  141.6 1.6 fusion.1
  143.1 3.7 %all-to-all-start.6 = ((bf16[16,16,4224]{2,1,0:T(8,128)(2,1)}), bf16[16,16,4224]{2,1,0:T(8,128)(2,1)S(1)}, u32[]{:S(2)}, u32[]{:S(2)}) async-start(bf16[16,16,4224]{2,1,0:T(8,128)(2,1)} %fusion.1), calls=%async_computation.7 | async-start | bytes 4325376 | tf_op jit(solution)/shard_map/all_to_all | solution.py:509
  154.4 2.5 %add_convert_fusion = (bf16[592,256]{1,0:T(8,128)(2,1)}, bf16[592,256]{1,0:T(8,128)(2,1)}, bf16[592,256]{1,0:T(8,128)(2,1)}, bf16[592,256]{1,0:T(8,128)(2,1)S(1)}) fusion(f32[592,1024]{1,0:T(8,128)S(1)} %pad_maximum_fusion, s32[]{:T(128)S(6)} %select_n.225, bf16[592,1024]{1,0:T(8,128)(2,1)} %collective-permute-done.2, s32[]{:T(128)S(6)} %select_n.223, ...), kind=kLoop, calls=%fused_computation.13 | loop fusion | flops 1818624 | bytes 4849680 | tf_op jit(solution)/shard_map/convert_element_type | solution.py:552
  156.9 1.4 collective-permute-start.5
  158.3 1.4 collective-permute-start.4
  159.8 4.0 %all-gather.4.cloned.1.call-done.piece_ref = bf16[2048,1152]{1,0:T(8,128)(2,1)} async-done(((bf16[256,1152]{1,0:T(8,128)(2,1)}), bf16[2048,1152]{1,0:T(8,128)(2,1)}) %all-gather.4.cloned.1.call-update) | async-done | bytes 4718608 | tf_op jit(solution)/shard_map/all_gather | solution.py:850
  163.7 7.7 %place_mlp.1 = (f32[2048,384]{1,0:T(8,128)}, f32[2048,384]{1,0:T(8,128)}, f32[384,2048]{1,0:T(8,128)}) custom-call(bf16[2048,1152]{1,0:T(8,128)(2,1)} %all-gather.4.cloned.1.call-done.piece_ref), custom_call_target="tpu_custom_call" | custom-call | bytes 14155776 | tf_op jit(solution)/shard_map/place_mlp/pallas_call | solution.py:694
  171.4 1.7 collective-permute-done.4.refs_7_
  173.2 1.4 collective-permute-done.3.refs_6_
  175.3 5.6 %all-to-all-done.6.refs_0_ = bf16[16,16,4224]{2,1,0:T(8,128)(2,1)S(1)} async-done(((bf16[16,16,4224]{2,1,0:T(8,128)(2,1)}), bf16[16,16,4224]{2,1,0:T(8,128)(2,1)S(1)}, u32[]{:S(2)}, u32[]{:S(2)}) %all-to-all-start.6) | async-done | bytes 2162720 | tf_op jit(solution)/shard_map/all_to_all | solution.py:509
  181.9 1.8 d_tokens.1
  185.1 31.9 %all_to_all.43.both_ref = bf16[16,2,16,2048]{3,2,1,0:T(8,128)(2,1)S(1)} all-to-all(bf16[16,2,16,2048]{3,2,1,0:T(8,128)(2,1)} %copy-done.2), channel_id=1, replica_groups=mesh['seq'=8,'ch'=16] {'ch'}, dimensions={0} | all-to-all | bytes 4194304 | tf_op jit(solution)/shard_map/all_to_all | solution.py:509
  217.0 4.8 %finish.1 = (f32[16,16,2048]{2,1,0:T(8,128)}, bf16[16,16,2048]{2,1,0:T(8,128)(2,1)}, f32[171,2048]{1,0:T(8,128)}, f32[171,2048]{1,0:T(8,128)}, f32[171,2048]{1,0...) custom-call(bf16[16,2,16,2048]{3,2,1,0:T(8,128)(2,1)S(1)} %all_to_al, ...), custom_call_target="tpu_custom_call" | custom-call | bytes 10493952 | tf_op jit(solution)/shard_map/finish/pallas_call | solution.py:615
  (108 shorter events, 17.4 us)
Async XLA Ops:
  7.2 23.9 %copy-start = (bf16[171,2048]{1,0:T(8,128)(2,1)S(1)}, bf16[171,2048]{1,0:T(8,128)(2,1)}, u32[]{:S(2)}) copy-start(bf16[171,2048]{1,0:T(8,128)(2,1)} %param.34) | copy-start | bytes 2101252
  7.2 8.4 %copy-start.28 = (f32[171]{0:T(256)S(1)}, f32[171]{0:T(256)}, u32[]{:S(2)}) copy-start(f32[171]{0:T(256)} %param.33) | copy-start | bytes 2056
  7.2 9.1 %copy-start.14 = (f32[4,171]{1,0:T(4,128)S(1)}, f32[4,171]{1,0:T(4,128)}, u32[]{:S(2)}) copy-start(f32[4,171]{1,0:T(4,128)} %refs_11_.1) | copy-start | bytes 8212
  7.2 9.1 %copy-start.18 = (s32[3]{0:T(128)S(1)}, s32[3]{0:T(128)}, u32[]{:S(2)}) copy-start(s32[3]{0:T(128)} %refs_2_.3) | copy-start | bytes 40
  7.2 9.1 %copy-start.19 = (s32[8]{0:T(128)S(1)}, s32[8]{0:T(128)}, u32[]{:S(2)}) copy-start(s32[8]{0:T(128)} %refs_1_.3) | copy-start | bytes 100
  7.2 9.1 %copy-start.7 = (bf16[1,171,171]{2,1,0:T(8,128)(2,1)S(1)}, bf16[1,171,171]{2,1,0:T(8,128)(2,1)}, u32[]{:S(2)}) copy-start(bf16[1,171,171]{2,1,0:T(8,128)(2,1)} %refs_14_.1) | copy-start | bytes 175450
  7.3 9.1 %copy-start.6 = (bf16[1,171,171]{2,1,0:T(8,128)(2,1)S(1)}, bf16[1,171,171]{2,1,0:T(8,128)(2,1)}, u32[]{:S(2)}) copy-start(bf16[1,171,171]{2,1,0:T(8,128)(2,1)} %refs_13_.1) | copy-start | bytes 175450
  7.3 9.1 %copy-start.17 = (f32[171]{0:T(256)S(1)}, f32[171]{0:T(256)}, u32[]{:S(2)}) copy-start(f32[171]{0:T(256)} %param.32) | copy-start | bytes 2056
  7.3 9.1 %copy-start.16 = (f32[171]{0:T(256)S(1)}, f32[171]{0:T(256)}, u32[]{:S(2)}) copy-start(f32[171]{0:T(256)} %param.31) | copy-start | bytes 2056
  7.3 9.1 %copy-start.15 = (f32[171]{0:T(256)S(1)}, f32[171]{0:T(256)}, u32[]{:S(2)}) copy-start(f32[171]{0:T(256)} %param.28) | copy-start | bytes 2056
  10.6 44.0 %copy-start.10 = (bf16[16,2048]{1,0:T(8,128)(2,1)}, bf16[16,2048]{1,0:T(8,128)(2,1)S(1)}, u32[]{:S(2)}) copy-start(bf16[16,2048]{1,0:T(8,128)(2,1)S(1)} %get-tuple-element.69.refs_1_) | copy-start | bytes 196612
  10.6 5.7 %collective-permute-start = (bf16[2,3,171]{2,1,0:T(4,128)(2,1)S(1)}, bf16[2,3,171]{2,1,0:T(4,128)(2,1)S(1)}, u32[]{:S(2)}, u32[]{:S(2)}) collective-permute-start(bf16[2,3,171]{2,1,0:T(4,128)(2,1)S(1)} %get-tuple-element.64), channel_id=1, source_target_pairs={{0,16},{16,32},{32,48},{48,64},{64,80},{80,96},{96,112},{1,17},{17... | collective-permute-start | bytes 6164 | tf_op jit(solution)/shard_map/ppermute | solution.py:440
  19.2 10.8 %all-to-all-start = ((f32[8,2,2,171]{3,2,1,0:T(2,128)}), f32[8,2,2,171]{3,2,1,0:T(2,128)S(1)}, u32[]{:S(2)}, u32[]{:S(2)}) async-start(f32[8,2,2,171]{3,2,1,0:T(2,128)} %get-tuple-element.67), calls=%async_computation | async-start | bytes 65536 | tf_op jit(solution)/shard_map/all_to_all | solution.py:445
  25.2 104.6 %reduce-scatter.2.cloned.1.call-start = ((), (), s32[]{:S(2)}) async-start(), calls=%async_computation.9 | async-start | bytes 5308416 | tf_op jit(solution)/shard_map/reduce_scatter | solution.py:801
  31.0 23.5 %copy-start.12 = (f32[2048]{0:T(1024)S(1)}, f32[2048]{0:T(1024)}, u32[]{:S(2)}) copy-start(f32[2048]{0:T(1024)} %param.24) | copy-start | bytes 24580
  31.1 42.2 %copy-start.22 = (bf16[384,2048]{1,0:T(8,128)(2,1)S(1)}, bf16[384,2048]{1,0:T(8,128)(2,1)}, u32[]{:S(2)}) copy-start(bf16[384,2048]{1,0:T(8,128)(2,1)} %three.1) | copy-start | bytes 4718596
  31.5 41.8 %copy-start.3 = (bf16[2,128,2048]{2,1,0:T(8,128)(2,1)S(1)}, bf16[2,128,2048]{2,1,0:T(8,128)(2,1)}, u32[]{:S(2)}) copy-start(bf16[2,128,2048]{2,1,0:T(8,128)(2,1)} %param.20) | copy-start | bytes 3145732
  31.5 41.7 %copy-start.20 = (bf16[2048,384]{1,0:T(8,128)(2,1)S(1)}, bf16[2048,384]{1,0:T(8,128)(2,1)}, u32[]{:S(2)}) copy-start(bf16[2048,384]{1,0:T(8,128)(2,1)} %one.1) | copy-start | bytes 4718596
  31.5 41.7 %copy-start.21 = (bf16[2048,384]{1,0:T(8,128)(2,1)S(1)}, bf16[2048,384]{1,0:T(8,128)(2,1)}, u32[]{:S(2)}) copy-start(bf16[2048,384]{1,0:T(8,128)(2,1)} %two.1) | copy-start | bytes 4718596
  54.9 40.1 %copy-start.5 = (f32[16,2048]{1,0:T(8,128)}, f32[16,2048]{1,0:T(8,128)S(1)}, u32[]{:S(2)}) copy-start(f32[16,2048]{1,0:T(8,128)S(1)} %get-tuple-element.72.refs_1_.refs_2_) | copy-start | bytes 393220
  96.9 18.3 %copy-start.4 = (f32[2,128,171]{2,1,0:T(8,128)S(1)}, f32[2,128,171]{2,1,0:T(8,128)}, u32[]{:S(2)}) copy-start(f32[2,128,171]{2,1,0:T(8,128)} %get-tuple-element.68.refs_1_) | copy-start | bytes 525316
  96.9 17.3 %all-to-all-start.4 = ((bf16[16,16,2048]{2,1,0:T(8,128)(2,1)}), bf16[16,16,2048]{2,1,0:T(8,128)(2,1)S(1)}, u32[]{:S(2)}, u32[]{:S(2)}) async-start(bf16[16,16,2048]{2,1,0:T(8,128)(2,1)} %get-tuple-element.76), calls=%async_computation.4 | async-start | bytes 2097152 | tf_op jit(solution)/shard_map/all_to_all | solution.py:509
  116.7 13.1 %all-to-all-start.5 = ((f32[8,2,2,171]{3,2,1,0:T(2,128)}), f32[8,2,2,171]{3,2,1,0:T(2,128)S(1)}, u32[]{:S(2)}, u32[]{:S(2)}) async-start(f32[8,2,2,171]{3,2,1,0:T(2,128)} %get-tuple-element.80), calls=%async_computation.5 | async-start | bytes 65536 | tf_op jit(solution)/shard_map/all_to_all | solution.py:445
  125.1 38.7 %all-gather.4.cloned.1.call-start = ((), (), s32[]{:S(2)}) async-start(), calls=%async_computation.10 | async-start | bytes 5308416 | tf_op jit(solution)/shard_map/all_gather | solution.py:850
  133.8 5.0 %collective-permute-start.1 = (f32[2,3,171]{2,1,0:T(4,128)S(1)}, f32[2,3,171]{2,1,0:T(4,128)S(1)}, u32[]{:S(2)}, u32[]{:S(2)}) collective-permute-start(f32[2,3,171]{2,1,0:T(4,128)S(1)} %get-tuple-element.83), channel_id=1, source_target_pairs={{16,0},{32,16},{48,32},{64,48},{80,64},{96,80},{112,96},{17,1},{33... | collective-permute-start | bytes 12320 | tf_op jit(solution)/shard_map/ppermute | solution.py:440
  143.1 37.8 %all-to-all-start.6 = ((bf16[16,16,4224]{2,1,0:T(8,128)(2,1)}), bf16[16,16,4224]{2,1,0:T(8,128)(2,1)S(1)}, u32[]{:S(2)}, u32[]{:S(2)}) async-start(bf16[16,16,4224]{2,1,0:T(8,128)(2,1)} %fusion.1), calls=%async_computation.7 | async-start | bytes 4325376 | tf_op jit(solution)/shard_map/all_to_all | solution.py:509
  146.9 70.1 %all-gather.6.cloned.1.call-start = ((), (), s32[]{:S(2)}) async-start(), calls=%async_computation.11 | async-start | bytes 2801664 | tf_op jit(solution)/shard_map/all_gather | solution.py:916
  151.1 3.2 %collective-permute-start.2 = (bf16[592,1024]{1,0:T(8,128)(2,1)}, bf16[592,1024]{1,0:T(8,128)(2,1)}, u32[]{:S(2)}, u32[]{:S(2)}) collective-permute-start(bf16[592,1024]{1,0:T(8,128)(2,1)} %pad_maximum_fusion.1), channel_id=1, source_target_pairs={{0,16},{16,0},{32,48},{48,32},{64,80},{80,64},{96,112},{112,96},{1... | collective-permute-start | bytes 3637256 | tf_op jit(solution)/shard_map/ppermute | solution.py:531
  156.9 14.5 %collective-permute-start.5 = (bf16[592,256]{1,0:T(8,128)(2,1)}, bf16[592,256]{1,0:T(8,128)(2,1)S(1)}, u32[]{:S(2)}, u32[]{:S(2)}) collective-permute-start(bf16[592,256]{1,0:T(8,128)(2,1)} %get-tuple-element.125), channel_id=1, source_target_pairs={{0,64},{16,80},{32,96},{48,112},{64,0},{80,16},{96,32},{112,48},{1... | collective-permute-start | bytes 909320 | tf_op jit(solution)/shard_map/ppermute | solution.py:535
  158.3 14.9 %collective-permute-start.4 = (bf16[592,256]{1,0:T(8,128)(2,1)}, bf16[592,256]{1,0:T(8,128)(2,1)S(1)}, u32[]{:S(2)}, u32[]{:S(2)}) collective-permute-start(bf16[592,256]{1,0:T(8,128)(2,1)} %get-tuple-element.126), channel_id=1, source_target_pairs={{0,96},{16,112},{32,0},{48,16},{64,32},{80,48},{96,64},{112,80},{1... | collective-permute-start | bytes 909320 | tf_op jit(solution)/shard_map/ppermute | solution.py:535
  159.7 21.2 %copy-start.13 = (f32[2048]{0:T(1024)S(1)}, f32[2048]{0:T(1024)}, u32[]{:S(2)}) copy-start(f32[2048]{0:T(1024)} %param.23) | copy-start | bytes 24580
  159.7 14.8 %collective-permute-start.3 = (bf16[592,256]{1,0:T(8,128)(2,1)}, bf16[592,256]{1,0:T(8,128)(2,1)S(1)}, u32[]{:S(2)}, u32[]{:S(2)}) collective-permute-start(bf16[592,256]{1,0:T(8,128)(2,1)} %get-tuple-element.127), channel_id=1, source_target_pairs={{0,32},{16,48},{32,64},{48,80},{64,96},{80,112},{96,0},{112,16},{1... | collective-permute-start | bytes 909320 | tf_op jit(solution)/shard_map/ppermute | solution.py:535
  (10 other events, 22.8 us)
Sparse Core Ops, SparseCore 0:
  78.6 34.2 reduce-scatter.1
  132.7 30.9 all-gather.3
  185.2 24.2 all-gather.5

commit v5 on v4

--- a/solution.py
+++ b/solution.py
@@ -15,6 +15,7 @@
 LANES = 256
 GATE_ROWS = 24
 SMALL_ROWS = 64
+EARLY = 256
 WIDE = 512
 GAIN_ROWS = 16
 HBM_PER_US = 3_600_000
@@ -117,10 +118,9 @@
 
     first = tuple((jnp.ones((1, chans), F32), jnp.zeros((1, chans), F32)) for _ in range(groups))
     last = lax.fori_loop(0, rows, step, first, unroll=8)
-    for g in range(groups):
-        for j in range(carry_ref.shape[0]):
-            carry_ref[j, 0, g : g + 1, :] = last[g][0]
-            carry_ref[j, 1, g : g + 1, :] = last[g][1]
+    carry = jnp.concatenate([last[g][n] for n in range(2) for g in range(groups)], axis=0)
+    for j in range(carry_ref.shape[0]):
+        carry_ref[j] = carry
 
 
 def gelu_parts(x):
@@ -164,10 +164,9 @@
 
     first = tuple((jnp.ones((1, chans), F32), jnp.zeros((1, chans), F32)) for _ in range(groups))
     last = lax.fori_loop(0, rows, step, first, unroll=8)
-    for g in range(groups):
-        for j in range(carry_ref.shape[0]):
-            carry_ref[j, 0, g : g + 1, :] = last[g][0]
-            carry_ref[j, 1, g : g + 1, :] = last[g][1]
+    carry = jnp.concatenate([last[g][n] for n in range(2) for g in range(groups)], axis=0)
+    for j in range(carry_ref.shape[0]):
+        carry_ref[j] = carry
 
 
 def gates_back_kernel(
@@ -443,9 +442,10 @@
 def carried_in(value, backward):
     count, mine = lax.axis_size("seq"), lax.axis_index("seq")
     pieces = lax.all_to_all(value, "seq", 0, 0)
-    total = jnp.zeros(value.shape[2:], F32)
+    groups = value.shape[1] // 2
+    total = jnp.zeros((groups, value.shape[2]), F32)
     for j in range(count - 1, 0, -1) if backward else range(count - 1):
-        longer = pieces[j, 1] + pieces[j, 0] * total
+        longer = pieces[j, groups:] + pieces[j, :groups] * total
         total = jnp.where((j > mine) if backward else (j < mine), longer, total)
     return total
 
@@ -477,32 +477,16 @@
     send_to_all(normed_ref, resid * rms(resid) * gain_ref[...])
 
 
-def mid_back_kernel(got_ref, resid_ref, cotangent_ref, gain_ref, d_mid_ref, g_gain_ref, d_mix_ref):
-    back, g_gain = norm_back(resid_ref[...], gain_ref[...], sum_parts(got_ref))
+def mid_back_kernel(got_ref, resid_ref, cotangent_ref, gain_ref, d_mid_ref, g_gain_ref, early_ref, d_mix_ref):
+    width = resid_ref.shape[1]
+    total = sum_parts(got_ref)
+    resid = resid_ref[...]
+    early_ref[...] = (resid[:, :EARLY] + total[:, width:]).astype(BF16)
+    back, g_gain = norm_back(resid, gain_ref[...], total[:, :width])
     d_mid = cotangent_ref[...].astype(F32) + back
     d_mid_ref[...] = d_mid
     g_gain_ref[...] = g_gain
     send_to_all(d_mix_ref, d_mid)
-
-
-def tokens_back_kernel(got_ref, tokens_ref, resid_ref, d_mid_ref, gain_ref, *refs):
-    *chunk_refs, both_ref, sent_ref = refs
-    width = tokens_ref.shape[1]
-    total = sum_parts(got_ref)
-    rows, lanes = chunk_refs[0].shape
-    chunk = chunk_refs[0][...].astype(F32)
-    for chunk_ref in chunk_refs[1:]:
-        chunk = chunk + chunk_ref[...].astype(F32)
-    gains = total[:GAIN_ROWS, 2 * width :]
-    sent_ref[:rows, :] = chunk.astype(BF16)
-    sent_ref[rows:, : gains.shape[1]] = gains.astype(BF16)
-    sent_ref[rows:, gains.shape[1] :] = jnp.zeros((GAIN_ROWS, lanes - gains.shape[1]), BF16)
-    back, _ = norm_back(tokens_ref[...].astype(F32), gain_ref[...], total[:, :width])
-    d_tokens = (d_mid_ref[...] + back).astype(BF16)
-    layer_out = (resid_ref[...] + total[:, width : 2 * width]).astype(BF16)
-    for j in range(both_ref.shape[0]):
-        both_ref[j, 0] = d_tokens
-        both_ref[j, 1] = layer_out
 
 
 def exchange(pieces):
@@ -552,6 +536,68 @@
         return (cut(kept) + cut(got)).astype(BF16)
 
     return [piece(0)] + [shift_z(piece(hops), hops) for hops in (1, 3, 2)]
+
+
+def tokens_back(got, tokens, resid, early, d_mid, gain, chunk_parts, after):
+    owners, share, _ = got.shape
+    width = tokens.shape[1]
+    rows, lanes = chunk_parts[0].shape
+    late = [in_hbm(a) for a in (tokens, resid, early, d_mid, *chunk_parts)]
+    count = len(late)
+
+    def run(got_ref, gain_ref, *refs):
+        sources, (both_hbm, sent_ref) = refs[:count], refs[count + 1 : count + 3]
+        held, block, sems = refs[count + 3 : 2 * count + 3], refs[-2], refs[-1]
+        tokens_ref, resid_ref, early_ref, d_mid_ref, *part_refs = [
+            Arriving(pltpu.make_async_copy(source, ref, sems.at[n]), ref)
+            for n, (source, ref) in enumerate(zip(sources, held))
+        ]
+        stores = []
+
+        def send(which):
+            for j in range(owners):
+                stores.append(
+                    pltpu.make_async_copy(block.at[which], both_hbm.at[j, which], sems.at[count + len(stores)])
+                )
+                stores[-1].start()
+
+        def total(at, size):
+            cols = slice(at, at + size)
+            result = got_ref[0, :, cols].astype(F32)
+            for j in range(1, owners):
+                result = result + got_ref[j, :, cols].astype(F32)
+            return result
+
+        grad = total(0, width)
+        back, _ = norm_back(tokens_ref[...].astype(F32), gain_ref[...], grad)
+        block[0] = (d_mid_ref[...] + back).astype(BF16)
+        send(0)
+        block[1, :, :EARLY] = early_ref[...]
+        block[1, :, EARLY:] = (resid_ref[:, EARLY:] + total(width, width - EARLY)).astype(BF16)
+        send(1)
+        gains = total(2 * width - EARLY, width // owners)[:GAIN_ROWS]
+        chunk = part_refs[0][...].astype(F32)
+        for part_ref in part_refs[1:]:
+            chunk = chunk + part_ref[...].astype(F32)
+        sent_ref[:rows, :] = chunk.astype(BF16)
+        sent_ref[rows:, : width // owners] = gains.astype(BF16)
+        sent_ref[rows:, width // owners :] = jnp.zeros((GAIN_ROWS, lanes - width // owners), BF16)
+        for store in stores:
+            store.wait()
+
+    vmem = pl.BlockSpec(memory_space=pltpu.VMEM)
+    anywhere = pl.BlockSpec(memory_space=pl.ANY)
+    return pl.pallas_call(
+        run,
+        name="d_tokens",
+        in_specs=[vmem] * 2 + [anywhere] * (count + 1),
+        out_specs=[anywhere, vmem],
+        out_shape=[pltpu.HBM((owners, 2, share, width), BF16), sds((rows + GAIN_ROWS, lanes), BF16)],
+        scratch_shapes=[pltpu.VMEM(a.shape, a.dtype) for a in late]
+        + [pltpu.VMEM((2, share, width), BF16), pltpu.SemaphoreType.DMA((count + 2 * owners,))],
+        cost_estimate=pl.CostEstimate(flops=0, bytes_accessed=2 * got.size, transcendentals=0),
+        compiler_params=pltpu.CompilerParams(vmem_limit_bytes=VMEM_LIMIT),
+    )(got, gain, *late, in_hbm(after))
 
 
 def finish(both, chunks, chans):
@@ -648,8 +694,11 @@
         d_up = (d_hidden * value).astype(BF16)
         for at in steps:
             cols = slice(at, at + WIDE)
-            out = dot(hidden, three[:, cols], ((1,), (0,)))
-            out_parts[:, :, cols] = out.astype(BF16).reshape(owners, share, WIDE)
+            out = dot(hidden, three[:, cols], ((1,), (0,))).astype(BF16).reshape(owners, share, WIDE)
+            early = max(EARLY - at, 0)
+            if early:
+                parts[:, :, width + at : width + EARLY] = out[:, :, :early]
+            out_parts[:, :, max(at - EARLY, 0) : at - EARLY + WIDE] = out[:, :, early:]
         store(out_parts, out_hbm)
         for at in steps:
             cols = slice(at, at + WIDE)
@@ -664,7 +713,8 @@
         for copy in stores:
             copy.wait()
 
-    parts = ((owners, share, width), BF16)
+    parts = ((owners, share, width + EARLY), BF16)
+    later = ((owners, share, width - EARLY), BF16)
     grads = ((width, 3 * units), BF16)
     vmem = pl.BlockSpec(memory_space=pltpu.VMEM)
     anywhere = pl.BlockSpec(memory_space=pl.ANY)
@@ -673,8 +723,8 @@
         name="mlp",
         in_specs=[vmem] * 5,
         out_specs=[vmem, anywhere, anywhere],
-        out_shape=[sds(*parts), pltpu.HBM(*parts), pltpu.HBM(*grads)],
-        scratch_shapes=[pltpu.VMEM(*parts), pltpu.VMEM(*grads), pltpu.SemaphoreType.DMA((len(steps) + 1,))],
+        out_shape=[sds(*parts), pltpu.HBM(*later), pltpu.HBM(*grads)],
+        scratch_shapes=[pltpu.VMEM(*later), pltpu.VMEM(*grads), pltpu.SemaphoreType.DMA((len(steps) + 1,))],
         cost_estimate=pl.CostEstimate(
             flops=18 * rows * width * units, bytes_accessed=14 * width * units, transcendentals=0
         ),
@@ -754,7 +804,7 @@
     keep, decay_run, local_state, carry = run_kernel(
         forward_kernel,
         "conv_gates_scan",
-        [big] * 3 + [sds((seq_count, 2, groups, chans))],
+        [big] * 3 + [sds((seq_count, 2 * groups, chans))],
         [
             start,
             short_lengths,
@@ -789,10 +839,10 @@
     normed_two = exchange(normed_two).reshape(total_rows, width)
 
     two_parts, partial_out, g_mlp = mlp_back(normed_two, w_one, w_two, w_three, cotangent, ch_count)
-    d_mid, gain_two_part, d_mix = run_kernel(
+    d_mid, gain_two_part, early, d_mix = run_kernel(
         mid_back_kernel,
         "d_mid",
-        [share, sds((1, width)), to_all],
+        [share, sds((1, width)), sds((share_rows, EARLY), BF16), to_all],
         [exchange(two_parts), resid_share, cotangent_share, gain_two[None]],
         after=[g_mlp, partial_out],
         waits=20,
@@ -804,13 +854,11 @@
     d_gate_pre, reach, local_adjoint, carry_back = run_kernel(
         adjoint_kernel,
         "adjoint_scan",
-        [sds((groups, rows, chans), BF16), big, big, sds((seq_count, 2, groups, chans))],
+        [sds((groups, rows, chans), BF16), big, big, sds((seq_count, 2 * groups, chans))],
         [d_mixed, gate_pre, hidden, keep],
         waits=20,
     )
     beyond = carried_in(carry_back, True)
-    d_gate_pre = d_gate_pre.reshape(total_rows, chans)
-    partial_y = lax.optimization_barrier(dot(d_gate_pre, w_y, ((1,), (1,))))
     d_conv_head, d_input, small, g_mlp = run_kernel(
         gates_back_kernel,
         "gates_back",
@@ -843,7 +891,6 @@
         ],
         flops=4 * flops,
         smem=3,
-        after=[partial_y],
         passed=g_mlp,
         waits=10,
     )
@@ -866,7 +913,9 @@
         late.append(total)
     late = jnp.pad(jnp.stack(late, axis=1), ((0, 0), (rows - TAPS + 1, 0), (0, 0)))
     d_input = (d_input + late).astype(BF16).reshape(total_rows, chans)
-    partial_one = dot(d_input, w_x, ((1,), (1,))) + partial_y
+    d_gate_pre = d_gate_pre.reshape(total_rows, chans)
+
+    partial_one = dot(d_input, w_x, ((1,), (1,))) + dot(d_gate_pre, w_y, ((1,), (1,)))
     gain_one_part = jnp.sum(partial_one * (tokens_f * scale_one), axis=0, keepdims=True)
     gain_parts = jnp.concatenate([gain_one_part, gain_two_part], axis=0)
     back_pieces = exchange(with_gains([by_owner(partial_one), partial_out], gain_parts))
@@ -890,13 +939,8 @@
     chunk_parts = reduce_chunk(terms(False), terms(True), 1)
 
     g_w_one, g_w_two, g_w_three = place_mlp(g_mlp, hidden_units)
-    both, chunk = run_kernel(
-        tokens_back_kernel,
-        "d_tokens",
-        [sds((ch_count, 2, share_rows, width), BF16), sds((chunk_parts[0].shape[0] + GAIN_ROWS, LANES), BF16)],
-        [back_pieces, Late(tokens_share), Late(resid_share), Late(d_mid), gain_one[None], *chunk_parts],
-        after=[g_w_one],
-        waits=30,
+    both, chunk = tokens_back(
+        back_pieces, tokens_share, resid_share, early, d_mid, gain_one[None], chunk_parts, g_w_one
     )
     (
         d_tokens,

time: 229 us -> 228 us (level)
  blocking collectives: 89.9 us -> 109 us
  waiting for transfers between devices: 36.8 us -> 25.1 us
  starting transfers between devices: 32.5 us -> 27.9 us
  local copies, waits for them, and re-layouts: 4.35 us -> 1.36 us
    all_to_all x4 -> x5, blocking collectives: 89.9 us -> 109 us  [exchange(): return lax.all_to_all(pieces, 'ch', 0, 0)]
    all_to_all x2 -> x1, waiting for transfers between devices: 19.1 us -> 4.78 us  [exchange(): return lax.all_to_all(pieces, 'ch', 0, 0)]
    all_to_all x2 -> x1, starting transfers between devices: 7.51 us -> 3.77 us  [exchange(): return lax.all_to_all(pieces, 'ch', 0, 0)]
    pallas_call x0 -> x1, Pallas kernels: none -> 3.4 us  [tokens_back(): pl.pallas_call(run, name='d_tokens', in_specs=[vmem] * 2 + [anywhere] * (...]
    unnamed x58 -> x68, local copies, waits for them, and re-layouts: 4.29 us -> 1.3 us
    all_to_all x2, waiting for transfers between devices: 6.59 us -> 9.45 us  [carried_in(): pieces = lax.all_to_all(value, 'seq', 0, 0)]
    pallas_call x6 -> x5, Pallas kernels: 10.3 us -> 7.44 us  [run_kernel(): pl.pallas_call(run, name=name, out_shape=outs, in_specs=in_specs, out_spe...]
  transfers between devices with their start and end apart: 13 -> 12, of which waited for: 10 -> 9; matrix products, arithmetic and copies ran while one was open for 8% -> 7% of each run, Pallas kernels for 5% -> 4%
where the time goes in v5:
time: 228 us; the launch traced here: 227 us
  blocking collectives  109 us (48%)
  Pallas kernels  31.8 us (14%)
  starting transfers between devices  27.9 us (12%)
  waiting for transfers between devices  25.1 us (11%)
  between operations  14.4 us (6%)
  matrix products  9.4 us (4%)
  other arithmetic  7.93 us (3%)
    all_to_all x5, blocking collectives, exchange(): return lax.all_to_all(pieces, 'ch', 0, 0)  109 us
    all_to_all x2, starting transfers between devices, carried_in(): pieces = lax.all_to_all(value, 'seq', 0, 0)  13.9 us
    all_to_all x2, waiting for transfers between devices, carried_in(): pieces = lax.all_to_all(value, 'seq', 0, 0)  9.45 us
    dot_general x10, matrix products, dot(): lax.dot_general(left, right, (contract, ((), ())), preferred_element_type...  9.4 us
    pallas_call x1, Pallas kernels, place_mlp(): pl.pallas_call(run, name='place_mlp', grid=(width // LANES,), in_specs=[p...  7.68 us
    ppermute x2, starting transfers between devices, shifted(): return lax.ppermute(block, axis, route)  7.56 us
    pallas_call x5, Pallas kernels, run_kernel(): pl.pallas_call(run, name=name, out_shape=outs, in_specs=in_specs, out_spe...  7.44 us
    pallas_call x1, Pallas kernels, mlp_back(): pl.pallas_call(run, name='mlp', in_specs=[vmem] * 5, out_specs=[vmem, any...  5.13 us
  transfers between devices with their start and end apart: 12, of which 9 were waited for; matrix products, arithmetic and copies ran while one was open for 7% of the time, Pallas kernels for 4%

profile of v5, /device:TPU:1, one launch (start us, length us, event | category | flops | bytes accessed | tf_op | source)
XLA Modules:
  0.0 227.0 jit_solution(10821894196511638303)
XLA Ops:
  7.3 3.3 %front.1 = (bf16[256,2048]{1,0:T(8,128)(2,1)}, f32[256,1]{1,0:T(8,128)S(1)}, bf16[2,128,171]{2,1,0:T(8,128)(2,1)S(1)}, bf16[2,3,171]{2,1,0:T(4,128)(2,1)S(1)}, f...) custom-call(f32[1,2048]{1,0:T(1,128)} %bitcast.297, ...), custom_call_target="tpu_custom_call" | custom-call | flops 358612992 | bytes 2097152 | tf_op jit(solution)/shard_map/front/pallas_call | solution.py:406
  11.3 4.9 %collective-permute-start = (bf16[2,3,171]{2,1,0:T(4,128)(2,1)S(1)}, bf16[2,3,171]{2,1,0:T(4,128)(2,1)S(1)}, u32[]{:S(2)}, u32[]{:S(2)}) collective-permute-start(bf16[2,3,171]{2,1,0:T(4,128)(2,1)S(1)} %get-tuple-element.65), channel_id=1, source_target_pairs={{0,16},{16,32},{32,48},{48,64},{64,80},{80,96},{96,112},{1,17},{17... | collective-permute-start | bytes 6164 | tf_op jit(solution)/shard_map/ppermute | solution.py:439
  17.0 2.8 %conv_gates_scan.1 = (f32[2,128,171]{2,1,0:T(8,128)S(1)}, f32[2,128,171]{2,1,0:T(8,128)S(1)}, f32[2,128,171]{2,1,0:T(8,128)S(1)}, f32[8,4,171]{2,1,0:T(4,128)}) custom-call(s32[1]{0:T(128)} %bitcast.refs_0_, s32[8]{0:T(128)S(1)} %copy-done.20, s32[3]{0:T(128)S(1)} %copy-done.18, bf16[2,128,171]{2,1,0:T(8,128)(2,1)S(1)} %get-tuple-element.64.refs_3_.refs_9_, ...), custom_call_target="tpu_custom_call" | custom-call | flops 29942784 | bytes 759288 | tf_op jit(solution)/shard_map/conv_gates_scan/pallas_call | solution.py:342
  19.8 6.1 %all-to-all-start = ((f32[8,4,171]{2,1,0:T(4,128)}), f32[8,4,171]{2,1,0:T(4,128)S(1)}, u32[]{:S(2)}, u32[]{:S(2)}) async-start(f32[8,4,171]{2,1,0:T(4,128)} %get-tuple-element.68), calls=%async_computation | async-start | bytes 65536 | tf_op jit(solution)/shard_map/all_to_all | solution.py:444
  25.8 4.7 %all-to-all-done = f32[8,4,171]{2,1,0:T(4,128)S(1)} async-done(((f32[8,4,171]{2,1,0:T(4,128)}), f32[8,4,171]{2,1,0:T(4,128)S(1)}, u32[]{:S(2)}, u32[]{:S(2)}) %all-to-all-start) | async-done | bytes 21920 | tf_op jit(solution)/shard_map/all_to_all | solution.py:444
  32.1 22.9 %all_to_all.40.refs_0_ = bf16[16,16,2048]{2,1,0:T(8,128)(2,1)S(1)} all-to-all(bf16[16,16,2048]{2,1,0:T(8,128)(2,1)S(1)} %bitcast.315), channel_id=1, replica_groups=mesh['seq'=8,'ch'=16] {'ch'}, dimensions={0} | all-to-all | bytes 2097152 | tf_op jit(solution)/shard_map/all_to_all | solution.py:493
  55.3 18.5 %all_to_all.41 = bf16[16,16,2048]{2,1,0:T(8,128)(2,1)S(1)} all-to-all(bf16[16,16,2048]{2,1,0:T(8,128)(2,1)S(1)} %get-tuple-element.71), channel_id=1, replica_groups=mesh['seq'=8,'ch'=16] {'ch'}, dimensions={0} | all-to-all | bytes 2097152 | tf_op jit(solution)/shard_map/all_to_all | solution.py:493
  73.9 5.1 %mlp.1 = (bf16[16,16,2304]{2,1,0:T(8,128)(2,1)S(1)}, bf16[16,16,1792]{2,1,0:T(8,128)(2,1)}, bf16[2048,1152]{1,0:T(8,128)(2,1)}) custom-call(bf16[256,2048]{1,0:T(8,128)(2,1)S(1)} %bitcast.293, bf16[2048,384]{1,0:T(8,128)(2,1)S(1)} %copy-done.22, bf16[2048,384]{1,0:T(8,128)(2,1)S(1)} %copy-done.23, bf16[384,2048]{1,0:T(8,128)(2,1)S(1)} %copy-done.24, ...), custom_call_target="tpu_custom_call" | custom-call | flops 3623878656 | bytes 11010048 | tf_op jit(solution)/shard_map/mlp/pallas_call | solution.py:721
  79.0 18.3 %all_to_all.42.refs_0_ = bf16[16,16,2304]{2,1,0:T(8,128)(2,1)S(1)} all-to-all(bf16[16,16,2304]{2,1,0:T(8,128)(2,1)S(1)} %get-tuple-element.72), channel_id=1, replica_groups=mesh['seq'=8,'ch'=16] {'ch'}, dimensions={0} | all-to-all | bytes 2359296 | tf_op jit(solution)/shard_map/all_to_all | solution.py:493
  97.6 17.3 %all_to_all.43 = bf16[16,16,2048]{2,1,0:T(8,128)(2,1)S(1)} all-to-all(bf16[16,16,2048]{2,1,0:T(8,128)(2,1)S(1)} %get-tuple-element.77), channel_id=1, replica_groups=mesh['seq'=8,'ch'=16] {'ch'}, dimensions={0} | all-to-all | bytes 2097152 | tf_op jit(solution)/shard_map/all_to_all | solution.py:493
  115.9 1.4 adjoint_scan.1
  117.3 7.8 %all-to-all-start.5 = ((f32[8,4,171]{2,1,0:T(4,128)}), f32[8,4,171]{2,1,0:T(4,128)S(1)}, u32[]{:S(2)}, u32[]{:S(2)}) async-start(f32[8,4,171]{2,1,0:T(4,128)} %get-tuple-element.81), calls=%async_computation.5 | async-start | bytes 65536 | tf_op jit(solution)/shard_map/all_to_all | solution.py:444
  125.1 4.7 %all-to-all-done.5 = f32[8,4,171]{2,1,0:T(4,128)S(1)} async-done(((f32[8,4,171]{2,1,0:T(4,128)}), f32[8,4,171]{2,1,0:T(4,128)S(1)}, u32[]{:S(2)}, u32[]{:S(2)}) %all-to-all-start.5) | async-done | bytes 21920 | tf_op jit(solution)/shard_map/all_to_all | solution.py:444
  130.0 2.7 %gates_back.1 = (f32[2,3,171]{2,1,0:T(4,128)S(1)}, f32[2,128,171]{2,1,0:T(8,128)S(1)}, f32[64,2048]{1,0:T(8,128)S(1)}, bf16[256,1152]{1,0:T(8,128)(2,1)}) custom-call(s32[1]{0:T(128)} %bitcast.refs_0_, s32[8]{0:T(128)S(1)} %copy-done.21, s32[3]{0:T(128)S(1)} %copy-done.19, f32[2,128,171]{2,1,0:T(8,128)S(1)} %get-tuple-element.79.refs_3_, ...), custom_call_target="tpu_custom_call" | custom-call | flops 59885568 | bytes 37619420 | tf_op jit(solution)/shard_map/gates_back/pallas_call | solution.py:342
  134.0 2.6 %collective-permute-start.1 = (f32[2,3,171]{2,1,0:T(4,128)S(1)}, f32[2,3,171]{2,1,0:T(4,128)S(1)}, u32[]{:S(2)}, u32[]{:S(2)}) collective-permute-start(f32[2,3,171]{2,1,0:T(4,128)S(1)} %get-tuple-element.83), channel_id=1, source_target_pairs={{16,0},{32,16},{48,32},{64,48},{80,64},{96,80},{112,96},{17,1},{33... | collective-permute-start | bytes 12320 | tf_op jit(solution)/shard_map/ppermute | solution.py:439
  136.6 2.3 %collective-permute-done.1 = f32[2,3,171]{2,1,0:T(4,128)S(1)} collective-permute-done((f32[2,3,171]{2,1,0:T(4,128)S(1)}, f32[2,3,171]{2,1,0:T(4,128)S(1)}, u32[]{:S(2)}, u32[]{:S(2)}) %collective-permute-start.1) | collective-permute-done | bytes 4136 | tf_op jit(solution)/shard_map/ppermute | solution.py:439
  139.0 1.7 fusion.105
  140.7 1.8 fusion.103
  142.6 1.4 fusion.1
  144.1 3.8 %all-to-all-start.6 = ((bf16[16,16,3968]{2,1,0:T(8,128)(2,1)}), bf16[16,16,3968]{2,1,0:T(8,128)(2,1)S(1)}, u32[]{:S(2)}, u32[]{:S(2)}) async-start(bf16[16,16,3968]{2,1,0:T(8,128)(2,1)} %fusion.1), calls=%async_computation.7 | async-start | bytes 4063232 | tf_op jit(solution)/shard_map/all_to_all | solution.py:493
  147.9 1.4 convolution_convert_fusion.1
  152.1 1.5 fusion.5
  155.4 2.6 %add_convert_fusion = (bf16[592,256]{1,0:T(8,128)(2,1)}, bf16[592,256]{1,0:T(8,128)(2,1)}, bf16[592,256]{1,0:T(8,128)(2,1)S(1)}, bf16[592,256]{1,0:T(8,128)(2,1)}) fusion(f32[592,1024]{1,0:T(8,128)S(1)} %pad_maximum_fusion, s32[]{:T(128)S(6)} %select_n.225, bf16[592,1024]{1,0:T(8,128)(2,1)} %collective-permute-done.2, s32[]{:T(128)S(6)} %select_n.223, ...), kind=kLoop, calls=%fused_computation.13 | loop fusion | flops 1818624 | bytes 4849680 | tf_op jit(solution)/shard_map/convert_element_type | solution.py:536
  158.8 1.8 collective-permute-start.4
  160.6 2.8 %all-gather.4.cloned.1.call-done.piece_ref = bf16[2048,1152]{1,0:T(8,128)(2,1)} async-done(((bf16[256,1152]{1,0:T(8,128)(2,1)}), bf16[2048,1152]{1,0:T(8,128)(2,1)}) %all-gather.4.cloned.1.call-update) | async-done | bytes 4718608 | tf_op jit(solution)/shard_map/all_gather | solution.py:897
  163.4 7.7 %place_mlp.1 = (f32[2048,384]{1,0:T(8,128)}, f32[2048,384]{1,0:T(8,128)}, f32[384,2048]{1,0:T(8,128)}) custom-call(bf16[2048,1152]{1,0:T(8,128)(2,1)} %all-gather.4.cloned.1.call-done.piece_ref), custom_call_target="tpu_custom_call" | custom-call | bytes 14155776 | tf_op jit(solution)/shard_map/place_mlp/pallas_call | solution.py:744
  171.1 2.3 collective-permute-done.4.refs_6_
  173.4 1.9 collective-permute-done.3.refs_5_
  175.3 4.8 %all-to-all-done.6.got_ref = bf16[16,16,3968]{2,1,0:T(8,128)(2,1)S(1)} async-done(((bf16[16,16,3968]{2,1,0:T(8,128)(2,1)}), bf16[16,16,3968]{2,1,0:T(8,128)(2,1)S(1)}, u32[]{:S(2)}, u32[]{:S(2)}) %all-to-all-start.6) | async-done | bytes 2031648 | tf_op jit(solution)/shard_map/all_to_all | solution.py:493
  180.1 3.4 %d_tokens.1 = (bf16[16,2,16,2048]{3,2,1,0:T(8,128)(2,1)}, bf16[608,256]{1,0:T(8,128)(2,1)}) custom-call(bf16[16,16,3968]{2,1,0:T(8,128)(2,1)S(1)} %all-to-all-done.6.got_ref, f32[1,2048]{1,0:T(1,128)S(1)} %bitcast.298, bf16[16,2048]{1,0:T(8,128)(2,1)} %copy-done.7, f32[16,2048]{1,0:T(8,128)} %copy-done.4, bf16[16,256]{1,0:T(8,128)(2,1)} %copy-done.14, ...), custom_call_target="tpu_custom_call" | custom-call | bytes 2031616 | tf_op jit(solution)/shard_map/d_tokens/pallas_call | solution.py:590
  183.5 32.1 %all_to_all.44.both_ref = bf16[16,2,16,2048]{3,2,1,0:T(8,128)(2,1)S(1)} all-to-all(bf16[16,2,16,2048]{3,2,1,0:T(8,128)(2,1)} %get-tuple-element.93), channel_id=1, replica_groups=mesh['seq'=8,'ch'=16] {'ch'}, dimensions={0} | all-to-all | bytes 4194304 | tf_op jit(solution)/shard_map/all_to_all | solution.py:493
  215.6 4.8 %finish.1 = (f32[16,16,2048]{2,1,0:T(8,128)}, bf16[16,16,2048]{2,1,0:T(8,128)(2,1)}, f32[171,2048]{1,0:T(8,128)}, f32[171,2048]{1,0:T(8,128)}, f32[171,2048]{1,0...) custom-call(bf16[16,2,16,2048]{3,2,1,0:T(8,128)(2,1)S(1)} %all_to_al, ...), custom_call_target="tpu_custom_call" | custom-call | bytes 10493952 | tf_op jit(solution)/shard_map/finish/pallas_call | solution.py:661
  (117 shorter events, 11.4 us)
Async XLA Ops:
  7.2 24.5 %copy-start = (bf16[171,2048]{1,0:T(8,128)(2,1)S(1)}, bf16[171,2048]{1,0:T(8,128)(2,1)}, u32[]{:S(2)}) copy-start(bf16[171,2048]{1,0:T(8,128)(2,1)} %param.34) | copy-start | bytes 2101252
  7.2 9.7 %copy-start.13 = (f32[4,171]{1,0:T(4,128)S(1)}, f32[4,171]{1,0:T(4,128)}, u32[]{:S(2)}) copy-start(f32[4,171]{1,0:T(4,128)} %refs_11_.1) | copy-start | bytes 8212
  7.2 9.7 %copy-start.18 = (s32[3]{0:T(128)S(1)}, s32[3]{0:T(128)}, u32[]{:S(2)}) copy-start(s32[3]{0:T(128)} %refs_2_.3) | copy-start | bytes 40
  7.2 9.7 %copy-start.20 = (s32[8]{0:T(128)S(1)}, s32[8]{0:T(128)}, u32[]{:S(2)}) copy-start(s32[8]{0:T(128)} %refs_1_.3) | copy-start | bytes 100
  7.3 9.7 %copy-start.6 = (bf16[1,171,171]{2,1,0:T(8,128)(2,1)S(1)}, bf16[1,171,171]{2,1,0:T(8,128)(2,1)}, u32[]{:S(2)}) copy-start(bf16[1,171,171]{2,1,0:T(8,128)(2,1)} %refs_14_.1) | copy-start | bytes 175450
  7.3 9.7 %copy-start.5 = (bf16[1,171,171]{2,1,0:T(8,128)(2,1)S(1)}, bf16[1,171,171]{2,1,0:T(8,128)(2,1)}, u32[]{:S(2)}) copy-start(bf16[1,171,171]{2,1,0:T(8,128)(2,1)} %refs_13_.1) | copy-start | bytes 175450
  11.3 43.8 %copy-start.7 = (bf16[16,2048]{1,0:T(8,128)(2,1)}, bf16[16,2048]{1,0:T(8,128)(2,1)S(1)}, u32[]{:S(2)}) copy-start(bf16[16,2048]{1,0:T(8,128)(2,1)S(1)} %get-tuple-element.70.refs_1_.refs_0_) | copy-start | bytes 196612
  11.3 5.7 %collective-permute-start = (bf16[2,3,171]{2,1,0:T(4,128)(2,1)S(1)}, bf16[2,3,171]{2,1,0:T(4,128)(2,1)S(1)}, u32[]{:S(2)}, u32[]{:S(2)}) collective-permute-start(bf16[2,3,171]{2,1,0:T(4,128)(2,1)S(1)} %get-tuple-element.65), channel_id=1, source_target_pairs={{0,16},{16,32},{32,48},{48,64},{64,80},{80,96},{96,112},{1,17},{17... | collective-permute-start | bytes 6164 | tf_op jit(solution)/shard_map/ppermute | solution.py:439
  19.8 10.8 %all-to-all-start = ((f32[8,4,171]{2,1,0:T(4,128)}), f32[8,4,171]{2,1,0:T(4,128)S(1)}, u32[]{:S(2)}, u32[]{:S(2)}) async-start(f32[8,4,171]{2,1,0:T(4,128)} %get-tuple-element.68), calls=%async_computation | async-start | bytes 65536 | tf_op jit(solution)/shard_map/all_to_all | solution.py:444
  25.8 104.1 %reduce-scatter.2.cloned.1.call-start = ((), (), s32[]{:S(2)}) async-start(), calls=%async_computation.9 | async-start | bytes 5308416 | tf_op jit(solution)/shard_map/reduce_scatter | solution.py:851
  31.7 23.4 %copy-start.11 = (f32[2048]{0:T(1024)S(1)}, f32[2048]{0:T(1024)}, u32[]{:S(2)}) copy-start(f32[2048]{0:T(1024)} %param.24) | copy-start | bytes 24580
  31.7 42.2 %copy-start.24 = (bf16[384,2048]{1,0:T(8,128)(2,1)S(1)}, bf16[384,2048]{1,0:T(8,128)(2,1)}, u32[]{:S(2)}) copy-start(bf16[384,2048]{1,0:T(8,128)(2,1)} %three.1) | copy-start | bytes 4718596
  32.1 41.7 %copy-start.23 = (bf16[2048,384]{1,0:T(8,128)(2,1)S(1)}, bf16[2048,384]{1,0:T(8,128)(2,1)}, u32[]{:S(2)}) copy-start(bf16[2048,384]{1,0:T(8,128)(2,1)} %two.1) | copy-start | bytes 4718596
  55.0 18.8 %copy-start.2 = (bf16[2,128,2048]{2,1,0:T(8,128)(2,1)S(1)}, bf16[2,128,2048]{2,1,0:T(8,128)(2,1)}, u32[]{:S(2)}) copy-start(bf16[2,128,2048]{2,1,0:T(8,128)(2,1)} %param.20) | copy-start | bytes 3145732
  55.0 18.8 %copy-start.22 = (bf16[2048,384]{1,0:T(8,128)(2,1)S(1)}, bf16[2048,384]{1,0:T(8,128)(2,1)}, u32[]{:S(2)}) copy-start(bf16[2048,384]{1,0:T(8,128)(2,1)} %one.1) | copy-start | bytes 4718596
  55.3 42.0 %copy-start.4 = (f32[16,2048]{1,0:T(8,128)}, f32[16,2048]{1,0:T(8,128)S(1)}, u32[]{:S(2)}) copy-start(f32[16,2048]{1,0:T(8,128)S(1)} %get-tuple-element.73.refs_1_) | copy-start | bytes 393220
  97.6 17.4 %copy-start.8 = (f32[16,2048]{1,0:T(8,128)}, f32[16,2048]{1,0:T(8,128)S(1)}, u32[]{:S(2)}) copy-start(f32[16,2048]{1,0:T(8,128)S(1)} %get-tuple-element.88.refs_3_) | copy-start | bytes 393220
  97.6 19.8 %copy-start.14 = (bf16[16,256]{1,0:T(8,128)(2,1)}, bf16[16,256]{1,0:T(8,128)(2,1)S(1)}, u32[]{:S(2)}) copy-start(bf16[16,256]{1,0:T(8,128)(2,1)S(1)} %get-tuple-element.87.refs_2_) | copy-start | bytes 24580
  97.6 18.3 %copy-start.3 = (f32[2,128,171]{2,1,0:T(8,128)S(1)}, f32[2,128,171]{2,1,0:T(8,128)}, u32[]{:S(2)}) copy-start(f32[2,128,171]{2,1,0:T(8,128)} %get-tuple-element.69.refs_1_) | copy-start | bytes 525316
  115.0 15.0 %copy-start.19 = (s32[3]{0:T(128)S(1)}, s32[3]{0:T(128)}, u32[]{:S(2)}) copy-start(s32[3]{0:T(128)} %refs_2_.3) | copy-start | bytes 40
  115.0 15.0 %copy-start.21 = (s32[8]{0:T(128)S(1)}, s32[8]{0:T(128)}, u32[]{:S(2)}) copy-start(s32[8]{0:T(128)} %refs_1_.3) | copy-start | bytes 100
  115.4 17.6 %copy-start.10 = (f32[256,1]{1,0:T(8,128)S(1)}, f32[256,1]{1,0:T(8,128)}, u32[]{:S(2)}) copy-start(f32[256,1]{1,0:T(8,128)} %copy-done.9) | copy-start | bytes 3076
  117.3 12.5 %all-to-all-start.5 = ((f32[8,4,171]{2,1,0:T(4,128)}), f32[8,4,171]{2,1,0:T(4,128)S(1)}, u32[]{:S(2)}, u32[]{:S(2)}) async-start(f32[8,4,171]{2,1,0:T(4,128)} %get-tuple-element.81), calls=%async_computation.5 | async-start | bytes 65536 | tf_op jit(solution)/shard_map/all_to_all | solution.py:444
  125.1 38.3 %all-gather.4.cloned.1.call-start = ((), (), s32[]{:S(2)}) async-start(), calls=%async_computation.10 | async-start | bytes 5308416 | tf_op jit(solution)/shard_map/all_gather | solution.py:897
  134.0 5.0 %collective-permute-start.1 = (f32[2,3,171]{2,1,0:T(4,128)S(1)}, f32[2,3,171]{2,1,0:T(4,128)S(1)}, u32[]{:S(2)}, u32[]{:S(2)}) collective-permute-start(f32[2,3,171]{2,1,0:T(4,128)S(1)} %get-tuple-element.83), channel_id=1, source_target_pairs={{16,0},{32,16},{48,32},{64,48},{80,64},{96,80},{112,96},{17,1},{33... | collective-permute-start | bytes 12320 | tf_op jit(solution)/shard_map/ppermute | solution.py:439
  144.1 36.0 %all-to-all-start.6 = ((bf16[16,16,3968]{2,1,0:T(8,128)(2,1)}), bf16[16,16,3968]{2,1,0:T(8,128)(2,1)S(1)}, u32[]{:S(2)}, u32[]{:S(2)}) async-start(bf16[16,16,3968]{2,1,0:T(8,128)(2,1)} %fusion.1), calls=%async_computation.7 | async-start | bytes 4063232 | tf_op jit(solution)/shard_map/all_to_all | solution.py:493
  147.8 67.7 %all-gather.6.cloned.1.call-start = ((), (), s32[]{:S(2)}) async-start(), calls=%async_computation.11 | async-start | bytes 2801664 | tf_op jit(solution)/shard_map/all_gather | solution.py:960
  152.1 3.2 %collective-permute-start.2 = (bf16[592,1024]{1,0:T(8,128)(2,1)}, bf16[592,1024]{1,0:T(8,128)(2,1)}, u32[]{:S(2)}, u32[]{:S(2)}) collective-permute-start(bf16[592,1024]{1,0:T(8,128)(2,1)} %pad_maximum_fusion.1), channel_id=1, source_target_pairs={{0,16},{16,0},{32,48},{48,32},{64,80},{80,64},{96,112},{112,96},{1... | collective-permute-start | bytes 3637256 | tf_op jit(solution)/shard_map/ppermute | solution.py:515
  157.9 13.2 %collective-permute-start.5 = (bf16[592,256]{1,0:T(8,128)(2,1)}, bf16[592,256]{1,0:T(8,128)(2,1)S(1)}, u32[]{:S(2)}, u32[]{:S(2)}) collective-permute-start(bf16[592,256]{1,0:T(8,128)(2,1)} %get-tuple-element.127), channel_id=1, source_target_pairs={{0,64},{16,80},{32,96},{48,112},{64,0},{80,16},{96,32},{112,48},{1... | collective-permute-start | bytes 909320 | tf_op jit(solution)/shard_map/ppermute | solution.py:519
  158.8 14.6 %collective-permute-start.4 = (bf16[592,256]{1,0:T(8,128)(2,1)}, bf16[592,256]{1,0:T(8,128)(2,1)S(1)}, u32[]{:S(2)}, u32[]{:S(2)}) collective-permute-start(bf16[592,256]{1,0:T(8,128)(2,1)} %get-tuple-element.128), channel_id=1, source_target_pairs={{0,96},{16,112},{32,0},{48,16},{64,32},{80,48},{96,64},{112,80},{1... | collective-permute-start | bytes 909320 | tf_op jit(solution)/shard_map/ppermute | solution.py:519
  160.6 19.4 %copy-start.12 = (f32[2048]{0:T(1024)S(1)}, f32[2048]{0:T(1024)}, u32[]{:S(2)}) copy-start(f32[2048]{0:T(1024)} %param.23) | copy-start | bytes 24580
  160.6 14.6 %collective-permute-start.3 = (bf16[592,256]{1,0:T(8,128)(2,1)S(1)}, bf16[592,256]{1,0:T(8,128)(2,1)S(1)}, u32[]{:S(2)}, u32[]{:S(2)}) collective-permute-start(bf16[592,256]{1,0:T(8,128)(2,1)S(1)} %get-tuple-element.129), channel_id=1, source_target_pairs={{0,32},{16,48},{32,64},{48,80},{64,96},{80,112},{96,0},{112,16},{1... | collective-permute-start | bytes 909320 | tf_op jit(solution)/shard_map/ppermute | solution.py:519
  (14 other events, 79.2 us)
Sparse Core Ops, SparseCore 0:
  79.2 34.4 reduce-scatter.1
  132.8 30.5 all-gather.3
  183.6 23.3 all-gather.5
